TPU v7x, 32 devices: a whole 2x2x4 slice. The times are simulated.
32 devices in a mesh: pipe: 2 (over core), tensor: 4 (over y, x), dp: 4 (over z).
Axes of the slice: x: 2, y: 2, z: 4, core: 2. Of those that a mesh axis runs over, the one named last changes fastest.
Arguments:
- tokens: bfloat16 [8192, 2048], P('dp'), may hold values from -6 to 6
- cotangent: bfloat16 [8192, 2048], P('dp'), may hold values from -6 to 6
- lengths: int32 [8], P('dp'), may hold values from 513 to 1024, as said below
- inward: float32 [2, 2048, 3, 2048], P('pipe', 'dp', None, 'tensor'), may hold values from -0.125 to 0.125
- outward: float32 [2, 2048, 2048], P('pipe', 'tensor', 'dp'), may hold values from -1 to 1
- expand: float32 [2, 2048, 8192], P('pipe', 'dp', 'tensor'), may hold values from -0.125 to 0.125
- contract: float32 [2, 8192, 2048], P('pipe', 'tensor', 'dp'), may hold values from -0.0625 to 0.0625
- vectors: float32 [2, 5, 2048], P('pipe', None, 'dp'), as said below
- offsets: float32 [2, 8192], P('pipe', ('tensor', 'dp')), may hold values from -3 to 3
- inward_first: float32 [2, 2048, 3, 2048], P('pipe', 'dp', None, 'tensor'), may hold values from -48 to 48
- inward_second: float32 [2, 2048, 3, 2048], P('pipe', 'dp', None, 'tensor'), may hold values from 327.68 to 1310.72
- outward_first: float32 [2, 2048, 2048], P('pipe', 'tensor', 'dp'), may hold values from -6 to 6
- outward_second: float32 [2, 2048, 2048], P('pipe', 'tensor', 'dp'), may hold values from 7.3728 to 29.4912
- expand_first: float32 [2, 2048, 8192], P('pipe', 'dp', 'tensor'), may hold values from -16 to 16
- expand_second: float32 [2, 2048, 8192], P('pipe', 'dp', 'tensor'), may hold values from 29.4912 to 117.9648
- contract_first: float32 [2, 8192, 2048], P('pipe', 'tensor', 'dp'), may hold values from -32 to 32
- contract_second: float32 [2, 8192, 2048], P('pipe', 'tensor', 'dp'), may hold values from 117.9648 to 471.8592
- vectors_first: float32 [2, 5, 2048], P('pipe', None, 'dp'), may hold values from -96 to 96
- vectors_second: float32 [2, 5, 2048], P('pipe', None, 'dp'), may hold values from 1310.72 to 5242.88
- offsets_first: float32 [2, 8192], P('pipe', ('tensor', 'dp')), may hold values from -16 to 16
- offsets_second: float32 [2, 8192], P('pipe', ('tensor', 'dp')), may hold values from 29.4912 to 117.9648
Outputs:
- activations: bfloat16 [2, 8, 1024, 2048], P('pipe', 'dp', 'tensor')
- input_grads: float32 [2, 8, 1024, 2048], P('pipe', 'dp', 'tensor')
- inward_new: float32 [2, 2048, 3, 2048], P('pipe', 'dp', None, 'tensor')
- inward_moment: float32 [2, 2048, 3, 2048], P('pipe', 'dp', None, 'tensor')
- inward_square: float32 [2, 2048, 3, 2048], P('pipe', 'dp', None, 'tensor')
- outward_new: float32 [2, 2048, 2048], P('pipe', 'tensor', 'dp')
- outward_moment: float32 [2, 2048, 2048], P('pipe', 'tensor', 'dp')
- outward_square: float32 [2, 2048, 2048], P('pipe', 'tensor', 'dp')
- expand_new: float32 [2, 2048, 8192], P('pipe', 'dp', 'tensor')
- expand_moment: float32 [2, 2048, 8192], P('pipe', 'dp', 'tensor')
- expand_square: float32 [2, 2048, 8192], P('pipe', 'dp', 'tensor')
- contract_new: float32 [2, 8192, 2048], P('pipe', 'tensor', 'dp')
- contract_moment: float32 [2, 8192, 2048], P('pipe', 'tensor', 'dp')
- contract_square: float32 [2, 8192, 2048], P('pipe', 'tensor', 'dp')
- vectors_new: float32 [2, 5, 2048], P('pipe', None, 'dp')
- vectors_moment: float32 [2, 5, 2048], P('pipe', None, 'dp')
- vectors_square: float32 [2, 5, 2048], P('pipe', None, 'dp')
- offsets_new: float32 [2, 8192], P('pipe', ('tensor', 'dp'))
- offsets_moment: float32 [2, 8192], P('pipe', ('tensor', 'dp'))
- offsets_square: float32 [2, 8192], P('pipe', ('tensor', 'dp'))
Inputs may be any that keep to these rules, and one draw needn't show every extreme that they name: `lengths`: valid slots of each sequence; some sequence is full (1024 valid slots). `vectors`: rows 0 and 2 of each section (the norms' gains) are positive.
All inputs are finite; a program needn't handle non-finite values.
Results may differ from a plain program's by a relative error of at most 0.025.
Values may be sent and summed in bfloat16 or wider, within the bound.
No kernel may reach another device: no remote copies, remote signals or barrier semaphores. Data moves between devices by JAX's collectives and lax.ppermute only.
A program may use at most 832 MiB of HBM per device.

v0:
```python
import jax
import jax.numpy as jnp
from jax import lax
from jax.sharding import PartitionSpec as P

HEAD_DIM = 256
ROT = 64
STEP = 10


RATES = (0.03, 0.2, 0.03, 0.015, 0.3, 0.3)
DECAYS = (0.01, 0.01, 0.01, 0.01, 0.0, 0.0)


def passed_along(array, axis, by):
    peers = lax.axis_size(axis)
    pairs = [(i, i + by) for i in range(peers) if 0 <= i + by < peers]
    return lax.ppermute(array, axis, pairs)


def angle_tables(slots):
    half = ROT // 2
    positions = jnp.arange(slots).astype(jnp.float32)
    frequency = 10000.0 ** (-(2.0 * jnp.arange(half).astype(jnp.float32)) / ROT)
    angles = positions[:, None] * frequency[None, :]
    return (jnp.cos(angles)[:, None, :], jnp.sin(angles)[:, None, :])


def rotate(block, cosine, sine):
    half = cosine.shape[-1]
    first = block[..., :half]
    second = block[..., half : 2 * half]
    return jnp.concatenate(
        [first * cosine - second * sine, second * cosine + first * sine, block[..., 2 * half :]],
        axis=-1,
    )


def rotate_back(grad, cosine, sine):
    half = cosine.shape[-1]
    first = grad[..., :half]
    second = grad[..., half : 2 * half]
    return jnp.concatenate(
        [first * cosine + second * sine, second * cosine - first * sine, grad[..., 2 * half :]],
        axis=-1,
    )


def norm_parts(rows, gain, shift):
    center = rows - jnp.mean(rows, axis=1, keepdims=True)
    scale = lax.rsqrt(jnp.mean(center * center, axis=1, keepdims=True) + 1e-05)
    normed = center * scale
    return (normed * gain + shift, normed, scale)


def norm_back(back, rows, gain):
    unused, normed, scale = norm_parts(rows, gain, 0.0)
    hat = back * gain
    row_grad = scale * (
        hat
        - jnp.mean(hat, axis=1, keepdims=True)
        - normed * jnp.mean(hat * normed, axis=1, keepdims=True)
    )
    return (row_grad, jnp.sum(back * normed, axis=0), jnp.sum(back, axis=0))


def gelu_slope(hidden):
    return (
        0.5 * (1.0 + lax.erf(hidden * 0.7071067811865476))
        + hidden * jnp.exp(-0.5 * hidden * hidden) * 0.3989422804014327
    )


def allowed_mask(slots, length):
    places = jnp.arange(slots)
    return (places[None, :] <= places[:, None]) & (places[None, :] < length)


def guarded(active, function, operand):
    return lax.cond(
        active, function, lambda packed: jax.tree.map(jnp.zeros_like, function(packed)), operand
    )


def forward_local(rows, length, working, tables):
    inward, outward, expand, contract, vectors, offsets = working
    vector_values = vectors.astype(jnp.float32)
    slots, width = rows.shape
    cosine, sine = tables
    first_in = norm_parts(rows, vector_values[0], vector_values[1])[0].astype(jnp.bfloat16)
    second_in = norm_parts(rows, vector_values[2], vector_values[3])[0].astype(jnp.bfloat16)
    heads_local = inward.shape[2] // HEAD_DIM
    mixed = jnp.dot(first_in, inward.reshape(width, -1), preferred_element_type=jnp.float32)
    mixed = mixed.reshape(slots, 3, heads_local, HEAD_DIM)
    query = rotate(mixed[:, 0], cosine, sine).astype(jnp.bfloat16)
    keys = rotate(mixed[:, 1], cosine, sine).astype(jnp.bfloat16)
    values = mixed[:, 2].astype(jnp.bfloat16)
    scores = jnp.einsum(
        "qhd,khd->hqk", query, keys, preferred_element_type=jnp.float32
    ) * HEAD_DIM ** (-0.5)
    scores = jnp.where(allowed_mask(slots, length)[None], scores, -jnp.inf)
    peak = jnp.max(scores, axis=-1, keepdims=True)
    expo = jnp.exp(scores - peak)
    total = jnp.sum(expo, axis=-1, keepdims=True)
    probs_low = (expo / total).astype(jnp.bfloat16)
    logsum = peak + jnp.log(total)
    heads_out = jnp.einsum("hqk,khd->qhd", probs_low, values, preferred_element_type=jnp.float32)
    heads_out = heads_out.reshape(slots, -1).astype(jnp.bfloat16)
    hidden = jnp.dot(second_in, expand, preferred_element_type=jnp.float32) + offsets.astype(
        jnp.float32
    )
    activated = jax.nn.gelu(hidden, approximate=False).astype(jnp.bfloat16)
    partial_value = jnp.dot(heads_out, outward, preferred_element_type=jnp.float32)
    partial_value = partial_value + jnp.dot(activated, contract, preferred_element_type=jnp.float32)
    saved = (first_in, second_in, query, keys, values, logsum, heads_out, hidden, activated)
    return (partial_value, saved)


def backward_local(rows, upstream, length, working, saved, tables):
    inward, outward, expand, contract, vectors, offsets = working
    vector_values = vectors.astype(jnp.float32)
    first_in, second_in, query, keys, values, logsum, heads_out, hidden, activated = saved
    slots, width = rows.shape
    cosine, sine = tables
    heads_local = query.shape[1]
    grad_low = upstream.astype(jnp.bfloat16)
    bias_grad = jnp.sum(upstream, axis=0)
    contract_grad = jnp.dot(activated.T, grad_low, preferred_element_type=jnp.float32)
    lifted = jnp.dot(grad_low, contract.T, preferred_element_type=jnp.float32)
    hidden_grad = (lifted * gelu_slope(hidden)).astype(jnp.bfloat16)
    offsets_grad = jnp.sum(hidden_grad.astype(jnp.float32), axis=0)
    expand_grad = jnp.dot(second_in.T, hidden_grad, preferred_element_type=jnp.float32)
    second_back = jnp.dot(hidden_grad, expand.T, preferred_element_type=jnp.float32)
    outward_grad = jnp.dot(heads_out.T, grad_low, preferred_element_type=jnp.float32)
    out_grad = jnp.dot(grad_low, outward.T, preferred_element_type=jnp.float32).astype(jnp.bfloat16)
    out_grad = out_grad.reshape(slots, heads_local, HEAD_DIM)
    scores = jnp.einsum(
        "qhd,khd->hqk", query, keys, preferred_element_type=jnp.float32
    ) * HEAD_DIM ** (-0.5)
    probs = jnp.where(allowed_mask(slots, length)[None], jnp.exp(scores - logsum), 0.0)
    probs_low = probs.astype(jnp.bfloat16)
    prob_grad = jnp.einsum("qhd,khd->hqk", out_grad, values, preferred_element_type=jnp.float32)
    value_grad = jnp.einsum("hqk,qhd->khd", probs_low, out_grad, preferred_element_type=jnp.float32)
    score_grad = (probs * (prob_grad - jnp.sum(probs * prob_grad, axis=-1, keepdims=True))).astype(
        jnp.bfloat16
    )
    query_grad = jnp.einsum(
        "hqk,khd->qhd", score_grad, keys, preferred_element_type=jnp.float32
    ) * HEAD_DIM ** (-0.5)
    key_grad = jnp.einsum(
        "hqk,qhd->khd", score_grad, query, preferred_element_type=jnp.float32
    ) * HEAD_DIM ** (-0.5)
    query_grad = rotate_back(query_grad, cosine, sine)
    key_grad = rotate_back(key_grad, cosine, sine)
    mixed_grad = (
        jnp.stack([query_grad, key_grad, value_grad], axis=1)
        .reshape(slots, -1)
        .astype(jnp.bfloat16)
    )
    inward_grad = jnp.dot(first_in.T, mixed_grad, preferred_element_type=jnp.float32).reshape(
        width, 3, -1
    )
    first_back = jnp.dot(
        mixed_grad, inward.reshape(width, -1).T, preferred_element_type=jnp.float32
    )
    first_rows, first_gain, first_shift = norm_back(first_back, rows, vector_values[0])
    second_rows, second_gain, second_shift = norm_back(second_back, rows, vector_values[2])
    norm_grads = jnp.stack([first_gain, first_shift, second_gain, second_shift])
    return (
        first_rows + second_rows,
        norm_grads,
        bias_grad,
        inward_grad,
        outward_grad,
        expand_grad,
        contract_grad,
        offsets_grad,
    )


def adam_update(master, grad, first, second, rate, decay):
    new_first = 0.9 * first + 0.1 * grad
    new_second = 0.95 * second + 0.05 * grad * grad
    corrected = new_first / (1.0 - 0.9**STEP)
    spread = jnp.sqrt(new_second / (1.0 - 0.95**STEP))
    return (master - rate * (corrected / (spread + 1e-08) + decay * master), new_first, new_second)


def local(
    tokens,
    cotangent,
    lengths,
    inward,
    outward,
    expand,
    contract,
    vectors,
    offsets,
    inward_first,
    inward_second,
    outward_first,
    outward_second,
    expand_first,
    expand_second,
    contract_first,
    contract_second,
    vectors_first,
    vectors_second,
    offsets_first,
    offsets_second,
):
    section = lax.axis_index("pipe")
    working = (
        lax.all_gather(inward[0].astype(jnp.bfloat16), "dp", axis=0, tiled=True),
        lax.all_gather(outward[0].astype(jnp.bfloat16), "dp", axis=1, tiled=True),
        lax.all_gather(expand[0].astype(jnp.bfloat16), "dp", axis=0, tiled=True),
        lax.all_gather(contract[0].astype(jnp.bfloat16), "dp", axis=1, tiled=True),
        lax.all_gather(vectors[0].astype(jnp.bfloat16), "dp", axis=1, tiled=True),
        lax.all_gather(offsets[0].astype(jnp.bfloat16), "dp", axis=0, tiled=True),
    )
    vector_values = working[4].astype(jnp.float32)
    batches = lengths.shape[0]
    width = tokens.shape[1]
    slots = tokens.shape[0] // batches
    row_share = slots // lax.axis_size("tensor")
    row_start = lax.axis_index("tensor") * row_share
    tables = angle_tables(slots)
    inputs = tokens.reshape(batches, slots, width)
    targets = cotangent.reshape(batches, slots, width)
    received = jnp.zeros((slots, width), jnp.bfloat16)
    produced = jnp.zeros((batches, row_share, width), jnp.bfloat16)
    kept = []
    for turn in range(batches + 1):
        index = turn - section
        active = (index >= 0) & (index < batches)
        place = jnp.clip(index, 0, batches - 1)
        own = lax.dynamic_index_in_dim(inputs, place, 0, keepdims=False)
        arrived = received
        rows = jnp.where(section == 0, own, arrived).astype(jnp.float32)
        length = lengths[place]
        partial_value, saved = guarded(
            active, lambda operand: forward_local(operand, length, working, tables), rows
        )
        summed = lax.psum(partial_value.astype(jnp.bfloat16), "tensor").astype(jnp.float32)
        whole = (rows + summed + vector_values[4]).astype(jnp.bfloat16)
        result = lax.dynamic_slice_in_dim(whole, row_start, row_share, 0)
        received = passed_along(whole, "pipe", 1)
        produced = jnp.where(
            active, lax.dynamic_update_index_in_dim(produced, result, place, 0), produced
        )
        kept.append((rows, saved))
    stacked = jax.tree.map(lambda *items: jnp.stack(items), *kept)
    totals = tuple((jnp.zeros(item.shape, jnp.float32) for item in working))
    coming = jnp.zeros((slots, width), jnp.bfloat16)
    gradients = jnp.zeros((batches, row_share, width), jnp.float32)
    for turn in range(batches + 1):
        index = turn - (1 - section)
        active = (index >= 0) & (index < batches)
        place = jnp.clip(index, 0, batches - 1)
        length = lengths[place]
        valid = (jnp.arange(slots) < length).astype(jnp.float32)[:, None]
        own = (
            lax.dynamic_index_in_dim(targets, place, 0, keepdims=False).astype(jnp.float32) * valid
        )
        own = own * active.astype(jnp.float32)
        arrived = coming
        upstream = jnp.where(section == 1, own, arrived.astype(jnp.float32))
        source = jnp.clip(place + section, 0, batches)
        rows, saved = jax.tree.map(
            lambda item: lax.dynamic_index_in_dim(item, source, 0, keepdims=False), stacked
        )
        results = guarded(
            active,
            lambda packed: backward_local(packed[0], packed[1], length, working, packed[2], tables),
            (rows, upstream, saved),
        )
        (
            row_part,
            norm_part,
            bias_grad,
            inward_grad,
            outward_grad,
            expand_grad,
            contract_grad,
            offsets_grad,
        ) = results
        row_sum, norm_sum = (
            lax.psum(row_part.astype(jnp.bfloat16), "tensor").astype(jnp.float32),
            lax.psum(norm_part.astype(jnp.bfloat16), "tensor").astype(jnp.float32),
        )
        whole_grad = upstream + row_sum
        row_grad = lax.dynamic_slice_in_dim(whole_grad, row_start, row_share, 0)
        coming = passed_along(whole_grad.astype(jnp.bfloat16), "pipe", -1)
        vector_grad = jnp.concatenate([norm_sum, bias_grad[None]], axis=0)
        gradients = jnp.where(
            active, lax.dynamic_update_index_in_dim(gradients, row_grad, place, 0), gradients
        )
        totals = (
            totals[0] + inward_grad,
            totals[1] + outward_grad,
            totals[2] + expand_grad,
            totals[3] + contract_grad,
            totals[4] + vector_grad,
            totals[5] + offsets_grad,
        )
    reduced = (
        lax.psum_scatter(
            totals[0].astype(jnp.bfloat16), "dp", scatter_dimension=0, tiled=True
        ).astype(jnp.float32),
        lax.psum_scatter(
            totals[1].astype(jnp.bfloat16), "dp", scatter_dimension=1, tiled=True
        ).astype(jnp.float32),
        lax.psum_scatter(
            totals[2].astype(jnp.bfloat16), "dp", scatter_dimension=0, tiled=True
        ).astype(jnp.float32),
        lax.psum_scatter(
            totals[3].astype(jnp.bfloat16), "dp", scatter_dimension=1, tiled=True
        ).astype(jnp.float32),
        lax.psum_scatter(
            totals[4].astype(jnp.bfloat16), "dp", scatter_dimension=1, tiled=True
        ).astype(jnp.float32),
        lax.psum_scatter(
            totals[5].astype(jnp.bfloat16), "dp", scatter_dimension=0, tiled=True
        ).astype(jnp.float32),
    )
    masters = (inward, outward, expand, contract, vectors, offsets)
    firsts = (
        inward_first,
        outward_first,
        expand_first,
        contract_first,
        vectors_first,
        offsets_first,
    )
    seconds = (
        inward_second,
        outward_second,
        expand_second,
        contract_second,
        vectors_second,
        offsets_second,
    )
    updated = [
        adam_update(masters[i], reduced[i][None], firsts[i], seconds[i], RATES[i], DECAYS[i])
        for i in range(6)
    ]
    activations = produced[None]
    input_grads = gradients[None]
    return (
        activations,
        input_grads,
        updated[0][0],
        updated[0][1],
        updated[0][2],
        updated[1][0],
        updated[1][1],
        updated[1][2],
        updated[2][0],
        updated[2][1],
        updated[2][2],
        updated[3][0],
        updated[3][1],
        updated[3][2],
        updated[4][0],
        updated[4][1],
        updated[4][2],
        updated[5][0],
        updated[5][1],
        updated[5][2],
    )


def solution(mesh):
    return jax.shard_map(
        local,
        mesh=mesh,
        in_specs=(
            P("dp", None),
            P("dp", None),
            P("dp"),
            P("pipe", "dp", None, "tensor"),
            P("pipe", "tensor", "dp"),
            P("pipe", "dp", "tensor"),
            P("pipe", "tensor", "dp"),
            P("pipe", None, "dp"),
            P("pipe", ("tensor", "dp")),
            P("pipe", "dp", None, "tensor"),
            P("pipe", "dp", None, "tensor"),
            P("pipe", "tensor", "dp"),
            P("pipe", "tensor", "dp"),
            P("pipe", "dp", "tensor"),
            P("pipe", "dp", "tensor"),
            P("pipe", "tensor", "dp"),
            P("pipe", "tensor", "dp"),
            P("pipe", None, "dp"),
            P("pipe", None, "dp"),
            P("pipe", ("tensor", "dp")),
            P("pipe", ("tensor", "dp")),
        ),
        out_specs=(
            P("pipe", "dp", "tensor", None),
            P("pipe", "dp", "tensor", None),
            P("pipe", "dp", None, "tensor"),
            P("pipe", "dp", None, "tensor"),
            P("pipe", "dp", None, "tensor"),
            P("pipe", "tensor", "dp"),
            P("pipe", "tensor", "dp"),
            P("pipe", "tensor", "dp"),
            P("pipe", "dp", "tensor"),
            P("pipe", "dp", "tensor"),
            P("pipe", "dp", "tensor"),
            P("pipe", "tensor", "dp"),
            P("pipe", "tensor", "dp"),
            P("pipe", "tensor", "dp"),
            P("pipe", None, "dp"),
            P("pipe", None, "dp"),
            P("pipe", None, "dp"),
            P("pipe", ("tensor", "dp")),
            P("pipe", ("tensor", "dp")),
            P("pipe", ("tensor", "dp")),
        ),
        check_vma=False,
    )
```

profile of v0, /device:TPU:0, one launch (start us, length us, event | category | flops | bytes accessed | tf_op | source)
XLA Modules:
  0.0 2526.8 jit_solution(9178591907707514167)
XLA Ops:
  20.4 14.0 all-gather.4
  34.3 13.4 all-gather
  59.4 116.3 %all-gather.11.cloned.1.call-done = bf16[1,2048,3,512]{1,3,2,0:T(8,128)(2,1)} async-done(((bf16[1,512,3,512]{1,3,2,0:T(8,128)(2,1)}), bf16[1,2048,3,512]{1,3,2,0:T(8,128)(2,1)}) %all-gather.11.cloned.1.call-update) | async-done | bytes 6291472 | tf_op jit(solution)/shard_map/all_gather | solution.py:214
  175.7 150.0 %all-gather.15.cloned.1.call-done = bf16[1,2048,2048]{2,1,0:T(8,128)(2,1)} async-done(((bf16[1,512,2048]{2,1,0:T(8,128)(2,1)}), bf16[1,2048,2048]{2,1,0:T(8,128)(2,1)}) %all-gather.15.cloned.1.call-update) | async-done | bytes 8388624 | tf_op jit(solution)/shard_map/all_gather | solution.py:216
  325.7 149.9 %all-gather.17.cloned.1.call-done = bf16[1,2048,2048]{2,1,0:T(8,128)(2,1)} async-done(((bf16[1,2048,512]{2,1,0:T(8,128)(2,1)}), bf16[1,2048,2048]{2,1,0:T(8,128)(2,1)}) %all-gather.17.cloned.1.call-update) | async-done | bytes 8388624 | tf_op jit(solution)/shard_map/all_gather | solution.py:217
  475.6 117.5 %conditional.6 = (bf16[1024,2048]{1,0:T(8,128)(2,1)}, bf16[1,1024,2048]{2,1,0:T(8,128)(2,1)}, f32[1,2,1024,1]{2,1,3,0:T(2,128)S(1)}, f32[1,1024,2048]{2,1,0:T(8,...) conditional(s32[]{:T(128)} %convert_element_type.777, ...), branch_computations={%region_0.1_spmd, %region_1.6_spmd} | conditional | flops 28147451904 | bytes 254552336 | solution.py:80
  485.1 14.2 fusion.12
  503.4 33.8 %add_bitcast_fusion = (f32[1,1024,2048]{2,1,0:T(8,128)}, bf16[1024,2048]{1,0:T(8,128)(2,1)}) fusion(f32[2048]{0:T(1024)S(1)} %convert_element_type.550, bf16[2048,2048]{1,0:T(8,128)(2,1)} %get-tuple-element.710, f32[1024,2048]{1,0:T(8,128)} %get-tuple-element.696, f32[2048]{0:T(1024)S(1)} %bitcast.740, f32[2048]{0:T(1024)S(1)} %bitcast.738, ...), kind=kOutput, calls=%fused_computation.25 | convolution fusion | flops 8738832384 | bytes 29392896 | tf_op jit(solution)/shard_map/cond/branch_1_fun/dot_general | solution.py:109
  544.2 14.7 fusion.340
  593.2 102.1 %all-reduce.9.cloned.1.call-done = bf16[1024,2048]{1,0:T(8,128)(2,1)} async-done(((bf16[1024,2048]{1,0:T(8,128)(2,1)}), bf16[1024,2048]{1,0:T(8,128)(2,1)}) %all-reduce.9.cloned.1.call-update) | async-done | bytes 4194320 | tf_op jit(solution)/shard_map/psum | solution.py:244
  718.1 117.3 %conditional.7 = (bf16[1024,2048]{1,0:T(8,128)(2,1)}, bf16[1,1024,2048]{2,1,0:T(8,128)(2,1)}, f32[1,2,1024,1]{2,1,3,0:T(2,128)S(1)}, f32[1,1024,2048]{2,1,0:T(8,...) conditional(s32[]{:T(128)} %convert_element_type.796, ...), branch_computations={%region_7.8_spmd, %region_8.0_spmd} | conditional | flops 28147451904 | bytes 254552336 | solution.py:80
  727.6 14.2 fusion.48
  746.0 33.7 %add_bitcast_fusion.2 = (f32[1,1024,2048]{2,1,0:T(8,128)}, bf16[1024,2048]{1,0:T(8,128)(2,1)}) fusion(f32[2048]{0:T(1024)S(1)} %convert_element_type.563, bf16[2048,2048]{1,0:T(8,128)(2,1)} %get-tuple-element.727, f32[1024,2048]{1,0:T(8,128)} %get-tuple-element.713, f32[2048]{0:T(1024)S(1)} %bitcast.748, f32[2048]{0:T(1024)S(1)} %bitcast.746, ...), kind=kOutput, calls=%fused_computation.94 | convolution fusion | flops 8738832384 | bytes 29392896 | tf_op jit(solution)/shard_map/cond/branch_1_fun/dot_general | solution.py:109
  786.7 14.7 fusion.341
  837.1 103.8 %all-reduce.11.cloned.1.call-done = bf16[1024,2048]{1,0:T(8,128)(2,1)} async-done(((bf16[1024,2048]{1,0:T(8,128)(2,1)}), bf16[1024,2048]{1,0:T(8,128)(2,1)}) %all-reduce.11.cloned.1.call-update) | async-done | bytes 4194320 | tf_op jit(solution)/shard_map/psum | solution.py:244
  1018.9 25.5 %conditional.8 = (bf16[1024,2048]{1,0:T(8,128)(2,1)}, bf16[1,1024,2048]{2,1,0:T(8,128)(2,1)}, f32[1,2,1024,1]{2,1,3,0:T(2,128)S(1)}, f32[1,1024,2048]{2,1,0:T(8,...) conditional(s32[]{:T(128)} %convert_element_type.801, ...), branch_computations={%region_14.15_spmd, %region_15.20_spmd} | conditional | flops 28147451904 | bytes 254552336 | solution.py:80
  1076.6 12.2 pad_maximum_fusion.9
  1088.8 33.4 %conditional.9 = (bf16[1024,2048]{1,0:T(8,128)(2,1)}, bf16[4,2048]{1,0:T(4,128)(2,1)}, f32[2048,3,512]{2,0,1:T(8,128)}, f32[512,2048]{1,0:T(8,128)}, f32[2048,20...) conditional(s32[]{:T(128)} %convert_element_type.809, () %tuple.134, ...), branch_computations={%region_21.22_spmd, %region_22.36_spmd} | conditional | flops 57052549120 | bytes 402496864 | solution.py:80
  1122.3 295.5 %all-reduce.13.cloned.1.call-done = bf16[1024,2048]{1,0:T(8,128)(2,1)} async-done(((bf16[1024,2048]{1,0:T(8,128)(2,1)}), bf16[1024,2048]{1,0:T(8,128)(2,1)}) %all-reduce.13.cloned.1.call-update) | async-done | bytes 4194320 | tf_op jit(solution)/shard_map/psum | solution.py:288
  1435.4 9.1 fusion.276
  1444.5 132.9 %conditional.10 = (bf16[1024,2048]{1,0:T(8,128)(2,1)}, bf16[4,2048]{1,0:T(4,128)(2,1)}, f32[2048,3,512]{2,0,1:T(8,128)}, f32[512,2048]{1,0:T(8,128)}, f32[2048,2...) conditional(s32[]{:T(128)} %convert_element_type.819, () %tuple.136, ...), branch_computations={%region_37.38_spmd, %region_38.52_spmd} | conditional | flops 57052549120 | bytes 402496864 | solution.py:80
  1455.7 15.6 convert_reduce_fusion.1
  1473.7 13.8 fusion.338
  1487.6 14.4 fusion.178
  1507.6 14.2 fusion.176
  1537.8 11.6 fusion.180
  1549.4 17.2 multiply_reduce_fusion.12
  1567.2 10.2 add_multiply_fusion.1
  1577.5 104.0 %all-reduce.15.cloned.1.call-done = bf16[1024,2048]{1,0:T(8,128)(2,1)} async-done(((bf16[1024,2048]{1,0:T(8,128)(2,1)}), bf16[1024,2048]{1,0:T(8,128)(2,1)}) %all-reduce.15.cloned.1.call-update) | async-done | bytes 4194320 | tf_op jit(solution)/shard_map/psum | solution.py:288
  1681.4 11.7 fusion.325
  1711.5 132.6 %conditional.11 = (bf16[1024,2048]{1,0:T(8,128)(2,1)}, bf16[4,2048]{1,0:T(4,128)(2,1)}, f32[2048,3,512]{2,0,1:T(8,128)}, f32[512,2048]{1,0:T(8,128)}, f32[2048,2...) conditional(s32[]{:T(128)} %convert_element_type.828, () %tuple.138, ...), branch_computations={%region_53.54_spmd, %region_54.0_spmd} | conditional | flops 57052549120 | bytes 415079808 | solution.py:80
  1722.9 15.9 convert_reduce_fusion.2
  1741.3 13.8 fusion.339
  1755.1 14.2 fusion.233
  1775.0 14.2 fusion.231
  1804.9 12.7 fusion.235
  1817.6 17.2 multiply_reduce_fusion.20
  1844.1 16.3 all-reduce.1
  1869.1 16.2 add_convert_fusion.20
  1885.3 20.8 add_convert_fusion.18
  1906.2 20.4 add_convert_fusion.19
  1943.0 12.0 all-reduce
  1961.7 139.6 %all-reduce.17.cloned.1.call-done = (bf16[1024,2048]{1,0:T(8,128)(2,1)}, bf16[1024,2048]{1,0:T(8,128)(2,1)}) async-done(((bf16[1024,2048]{1,0:T(8,128)(2,1)}, bf16[1024,2048]{1,0:T(8,128)(2,1)}), (bf16[1024,2048]{1,0:T(8,128)(2,1)}, bf16[1024,2048]{1,0:T(8,128)(2,1)})) %all-reduce.17.cloned.1.call-update) | async-done | bytes 8388624 | tf_op jit(solution)/shard_map/psum | solution.py:244
  2109.0 106.0 %reduce-scatter.6.cloned.1.call-done = bf16[512,3,512]{2,0,1:T(8,128)(2,1)} async-done(((bf16[2048,3,512]{2,0,1:T(8,128)(2,1)}), bf16[512,3,512]{2,0,1:T(8,128)(2,1)}) %reduce-scatter.6.cloned.1.call-update) | async-done | bytes 1572880 | tf_op jit(solution)/shard_map/reduce_scatter | solution.py:307
  2222.6 140.0 %reduce-scatter.12.cloned.1.call-done = bf16[2048,512]{1,0:T(8,128)(2,1)} async-done(((bf16[2048,2048]{1,0:T(8,128)(2,1)}), bf16[2048,512]{1,0:T(8,128)(2,1)}) %reduce-scatter.12.cloned.1.call-update) | async-done | bytes 2097168 | tf_op jit(solution)/shard_map/reduce_scatter | solution.py:316
  2362.6 9.9 multiply_subtract_fusion.6
  2372.5 137.6 %reduce-scatter.10.cloned.1.call-done = bf16[512,2048]{1,0:T(8,128)(2,1)} async-done(((bf16[2048,2048]{1,0:T(8,128)(2,1)}), bf16[512,2048]{1,0:T(8,128)(2,1)}) %reduce-scatter.10.cloned.1.call-update) | async-done | bytes 2097168 | tf_op jit(solution)/shard_map/reduce_scatter | solution.py:313
  2510.1 9.9 multiply_subtract_fusion.7
  (387 shorter events, 476.6 us)
Async XLA Ops:
  7.2 52.2 %all-gather.13.cloned.1.call-start = ((), (), s32[]{:S(2)}) async-start(), calls=%async_computation.15 | async-start | bytes 2621440 | tf_op jit(solution)/shard_map/all_gather | solution.py:215
  9.3 166.4 %all-gather.11.cloned.1.call-start = ((), (), s32[]{:S(2)}) async-start(), calls=%async_computation.14 | async-start | bytes 7864320 | tf_op jit(solution)/shard_map/all_gather | solution.py:214
  12.5 313.3 %all-gather.15.cloned.1.call-start = ((), (), s32[]{:S(2)}) async-start(), calls=%async_computation.16 | async-start | bytes 10485760 | tf_op jit(solution)/shard_map/all_gather | solution.py:216
  16.4 459.2 %all-gather.17.cloned.1.call-start = ((), (), s32[]{:S(2)}) async-start(), calls=%async_computation.17 | async-start | bytes 10485760 | tf_op jit(solution)/shard_map/all_gather | solution.py:217
  20.2 675.1 %all-reduce.9.cloned.1.call-start = ((), (), s32[]{:S(2)}) async-start(), calls=%async_computation.5 | async-start | bytes 8388608 | tf_op jit(solution)/shard_map/psum | solution.py:244
  48.3 427.4 %copy-start.45 = (s32[2]{0:T(128)S(1)}, s32[2]{0:T(128)}, u32[]{:S(2)}) copy-start(s32[2]{0:T(128)} %param.35) | copy-start | bytes 28
  593.1 110.2 %copy-start.39 = (f32[1,2,1024,1]{2,1,3,0:T(2,128)}, f32[1,2,1024,1]{2,1,3,0:T(2,128)S(1)}, u32[]{:S(2)}) copy-start(f32[1,2,1024,1]{2,1,3,0:T(2,128)S(1)} %get-tuple-element.911) | copy-start | bytes 24580
  593.2 347.7 %all-reduce.11.cloned.1.call-start = ((), (), s32[]{:S(2)}) async-start(), calls=%async_computation.6 | async-start | bytes 8388608 | tf_op jit(solution)/shard_map/psum | solution.py:244
  593.2 124.9 %copy-start.23 = (f32[1,1,2048]{2,1,0:T(1,128)}, f32[1,1,2048]{2,1,0:T(1,128)S(1)}, u32[]{:S(2)}) copy-start(f32[1,1,2048]{2,1,0:T(1,128)S(1)} %slice_convert_fusion.12) | copy-start | bytes 24580
  703.3 8.8 collective-permute-start
  718.1 222.7 %copy-start.24 = (f32[1,1,2048]{2,1,0:T(1,128)S(1)}, f32[1,1,2048]{2,1,0:T(1,128)}, u32[]{:S(2)}) copy-start(f32[1,1,2048]{2,1,0:T(1,128)} %copy-done.23) | copy-start | bytes 24580
  835.5 582.3 %all-reduce.13.cloned.1.call-start = ((), (), s32[]{:S(2)}) async-start(), calls=%async_computation.7 | async-start | bytes 8388608 | tf_op jit(solution)/shard_map/psum | solution.py:288
  837.1 113.6 %copy-start.30 = (f32[1024]{0:T(1024)}, f32[1024]{0:T(1024)S(1)}, u32[]{:S(2)}) copy-start(f32[1024]{0:T(1024)S(1)} %fusion.314) | copy-start | bytes 12292
  946.9 67.6 %collective-permute-start.1 = (bf16[1024,2048]{1,0:T(8,128)(2,1)S(1)}, bf16[1024,2048]{1,0:T(8,128)(2,1)}, u32[]{:S(2)}, u32[]{:S(2)}) collective-permute-start(bf16[1024,2048]{1,0:T(8,128)(2,1)S(1)} %add_convert_fusion.21), channel_id=1, source_target_pairs={{0,16},{1,17},{2,18},{3,19},{4,20},{5,21},{6,22},{7,23},{8,24},{9,... | collective-permute-start | bytes 12582920 | tf_op jit(solution)/shard_map/ppermute | solution.py:18
  986.9 14.9 copy-start.22
  1056.3 20.3 slice-start.2
  1061.1 15.5 slice-start
  1061.1 14.2 copy-start.2
  1061.1 15.5 slice-start.1
  1061.1 15.5 slice-start.3
  1088.8 329.0 %copy-start.31 = (f32[1024]{0:T(1024)S(1)}, f32[1024]{0:T(1024)}, u32[]{:S(2)}) copy-start(f32[1024]{0:T(1024)} %copy-done.30) | copy-start | bytes 12292
  1122.2 303.8 %copy-start.33 = (f32[1,2048]{1,0:T(1,128)}, f32[1,2048]{1,0:T(1,128)S(1)}, u32[]{:S(2)}) copy-start(f32[1,2048]{1,0:T(1,128)S(1)} %get-tuple-element.948) | copy-start | bytes 24580
  1122.3 559.2 %all-reduce.15.cloned.1.call-start = ((), (), s32[]{:S(2)}) async-start(), calls=%async_computation.8 | async-start | bytes 8388608 | tf_op jit(solution)/shard_map/psum | solution.py:288
  1426.0 9.4 collective-permute-start.2
  1455.7 15.6 copy-start.52
  1473.7 49.4 %copy-start.55 = (bf16[1024,512]{0,1:T(8,128)(2,1)}, bf16[1024,512]{0,1:T(8,128)(2,1)S(1)}, u32[]{:S(2)}) copy-start(bf16[1024,512]{0,1:T(8,128)(2,1)S(1)} %convolution_convert_fusion.1) | copy-start | bytes 3145732 | tf_op jit(solution)/shard_map/cond
  1507.6 14.2 copy-start.5
  1577.4 115.7 %copy-start.36 = (f32[1,2048]{1,0:T(1,128)}, f32[1,2048]{1,0:T(1,128)S(1)}, u32[]{:S(2)}) copy-start(f32[1,2048]{1,0:T(1,128)S(1)} %get-tuple-element.950) | copy-start | bytes 24580
  1577.4 378.3 %reduce-scatter.14.cloned.1.call-start = ((), (), s32[]{:S(2)}) async-start(), calls=%async_computation.13 | async-start | bytes 40960 | tf_op jit(solution)/shard_map/reduce_scatter | solution.py:319
  1693.1 9.4 collective-permute-start.3
  1711.5 148.9 %copy-start.34 = (f32[1,2048]{1,0:T(1,128)S(1)}, f32[1,2048]{1,0:T(1,128)}, u32[]{:S(2)}) copy-start(f32[1,2048]{1,0:T(1,128)} %copy-done.33) | copy-start | bytes 24580
  1711.5 148.9 %copy-start.37 = (f32[1,2048]{1,0:T(1,128)S(1)}, f32[1,2048]{1,0:T(1,128)}, u32[]{:S(2)}) copy-start(f32[1,2048]{1,0:T(1,128)} %copy-done.36) | copy-start | bytes 24580
  1722.9 16.0 copy-start.53
  1741.2 49.3 %copy-start.56 = (bf16[1024,512]{0,1:T(8,128)(2,1)}, bf16[1024,512]{0,1:T(8,128)(2,1)S(1)}, u32[]{:S(2)}) copy-start(bf16[1024,512]{0,1:T(8,128)(2,1)S(1)} %convolution_convert_fusion.2) | copy-start | bytes 3145732 | tf_op jit(solution)/shard_map/cond
  1775.0 14.2 copy-start.6
  1861.1 96.7 %reduce-scatter.8.cloned.1.call-start = ((), (), s32[]{:S(2)}) async-start(), calls=%async_computation.10 | async-start | bytes 2621440 | tf_op jit(solution)/shard_map/reduce_scatter | solution.py:310
  1868.3 233.0 %all-reduce.17.cloned.1.call-start = ((), (), s32[]{:S(2)}) async-start(), calls=%async_computation.18 | async-start | bytes 16777216 | tf_op jit(solution)/shard_map/psum | solution.py:244
  1869.0 346.0 %reduce-scatter.6.cloned.1.call-start = ((), (), s32[]{:S(2)}) async-start(), calls=%async_computation.9 | async-start | bytes 7864320 | tf_op jit(solution)/shard_map/reduce_scatter | solution.py:307
  1885.3 477.3 %reduce-scatter.12.cloned.1.call-start = ((), (), s32[]{:S(2)}) async-start(), calls=%async_computation.12 | async-start | bytes 10485760 | tf_op jit(solution)/shard_map/reduce_scatter | solution.py:316
  1906.2 603.9 %reduce-scatter.10.cloned.1.call-start = ((), (), s32[]{:S(2)}) async-start(), calls=%async_computation.11 | async-start | bytes 10485760 | tf_op jit(solution)/shard_map/reduce_scatter | solution.py:313
  1936.1 19.0 copy-start.44
  1936.1 19.0 copy-start.46
  1936.1 19.0 copy-start.47
  1936.1 20.3 copy-start.41
  1936.1 21.0 copy-start.29
  1936.1 21.0 copy-start.42
  1936.1 21.7 copy-start.11
  1942.2 163.5 %copy-start.25 = (f32[1,1,2048]{2,1,0:T(1,128)S(1)}, f32[1,1,2048]{2,1,0:T(1,128)}, u32[]{:S(2)}) copy-start(f32[1,1,2048]{2,1,0:T(1,128)} %copy-done.23) | copy-start | bytes 24580
  (37 other events, 267.9 us)
Sparse Core Ops, SparseCore 0:
  10.2 49.2 all-gather.12
  61.6 114.1 all-gather.10
  177.9 147.8 all-gather.14
  327.7 147.8 all-gather.16
  593.3 102.0 all-reduce.8
  835.6 105.1 all-reduce.10
  1122.4 295.3 all-reduce.12
  1577.5 103.8 all-reduce.14
  1861.2 18.8 reduce-scatter.13
  1883.0 41.9 reduce-scatter.7
  1929.3 171.9 all-reduce.16
  2103.6 111.4 reduce-scatter.5
  2217.5 144.9 reduce-scatter.11
  2364.9 145.1 reduce-scatter.9
where the time goes:
time: 2540 us; the launch traced here: 2530 us
  waiting for transfers between devices  1570 us (62%)
  matrix products  366 us (14%)
  other arithmetic  308 us (12%)
  local copies, waits for them, and re-layouts  189 us (7%)
  blocking collectives  55.7 us (2%)
    psum x2, waiting for transfers between devices, local(): lax.psum(row_part.astype(jnp.bfloat16), 'tensor').astype(jnp.float32)  399 us
    psum x3, waiting for transfers between devices, local(): lax.psum(partial_value.astype(jnp.bfloat16), 'tensor').astype(jnp.float32)  345 us
    all_gather x1, waiting for transfers between devices, local(): lax.all_gather(expand[0].astype(jnp.bfloat16), 'dp', axis=0, tiled=True)  150 us
    all_gather x1, waiting for transfers between devices, local(): lax.all_gather(contract[0].astype(jnp.bfloat16), 'dp', axis=1, tiled=True)  150 us
    reduce_scatter x1, waiting for transfers between devices, local(): lax.psum_scatter(totals[3].astype(jnp.bfloat16), 'dp', scatter_dimension=...  140 us
    reduce_scatter x1, waiting for transfers between devices, local(): lax.psum_scatter(totals[2].astype(jnp.bfloat16), 'dp', scatter_dimension=...  138 us
    all_gather x1, waiting for transfers between devices, local(): lax.all_gather(inward[0].astype(jnp.bfloat16), 'dp', axis=0, tiled=True)  116 us
    reduce_scatter x1, waiting for transfers between devices, local(): lax.psum_scatter(totals[0].astype(jnp.bfloat16), 'dp', scatter_dimension=...  106 us
  transfers between devices with their start and end apart: 18, of which 15 were waited for; matrix products, arithmetic and copies ran while one was open for 8% of the time, Pallas kernels for 0%

commit v1 on v0

v1 whole, which is shorter than its diff:
```python
import functools

import jax
import jax.numpy as jnp
from jax import lax
from jax.experimental import pallas as pl
from jax.experimental.pallas import tpu as pltpu
from jax.sharding import PartitionSpec as P

HEAD_DIM = 256
ROT = 64
STEP = 10


RATES = (0.03, 0.2, 0.03, 0.015, 0.3, 0.3)
DECAYS = (0.01, 0.01, 0.01, 0.01, 0.0, 0.0)


def angle_tables(slots):
    half = ROT // 2
    positions = jnp.arange(slots).astype(jnp.float32)
    frequency = 10000.0 ** (-(2.0 * jnp.arange(half).astype(jnp.float32)) / ROT)
    angles = positions[:, None] * frequency[None, :]
    return (jnp.cos(angles)[:, None, :], jnp.sin(angles)[:, None, :])


def rotate(block, cosine, sine):
    half = cosine.shape[-1]
    first = block[..., :half]
    second = block[..., half : 2 * half]
    return jnp.concatenate(
        [first * cosine - second * sine, second * cosine + first * sine, block[..., 2 * half :]],
        axis=-1,
    )


def rotate_back(grad, cosine, sine):
    half = cosine.shape[-1]
    first = grad[..., :half]
    second = grad[..., half : 2 * half]
    return jnp.concatenate(
        [first * cosine + second * sine, second * cosine - first * sine, grad[..., 2 * half :]],
        axis=-1,
    )


def norm_parts(rows, gain, shift):
    center = rows - jnp.mean(rows, axis=1, keepdims=True)
    scale = lax.rsqrt(jnp.mean(center * center, axis=1, keepdims=True) + 1e-05)
    normed = center * scale
    return (normed * gain + shift, normed, scale)


def norm_back(back, rows, gain):
    unused, normed, scale = norm_parts(rows, gain, 0.0)
    hat = back * gain
    row_grad = scale * (
        hat
        - jnp.mean(hat, axis=1, keepdims=True)
        - normed * jnp.mean(hat * normed, axis=1, keepdims=True)
    )
    return (row_grad, jnp.sum(back * normed, axis=0), jnp.sum(back, axis=0))


def gelu_slope(hidden):
    return (
        0.5 * (1.0 + lax.erf(hidden * 0.7071067811865476))
        + hidden * jnp.exp(-0.5 * hidden * hidden) * 0.3989422804014327
    )


def allowed_mask(slots, length):
    places = jnp.arange(slots)
    return (places[None, :] <= places[:, None]) & (places[None, :] < length)


def after(array, *earlier):
    return lax.optimization_barrier((array, *earlier))[0]


def added(array, axis):
    peers = lax.axis_size(axis)
    bits = peers.bit_length() - 1
    if peers != 1 << bits:
        return lax.psum(array, axis)
    for bit in range(bits):
        array = array + lax.ppermute(array, axis, [(i, i ^ (1 << bit)) for i in range(peers)])
    return array


def swap(array):
    return lax.ppermute(array, "pipe", [(0, 1), (1, 0)])


def halves(array, core):
    size = array.shape[-1] // 2
    axis = array.ndim - 1
    mine = lax.dynamic_slice_in_dim(array, core * size, size, axis)
    theirs = lax.dynamic_slice_in_dim(array, (1 - core) * size, size, axis)
    return (mine, theirs)


def ordered(mine, theirs, core):
    return jnp.where(
        core == 0,
        jnp.concatenate([mine, theirs], axis=-1),
        jnp.concatenate([theirs, mine], axis=-1),
    )


def flipped(array, peers, bit):
    return lax.ppermute(array, "tensor", [(i, i ^ (1 << bit)) for i in range(peers)])


def halving(peers, rows):
    bits = peers.bit_length() - 1
    return bits if peers == 1 << bits and bits > 0 and rows % (16 * peers) == 0 else 0


def step_bits(bits, stream):
    return [step if stream == 0 else bits - 1 - step for step in range(bits)]


def relative_order(bits, stream):
    order = [0]
    for bit in reversed(step_bits(bits, stream)):
        order = order + [other ^ (1 << bit) for other in order]
    return order


def scatter_places(me, peers, bits):
    half = peers // 2
    places = []
    for stream in (0, 1):
        bit = step_bits(bits, stream)[0]
        own = (me >> bit) & 1
        for value in (1 - own, own):
            for place in range(half):
                low = place & ((1 << bit) - 1)
                high = (place >> bit) << (bit + 1)
                places.append(high | (value << bit) | low)
    return places


def sum_scatter(pieces, peers, bits):
    me = lax.axis_index("tensor")
    half = peers // 2
    width = pieces[0].shape[1]
    sends = [pieces[k * (half + 1) : k * (half + 1) + half] for k in (0, 1)]
    keeps = [pieces[k * (half + 1) + half] for k in (0, 1)]
    left = [[b for b in reversed(range(bits)) if b != step_bits(bits, k)[0]] for k in (0, 1)]
    for step in range(bits):
        arrived = lax.optimization_barrier(
            [[flipped(item, peers, step_bits(bits, k)[step]) for item in sends[k]] for k in (0, 1)]
        )
        for k in (0, 1):
            got = arrived[k]
            total = jnp.stack(
                [
                    keep.astype(jnp.float32) + item.astype(jnp.float32)
                    for keep, item in zip(jnp.split(keeps[k], len(got), axis=0), got)
                ]
            )
            if step == bits - 1:
                keeps[k] = total[0]
                continue
            total = total.astype(jnp.bfloat16).reshape((2,) * len(left[k]) + (-1, width))
            bit = step_bits(bits, k)[step + 1]
            axis = left[k].index(bit)
            own = (me >> bit) & 1
            keep = lax.dynamic_index_in_dim(total, own, axis, keepdims=False)
            send = lax.dynamic_index_in_dim(total, 1 - own, axis, keepdims=False)
            keeps[k] = keep.reshape(-1, width)
            sends[k] = jnp.split(send.reshape(-1, width), len(got) // 2, axis=0)
            left[k].pop(axis)
    return keeps


def rows_pieces(blocks, peers, bits):
    current = [[item] for item in blocks]
    for step in reversed(range(bits)):
        arrived = lax.optimization_barrier(
            [[flipped(item, peers, step_bits(bits, k)[step]) for item in current[k]] for k in (0, 1)]
        )
        current = [current[k] + arrived[k] for k in (0, 1)]
    return current[0] + current[1]


def attend(mixed, length, tables):
    slots = mixed.shape[0]
    cosine, sine = tables
    query = rotate(mixed[:, 0], cosine, sine).astype(jnp.bfloat16)
    keys = rotate(mixed[:, 1], cosine, sine).astype(jnp.bfloat16)
    values = mixed[:, 2].astype(jnp.bfloat16)
    scores = jnp.einsum(
        "qhd,khd->hqk", query, keys, preferred_element_type=jnp.float32
    ) * HEAD_DIM ** (-0.5)
    scores = jnp.where(allowed_mask(slots, length)[None], scores, -jnp.inf)
    peak = jnp.max(scores, axis=-1, keepdims=True)
    expo = jnp.exp(scores - peak)
    total = jnp.sum(expo, axis=-1, keepdims=True)
    probs_low = (expo / total).astype(jnp.bfloat16)
    logsum = peak + jnp.log(total)
    heads_out = jnp.einsum("hqk,khd->qhd", probs_low, values, preferred_element_type=jnp.float32)
    return (heads_out.reshape(slots, -1).astype(jnp.bfloat16), (query, keys, values, logsum))


def attend_back(out_grad, saved, length, tables):
    query, keys, values, logsum = saved
    slots, heads = query.shape[:2]
    cosine, sine = tables
    out_grad = out_grad.reshape(slots, heads, HEAD_DIM)
    scores = jnp.einsum(
        "qhd,khd->hqk", query, keys, preferred_element_type=jnp.float32
    ) * HEAD_DIM ** (-0.5)
    probs = jnp.where(allowed_mask(slots, length)[None], jnp.exp(scores - logsum), 0.0)
    probs_low = probs.astype(jnp.bfloat16)
    prob_grad = jnp.einsum("qhd,khd->hqk", out_grad, values, preferred_element_type=jnp.float32)
    value_grad = jnp.einsum("hqk,qhd->khd", probs_low, out_grad, preferred_element_type=jnp.float32)
    score_grad = (probs * (prob_grad - jnp.sum(probs * prob_grad, axis=-1, keepdims=True))).astype(
        jnp.bfloat16
    )
    query_grad = jnp.einsum(
        "hqk,khd->qhd", score_grad, keys, preferred_element_type=jnp.float32
    ) * HEAD_DIM ** (-0.5)
    key_grad = jnp.einsum(
        "hqk,qhd->khd", score_grad, query, preferred_element_type=jnp.float32
    ) * HEAD_DIM ** (-0.5)
    query_grad = rotate_back(query_grad, cosine, sine)
    key_grad = rotate_back(key_grad, cosine, sine)
    return jnp.stack([query_grad, key_grad, value_grad], axis=1).astype(jnp.bfloat16)


def dot(left, right):
    return jnp.dot(left, right, preferred_element_type=jnp.float32)


def dot_nt(left, right):
    return lax.dot_general(
        left, right, (((1,), (1,)), ((), ())), preferred_element_type=jnp.float32
    )


def dot_tn(left, right):
    return lax.dot_general(
        left, right, (((0,), (0,)), ((), ())), preferred_element_type=jnp.float32
    )


CHEAP = pl.CostEstimate(flops=1, transcendentals=0, bytes_accessed=1)
SCALE = HEAD_DIM ** (-0.5)


def call(body, grid, in_specs, out_specs, out_shape, info, args, scratch=(), cost=CHEAP):
    return pl.pallas_call(
        body,
        grid_spec=pltpu.PrefetchScalarGridSpec(
            num_scalar_prefetch=1,
            grid=grid,
            in_specs=in_specs,
            out_specs=out_specs,
            scratch_shapes=list(scratch),
        ),
        out_shape=out_shape,
        cost_estimate=cost,
        compiler_params=pltpu.CompilerParams(vmem_limit_bytes=56 << 20),
    )(info, *args)


def low_shape(*shape):
    return jax.ShapeDtypeStruct(shape, jnp.bfloat16)


def full_shape(*shape):
    return jax.ShapeDtypeStruct(shape, jnp.float32)


def fixed(shape):
    return pl.BlockSpec(
        shape, lambda *index: (0,) * len(shape), pipeline_mode=pl.Buffered(buffer_count=1)
    )


def held(width, columns, at):
    return pl.BlockSpec(
        (width, columns), lambda i, info: (0, at), pipeline_mode=pl.Buffered(buffer_count=1)
    )


def row_stats(rows):
    mean = jnp.mean(rows, axis=1, keepdims=True)
    center = rows - mean
    scale = lax.rsqrt(jnp.mean(center * center, axis=1, keepdims=True) + 1e-05)
    return (mean, scale)


def two_norms(rows, vec_ref, outs):
    rows = rows.astype(jnp.float32)
    mean, scale = row_stats(rows)
    normed = (rows - mean) * scale
    first = normed * vec_ref[0:1] + vec_ref[1:2]
    second = normed * vec_ref[2:3] + vec_ref[3:4]
    outs[0][...] = first.astype(jnp.bfloat16)
    outs[1][...] = second.astype(jnp.bfloat16)
    outs[2][...] = mean
    outs[3][...] = scale
    if len(outs) > 4:
        outs[4][...] = first.T.astype(jnp.bfloat16)
        outs[5][...] = second.T.astype(jnp.bfloat16)


def norms_body(info, z_ref, vec_ref, *outs):
    two_norms(z_ref[...], vec_ref, outs)


def norm_specs(tall, slots, width, row, turn):
    specs = [pl.BlockSpec((tall, width), lambda i, info: (row(i, info), 0))] * 2
    specs += [pl.BlockSpec((tall, 1), lambda i, info: (row(i, info), 0))] * 2
    shapes = [low_shape(slots, width)] * 2 + [full_shape(slots, 1)] * 2
    if turn:
        specs += [pl.BlockSpec((width, tall), lambda i, info: (0, row(i, info)))] * 2
        shapes += [low_shape(width, slots)] * 2
    return (specs, shapes)


def with_turned(out, turn):
    out = list(out)
    return out if turn else out + [out[0].T, out[1].T]


def norms_call(rows, vectors, info):
    slots, width = rows.shape
    tall = min(slots, 256)
    turn = tall % 128 == 0
    specs, shapes = norm_specs(tall, slots, width, lambda i, info: i, turn)
    out = call(
        norms_body,
        (slots // tall,),
        [pl.BlockSpec((tall, width), lambda i, info: (i, 0)), fixed(vectors.shape)],
        specs,
        shapes,
        info,
        (rows, vectors),
    )
    return with_turned(out, turn)


def target_body(info, x_ref, out_ref, *turned_ref):
    tall = x_ref.shape[0]
    place = pl.program_id(0) * tall + lax.broadcasted_iota(jnp.int32, x_ref.shape, 0)
    value = jnp.where(place < info[0], x_ref[...].astype(jnp.float32), 0.0)
    out_ref[...] = value.astype(jnp.bfloat16)
    if turned_ref:
        turned_ref[0][...] = value.T.astype(jnp.bfloat16)


def target_call(cotangent, slots, info):
    width = cotangent.shape[1]
    tall = min(slots, 256)
    steps = slots // tall
    turn = tall % 128 == 0
    out = call(
        target_body,
        (steps,),
        [pl.BlockSpec((tall, width), lambda i, info: (info[1] * steps + i, 0))],
        [pl.BlockSpec((tall, width), lambda i, info: (i, 0))]
        + [pl.BlockSpec((width, tall), lambda i, info: (0, i))] * turn,
        [low_shape(slots, width)] + [low_shape(width, slots)] * turn,
        info,
        (cotangent,),
    )
    return (out[0], out[1]) if turn else (out[0], out[0].T)


def assemble_body(count, normed, info, *refs):
    step = pl.program_id(0)
    rest = refs[count:]
    for which in range(count):

        @pl.when(step == which)
        def _():
            block = refs[which][...]
            if normed:
                rest[1][...] = block
                two_norms(block, rest[0], rest[2:])
            else:
                rest[0][...] = block
                if len(rest) > 1:
                    rest[1][...] = block.astype(jnp.float32).T.astype(jnp.bfloat16)


def assemble(pieces, peers, bits, vectors=None):
    count = len(pieces)
    tall, width = pieces[0].shape
    slots = count * tall
    turn = tall % 128 == 0
    me = lax.axis_index("tensor")
    order = [2 * (me ^ r) + k for k in (0, 1) for r in relative_order(bits, k)]
    info = jnp.stack([jnp.asarray(item, jnp.int32) for item in order])

    def row(s, info):
        return info[s]

    in_specs, args = [fixed(item.shape) for item in pieces], list(pieces)
    specs = [pl.BlockSpec((tall, width), lambda s, info: (info[s], 0))]
    shapes = [low_shape(slots, width)]
    if vectors is not None:
        in_specs.append(fixed(vectors.shape))
        args.append(vectors)
        more, more_shapes = norm_specs(tall, slots, width, row, turn)
        specs, shapes = specs + more, shapes + more_shapes
    elif turn:
        specs.append(pl.BlockSpec((width, tall), lambda s, info: (0, info[s])))
        shapes.append(low_shape(width, slots))
    out = call(
        functools.partial(assemble_body, count, vectors is not None),
        (count,),
        in_specs,
        specs,
        shapes,
        info,
        args,
    )
    if vectors is not None:
        return (out[0], with_turned(out[1:], turn))
    return (out[0], out[1] if turn else out[0].T)


def turned(block, tables, sign):
    cosine, low, high = tables
    front = block[:, :128]
    front = front * cosine + sign * (
        pltpu.roll(front, 128 - ROT // 2, 1) * low + pltpu.roll(front, ROT // 2, 1) * high
    )
    return jnp.concatenate([front, block[:, 128:]], axis=1)


def turn_tables(slots):
    cosine, sine = (item[:, 0] for item in angle_tables(slots))
    rest = 128 - ROT
    zero = jnp.zeros_like(sine)
    pad = jnp.zeros((slots, rest), jnp.float32)
    return (
        jnp.concatenate([cosine, cosine, pad + 1.0], axis=1),
        jnp.concatenate([-sine, zero, pad], axis=1),
        jnp.concatenate([zero, sine, pad], axis=1),
    )


def allowed_block(start, rows, span, length):
    query = start + lax.broadcasted_iota(jnp.int32, (rows, span), 0)
    key = lax.broadcasted_iota(jnp.int32, (rows, span), 1)
    return (key <= query) & (key < length)


def heads_body(
    steps, info, x_ref, w_ref, cos_ref, low_ref, high_ref, out_ref, qkv_ref, lse_ref, k_ref, v_ref
):
    step = pl.program_id(0)
    rows = x_ref.shape[0]
    tables = (cos_ref[...], low_ref[...], high_ref[...])
    mixed = dot(x_ref[...], w_ref[...])
    query = turned(mixed[:, :HEAD_DIM], tables, 1.0).astype(jnp.bfloat16)
    keys = turned(mixed[:, HEAD_DIM : 2 * HEAD_DIM], tables, 1.0).astype(jnp.bfloat16)
    values = mixed[:, 2 * HEAD_DIM :].astype(jnp.bfloat16)
    qkv_ref[:, :HEAD_DIM] = query
    qkv_ref[:, HEAD_DIM : 2 * HEAD_DIM] = keys
    qkv_ref[:, 2 * HEAD_DIM :] = values
    place = pl.multiple_of(step * rows, rows)
    k_ref[pl.ds(place, rows), :] = keys
    v_ref[pl.ds(place, rows), :] = values
    for now in range(steps):

        @pl.when(step == now)
        def _():
            span = (now + 1) * rows
            scores = dot_nt(query, k_ref[:span]) * SCALE
            scores = jnp.where(allowed_block(now * rows, rows, span, info[0]), scores, -jnp.inf)
            peak = jnp.max(scores, axis=1, keepdims=True)
            expo = jnp.exp(scores - peak)
            total = jnp.sum(expo, axis=1, keepdims=True)
            probs = (expo / total).astype(jnp.bfloat16)
            out_ref[...] = dot(probs, v_ref[:span]).astype(jnp.bfloat16)
            lse_ref[...] = peak + jnp.log(total)


def heads_call(first_in, inward, tables, info):
    slots, width = first_in.shape
    rows = min(slots, 256)
    steps = slots // rows
    columns = 3 * HEAD_DIM

    def tall(size):
        return pl.BlockSpec((rows, size), lambda i, info: (i, 0))

    out, qkv, lse = call(
        functools.partial(heads_body, steps),
        (steps,),
        [
            tall(width),
            pl.BlockSpec(
                (width, columns), lambda i, info: (0, 0), pipeline_mode=pl.Buffered(buffer_count=1)
            ),
        ]
        + [tall(128)] * 3,
        [tall(HEAD_DIM), tall(columns), tall(1)],
        [low_shape(slots, HEAD_DIM), low_shape(slots, columns), full_shape(slots, 1)],
        info,
        (first_in, inward, *tables),
        [pltpu.VMEM((slots, HEAD_DIM), jnp.bfloat16)] * 2,
    )
    return (out, (qkv, lse))


def heads_back_body(
    steps, info, qkv_ref, lse_ref, grad_ref, cos_ref, low_ref, high_ref, out_ref, dk_ref, dv_ref
):
    step = pl.program_id(0)
    slots = qkv_ref.shape[0]
    rows = slots // steps

    def tables(start, size):
        return tuple(ref[start : start + size] for ref in (cos_ref, low_ref, high_ref))

    @pl.when(step == 0)
    def _():
        dk_ref[...] = jnp.zeros_like(dk_ref)
        dv_ref[...] = jnp.zeros_like(dv_ref)

    for now in range(steps):

        @pl.when(step == now)
        def _():
            span, start = (now + 1) * rows, now * rows
            query = qkv_ref[start:span, :HEAD_DIM]
            keys = qkv_ref[:span, HEAD_DIM : 2 * HEAD_DIM]
            values = qkv_ref[:span, 2 * HEAD_DIM :]
            grad = grad_ref[...]
            scores = dot_nt(query, keys) * SCALE
            allowed = allowed_block(start, rows, span, info[0])
            probs = jnp.where(allowed, jnp.exp(scores - lse_ref[...]), 0.0)
            prob_grad = dot_nt(grad, values)
            spread = jnp.sum(probs * prob_grad, axis=1, keepdims=True)
            score_grad = (probs * (prob_grad - spread)).astype(jnp.bfloat16)
            query_grad = dot(score_grad, keys) * SCALE
            out_ref[start:span, :HEAD_DIM] = turned(
                query_grad, tables(start, rows), -1.0
            ).astype(jnp.bfloat16)
            dv_ref[:span] += dot_tn(probs.astype(jnp.bfloat16), grad)
            dk_ref[:span] += dot_tn(score_grad, query)

    @pl.when(step == steps - 1)
    def _():
        out_ref[:, HEAD_DIM : 2 * HEAD_DIM] = turned(
            dk_ref[...] * SCALE, tables(0, slots), -1.0
        ).astype(jnp.bfloat16)
        out_ref[:, 2 * HEAD_DIM :] = dv_ref[...].astype(jnp.bfloat16)


def heads_back_call(saved, out_grad, tables, info):
    qkv, lse = saved
    slots, columns = qkv.shape
    rows = min(slots, 256)
    steps = slots // rows
    return call(
        functools.partial(heads_back_body, steps),
        (steps,),
        [
            fixed(qkv.shape),
            pl.BlockSpec((rows, 1), lambda i, info: (i, 0)),
            pl.BlockSpec((rows, HEAD_DIM), lambda i, info: (i, 0)),
        ]
        + [fixed((slots, 128))] * 3,
        pl.BlockSpec((slots, columns), lambda i, info: (0, 0)),
        low_shape(slots, columns),
        info,
        (qkv, lse, out_grad, *tables),
        [pltpu.VMEM((slots, HEAD_DIM), jnp.float32)] * 2,
    )


def units_body(info, x_ref, w_ref, offset_ref, act_ref, slope_ref):
    columns = w_ref.shape[1]
    size = min(columns, 512)
    for start in range(0, columns, size):
        here = slice(start, start + size)
        hidden = dot(x_ref[...], w_ref[:, here]) + offset_ref[:, here]
        cdf = 0.5 * (1.0 + lax.erf(hidden * 0.7071067811865476))
        act_ref[:, here] = (hidden * cdf).astype(jnp.bfloat16)
        bell = jnp.exp(-0.5 * hidden * hidden) * 0.3989422804014327
        slope_ref[:, here] = (cdf + hidden * bell).astype(jnp.bfloat16)


def units_call(second_in, expand, start, offsets, unit, info):
    slots, width = second_in.shape
    columns = offsets.shape[0]
    tall = min(slots, 256)
    spec = pl.BlockSpec((tall, columns), lambda i, info: (i, 0))
    return call(
        units_body,
        (slots // tall,),
        [
            pl.BlockSpec((tall, width), lambda i, info: (i, 0)),
            held(width, columns, start * unit // columns),
            fixed((1, columns)),
        ],
        [spec, spec],
        [low_shape(slots, columns)] * 2,
        info,
        (second_in, expand, offsets[None]),
    )


def halving_blocks(half, tall):
    return ([tall] * half + [half * tall]) * 2


def place_rows(info, value_ref, outs, half, tall):
    for which in range(4):
        stream, kept = which // 2, which % 2
        for place in range(half):
            start = (2 * info[which * half + place] + stream) * tall
            rows = value_ref[pl.ds(pl.multiple_of(start, tall), tall)]
            if kept:
                outs[stream * (half + 1) + half][place * tall : (place + 1) * tall] = rows
            else:
                outs[stream * (half + 1) + place][...] = rows


def partial_body(half, tall, info, *refs):
    value = None
    for left, right in zip(refs[:4], refs[4:8]):
        term = dot_nt(left[...], right[...])
        value = term if value is None else value + term
    outs, value_ref = refs[8:-1], refs[-1]
    value_ref[...] = value.astype(jnp.bfloat16)
    if half:
        place_rows(info, value_ref, outs, half, tall)
    else:
        outs[0][...] = value_ref[...]


def partial_call(heads, acts, outward, contract, outward_at, contract_at, places):
    slots, unit = heads[0].shape
    wide = acts[0].shape[1]
    width = outward[0].shape[0]
    block = min(width, 512)
    half = len(places) // 4
    tall = slots // (4 * half) if half else 0
    heights = halving_blocks(half, tall) if half else [slots]
    info = jnp.stack([jnp.asarray(item, jnp.int32) for item in (places or [0])])
    return call(
        functools.partial(partial_body, half, tall),
        (width // block,),
        [fixed(item.shape) for item in (*heads, *acts)]
        + [pl.BlockSpec((block, unit), lambda j, info: (j, outward_at))] * 2
        + [pl.BlockSpec((block, wide), lambda j, info: (j, contract_at * unit // wide))] * 2,
        [pl.BlockSpec((height, block), lambda j, info: (0, j)) for height in heights],
        [low_shape(height, width) for height in heights],
        info,
        (*heads, *acts, *outward, *contract),
        [pltpu.VMEM((slots, block), jnp.bfloat16)],
    )


PIECES = 4


def grads_body(count, split, info, *refs):
    lefts, rights, rest = refs[:count], refs[count : 2 * count], refs[2 * count :]
    got, outs = ((), rest) if split else (rest[:PIECES], rest[PIECES:])
    size = (outs[0].shape[1]) if split else got[0].shape[1]
    start = 0
    for left, right in zip(lefts, rights):
        value = dot(left[...], right[...])
        for piece in range(PIECES):
            low = max(start, piece * size)
            high = min(start + right.shape[1], (piece + 1) * size)
            if low >= high:
                continue
            term = value[:, low - start : high - start]
            inner = slice(low - piece * size, high - piece * size)
            if split:
                outs[piece][:, inner] = term.astype(jnp.bfloat16)
            else:
                term = term + got[piece][:, inner].astype(jnp.float32)
                outs[0][:, low:high] = term.astype(jnp.bfloat16)
        start = start + right.shape[1]


def grads_call(lefts, rights, info, got=None, cost=CHEAP):
    width, slots = lefts[0].shape
    columns = sum(item.shape[1] for item in rights)
    block = min(width, 256)
    split = got is None
    spec = pl.BlockSpec((block, columns), lambda j, info: (j, 0))
    piece_specs = [pl.BlockSpec((block, columns // PIECES), lambda j, info: (j, 0))] * PIECES
    out = call(
        functools.partial(grads_body, len(lefts), split),
        (width // block,),
        [pl.BlockSpec((block, slots), lambda j, info: (j, 0))] * len(lefts)
        + [fixed(item.shape) for item in rights]
        + ([] if split else piece_specs),
        piece_specs if split else spec,
        [low_shape(width, columns // PIECES)] * PIECES if split else low_shape(width, columns),
        info,
        (*lefts, *rights, *(got or ())),
        cost=cost,
    )
    return out


def lifted_body(info, g_ref, outward_ref, contract_ref, slope_ref, out_ref, hidden_ref, sum_ref):
    columns = contract_ref.shape[1]
    size = min(columns, 512)

    @pl.when(pl.program_id(0) == 0)
    def _():
        sum_ref[...] = jnp.zeros_like(sum_ref)

    for start in range(0, columns, size):
        here = slice(start, start + size)
        value = dot(g_ref[...], contract_ref[:, here]) * slope_ref[:, here].astype(jnp.float32)
        value = value.astype(jnp.bfloat16)
        hidden_ref[:, here] = value
        sum_ref[:, here] += jnp.sum(value.astype(jnp.float32), axis=0, keepdims=True)
    out_ref[...] = dot(g_ref[...], outward_ref[...]).astype(jnp.bfloat16)


def lifted_call(grad, outward, contract, outward_at, contract_at, slope, unit, info):
    slots, width = grad.shape
    columns = slope.shape[1]
    tall = min(slots, 256)

    def rows(size):
        return pl.BlockSpec((tall, size), lambda i, info: (i, 0))

    return call(
        lifted_body,
        (slots // tall,),
        [
            rows(width),
            held(width, unit, outward_at),
            held(width, columns, contract_at * unit // columns),
            rows(columns),
        ],
        [rows(unit), rows(columns), pl.BlockSpec((1, columns), lambda i, info: (0, 0))],
        [low_shape(slots, unit), low_shape(slots, columns), full_shape(1, columns)],
        info,
        (grad, outward, contract, slope),
    )


def back_body(half, tall, info, *refs):
    z_ref, mean_ref, scale_ref, vec_ref = refs[:4]
    mixed, hidden, inward, expand = refs[4:6], refs[6:8], refs[8:10], refs[10:12]
    outs, sums_ref, hat_ref, total_ref, along_ref = refs[12:-4], *refs[-4:]
    part, block = pl.program_id(0), pl.program_id(1)
    size = inward[0].shape[0]
    width = z_ref.shape[1]
    columns = pl.ds(pl.multiple_of(block * size, size), size)
    mean, scale = mean_ref[...], scale_ref[...]
    first = dot_nt(mixed[0][...], inward[0][...]) + dot_nt(mixed[1][...], inward[1][...])
    second = dot_nt(hidden[0][...], expand[0][...]) + dot_nt(hidden[1][...], expand[1][...])
    normed = (z_ref[:, columns].astype(jnp.float32) - mean) * scale
    sums = [
        jnp.sum(value, axis=0, keepdims=True)
        for value in (first * normed, first, second * normed, second)
    ]

    @pl.when(part == 0)
    def _():
        for row in range(4):
            sums_ref[row : row + 1, columns] = sums[row]

    @pl.when(part > 0)
    def _():
        for row in range(4):
            sums_ref[row : row + 1, columns] += sums[row]

    hat = first * vec_ref[0:1] + second * vec_ref[2:3]
    hat_ref[:, columns] = hat
    total = jnp.sum(hat, axis=1, keepdims=True)
    along = jnp.sum(hat * normed, axis=1, keepdims=True)

    @pl.when(block == 0)
    def _():
        total_ref[...] = total
        along_ref[...] = along

    @pl.when(block > 0)
    def _():
        total_ref[...] += total
        along_ref[...] += along

    @pl.when(block == pl.num_programs(1) - 1)
    def _():
        rows = hat_ref.shape[0]
        step = tall if half else min(rows, 256)
        for start in range(0, rows, step):
            here = slice(start, start + step)
            normed_here = (z_ref[here].astype(jnp.float32) - mean_ref[here]) * scale_ref[here]
            result = scale_ref[here] * (
                hat_ref[here]
                - total_ref[here] / width
                - normed_here * (along_ref[here] / width)
            )
            result = result.astype(jnp.bfloat16)
            if not half:
                outs[0][pl.ds(part * rows + start, step)] = result
                continue
            stream = start // tall % 2
            peer = part * (rows // (2 * tall)) + start // (2 * tall)
            at = 2 * (2 * peer + stream)
            own_outs = outs[stream * (half + 1) : (stream + 1) * (half + 1)]

            @pl.when(info[at] == 0)
            def _():
                own_outs[half][pl.ds(pl.multiple_of(info[at + 1] * tall, tall), tall)] = result

            for place in range(half):

                @pl.when((info[at] == 1) & (info[at + 1] == place))
                def _():
                    own_outs[place][...] = result


def back_call(rows, stats, vectors, mixed_grads, hidden_grads, inward, expand, expand_at, me, peers, bits):
    slots, width = rows.shape
    parts = 2 if bits else 1
    rows_each = slots // parts
    block = min(width, 512)
    half = peers // 2 if bits else 0
    tall = slots // (2 * peers) if bits else 0
    heads_columns, wide = mixed_grads[0].shape[1], hidden_grads[0].shape[1]
    table = []
    for peer in range(peers if bits else 0):
        for stream in (0, 1):
            bit = step_bits(bits, stream)[0]
            own = (me >> bit) & 1
            place = (peer & ((1 << bit) - 1)) | ((peer >> (bit + 1)) << bit)
            table.append(jnp.asarray(((peer >> bit) & 1) != own, jnp.int32))
            table.append(jnp.asarray(place, jnp.int32))
    info = jnp.stack(table or [jnp.asarray(0, jnp.int32)])
    heights = halving_blocks(half, tall) if half else [slots]

    def spec(columns):
        return pl.BlockSpec((rows_each, columns), lambda i, j, info: (i, 0))

    def weights(columns, at):
        return pl.BlockSpec((block, columns), lambda i, j, info: (j, at))

    def whole(*shape):
        return pl.BlockSpec(shape, lambda i, j, info: (0, 0))

    out = call(
        functools.partial(back_body, half, tall),
        (parts, width // block),
        [spec(width), spec(1), spec(1)]
        + [pl.BlockSpec((vectors.shape[0], block), lambda i, j, info: (0, j))]
        + [spec(item.shape[1]) for item in (*mixed_grads, *hidden_grads)]
        + [weights(heads_columns, 0)] * 2
        + [weights(wide, expand_at * heads_columns // (3 * wide))] * 2,
        [whole(height, width) for height in heights] + [whole(4, width)],
        [low_shape(height, width) for height in heights] + [full_shape(4, width)],
        info,
        (rows, *stats, vectors, *mixed_grads, *hidden_grads, *inward, *expand),
        [pltpu.VMEM((rows_each, width), jnp.float32)]
        + [pltpu.VMEM((rows_each, 1), jnp.float32)] * 2,
    )
    return out[:-1], out[-1]


def share_of(total):
    return lax.psum_scatter(total, "dp", scatter_dimension=0, tiled=True)


def adam_kernel(rate, decay, arrange, info, *refs):
    grads, (master, first, second), outs = refs[:4], refs[4:7], refs[7:]

    def run(half, region, turn):
        grad = jnp.where(info[0] == 0, grads[half][...], grads[2 + half][...]).astype(jnp.float32)
        grad = grad.T if turn else grad
        new = adam_update(master[region], grad, first[region], second[region], rate, decay)
        for out, value in zip(outs, new):
            out[region] = value

    arrange(run)


def adam_columns(index, grads, arrays, depth, starts, core):
    parts, _, columns = arrays[0].shape
    half = columns // 2
    tall = depth // 4

    def arrange(run):
        for which in (0, 1):
            run(which, (0, slice(None), pl.ds(which * half, half)), False)

    def grad_spec(start):
        return pl.BlockSpec((tall, half), lambda i, j, info: (j, start + i))

    block_spec = pl.BlockSpec((1, tall, columns), lambda i, j, info: (i, j, 0))
    return call(
        functools.partial(adam_kernel, RATES[index], DECAYS[index], arrange),
        (parts, depth // tall),
        [grad_spec(starts[which // 2]) for which in range(4)] + [block_spec] * 3,
        [block_spec] * 3,
        [jax.ShapeDtypeStruct(arrays[0].shape, jnp.float32)] * 3,
        core,
        (*grads, *arrays),
    )


def adam_rows(index, grads, arrays, starts, block, core):
    units, depth = arrays[0].shape
    each = units // 2 // block

    def arrange(run):
        for half in (0, 1):

            @pl.when(pl.program_id(0) == half)
            def _():
                run(half, Ellipsis, True)

    def grad_spec(half, start):
        def place(h, j, info):
            return (0, start + jnp.where(h == half, j, (each - 1) * (1 - half)))

        return pl.BlockSpec((depth, block), place)

    block_spec = pl.BlockSpec((block, depth), lambda h, j, info: (h * each + j, 0))
    return call(
        functools.partial(adam_kernel, RATES[index], DECAYS[index], arrange),
        (2, each),
        [grad_spec(which % 2, starts[which // 2]) for which in range(4)] + [block_spec] * 3,
        [block_spec] * 3,
        [jax.ShapeDtypeStruct(arrays[0].shape, jnp.float32)] * 3,
        core,
        (*grads, *arrays),
    )


def adam_update(master, grad, first, second, rate, decay):
    new_first = 0.9 * first + 0.1 * grad
    new_second = 0.95 * second + 0.05 * grad * grad
    corrected = new_first / (1.0 - 0.9**STEP)
    spread = jnp.sqrt(new_second / (1.0 - 0.95**STEP))
    return (master - rate * (corrected / (spread + 1e-08) + decay * master), new_first, new_second)


def local(
    tokens,
    cotangent,
    lengths,
    inward,
    outward,
    expand,
    contract,
    vectors,
    offsets,
    inward_first,
    inward_second,
    outward_first,
    outward_second,
    expand_first,
    expand_second,
    contract_first,
    contract_second,
    vectors_first,
    vectors_second,
    offsets_first,
    offsets_second,
):
    core = lax.axis_index("pipe")
    peers = lax.axis_size("tensor")
    groups = lax.axis_size("dp")
    place = lax.axis_index("tensor")
    depth = inward.shape[1]
    heads_local = inward.shape[3] // HEAD_DIM
    lone = heads_local == 2
    head_share = inward.shape[3] // 2
    unit_share = expand.shape[2] // 2
    batches = lengths.shape[0]
    width = tokens.shape[1]
    slots = tokens.shape[0] // batches
    row_share = slots // peers

    bits = halving(peers, slots)

    def packed(shard):
        mine, theirs = (item.astype(jnp.bfloat16).reshape(depth, -1) for item in halves(shard, core))
        got = swap(theirs)
        return (jnp.where(core == 0, mine, got), jnp.where(core == 0, got, mine))

    packs = [packed(item) for item in (inward[0], expand[0], outward[0].T, contract[0].T)]
    count = unit_share // head_share

    small = jnp.concatenate([vectors.reshape(-1), offsets.reshape(-1)]).astype(jnp.bfloat16)
    small = lax.all_gather(small, ("pipe", "dp"), axis=0, tiled=False).reshape(2, groups, -1)
    small = small.astype(jnp.float32)
    vector_values = [
        small[layer, :, : 5 * depth].reshape(groups, 5, depth).transpose(1, 0, 2).reshape(5, width)
        for layer in (0, 1)
    ]
    offset_pairs = [halves(small[layer, :, 5 * depth :].reshape(-1), core) for layer in (0, 1)]

    tables = angle_tables(slots)
    turns = turn_tables(slots)
    length = lax.dynamic_index_in_dim(lengths, core, 0, keepdims=False)
    info = length[None]
    own = lax.dynamic_slice_in_dim(tokens, core * slots, slots, 0)
    target, target_turned = target_call(cotangent, slots, jnp.stack([length, core]))
    places = scatter_places(place, peers, bits) if bits else []

    def whole_of(shard):
        return lax.all_gather(shard, "dp", axis=0, tiled=True)

    def pair_of(whole, *earlier):
        whole = after(whole, *earlier)
        return (whole, swap(whole))

    def block_of(array):
        block = lax.dynamic_slice_in_dim(array, place * row_share, row_share, 0)
        return block.astype(jnp.float32)

    def summed(pieces):
        if bits:
            return jnp.concatenate(sum_scatter(pieces, peers, bits), axis=0)
        return lax.psum_scatter(pieces[0], "tensor", scatter_dimension=0, tiled=True).astype(
            jnp.float32
        )

    def spread(block):
        tall = row_share // 2
        return rows_pieces((block[:tall], block[tall:]), peers, bits)

    def heads_of(first_in, inward_pair):
        if lone:
            done = [heads_call(first_in, item, turns, info) for item in inward_pair]
            return ([item[0] for item in done], [item[1] for item in done])
        mixed = [dot(first_in, w[:, : 3 * head_share]).reshape(slots, 3, -1) for w in inward_pair]
        mixed = ordered(mixed[0], mixed[1], core).reshape(slots, 3, -1, HEAD_DIM)
        out, saved = attend(mixed, length, tables)
        return (list(halves(out, core)), saved)

    def heads_back(out_grads, saved):
        if lone:
            return [heads_back_call(kept, grad, turns, info) for grad, kept in zip(out_grads, saved)]
        grad = ordered(out_grads[0], out_grads[1], core)
        mixed_grad = attend_back(grad, saved, length, tables).reshape(slots, 3, -1)
        return [item.reshape(slots, -1) for item in halves(mixed_grad, core)]

    def units_of(second_in, expand_pair, start, layer):
        done = [
            units_call(
                second_in, expand_pair[which], start, offset_pairs[layer][which], head_share, info
            )
            for which in (0, 1)
        ]
        return ([item[0] for item in done], [item[1] for item in done])

    def layer_output(layer, outward_pair, contract_pair, heads, acts):
        pieces = partial_call(
            heads, acts, outward_pair, contract_pair, outward_at[layer], contract_at[layer], places
        )
        block = summed(pieces) + block_of(inputs[layer]) + vector_values[layer][4]
        return block.astype(jnp.bfloat16)

    outward_at, contract_at, expand_at = (2 * count, 3), (0, 0), (count, 4)
    shards = [packs[0][0], jnp.concatenate([packs[3][0], packs[1][0], packs[2][0]], axis=1)]
    shards.append(jnp.concatenate([after(packs[0][1], shards[1]), packs[2][1], packs[1][1]], axis=1))
    shards.append(after(packs[3][1], shards[2]))
    shards[1] = after(shards[1], shards[0])
    wholes = [whole_of(item) for item in shards]
    inputs = [own]
    normed = norms_call(own, vector_values[0], info)
    first_in, second_in = normed[:2]
    inward_pairs = [pair_of(wholes[0], first_in, second_in, target_turned)]
    heads, saved = heads_of(first_in, inward_pairs[0])
    rest_pair = pair_of(wholes[1], *heads)
    acts, slopes = units_of(second_in, rest_pair, expand_at[0], 0)
    kept = [(normed, heads, saved, acts, slopes)]
    outward_pairs, contract_pairs, expand_pairs = [rest_pair], [rest_pair], [rest_pair]
    results = [layer_output(0, rest_pair, rest_pair, heads, acts)]
    if bits:
        rows, normed = assemble(
            spread(results[0]), peers, bits, vector_values[1]
        )
        inputs.append(rows)
    else:
        inputs.append(lax.all_gather(results[0], "tensor", axis=0, tiled=True))
        normed = norms_call(inputs[1], vector_values[1], info)
    first_in, second_in = normed[:2]
    rest_pair = pair_of(wholes[2], first_in, second_in)
    for store in (inward_pairs, outward_pairs, expand_pairs):
        store.append(rest_pair)
    acts, slopes = units_of(second_in, rest_pair, expand_at[1], 1)

    grad_low, grad_turned = target, target_turned
    shares, row_grads, vector_grads, offset_grads = [None] * 2, [None] * 2, [None] * 2, [None] * 2
    for layer in (1, 0):
        if layer == 0:
            normed, heads, saved, acts, slopes = kept[0]
        theirs = grads_call([grad_turned], [acts[1]], info)
        if layer == 1:
            heads, saved = heads_of(after(first_in, *theirs), rest_pair)
            theirs = [after(after(item, acts[0], *heads), wholes[3]) for item in theirs]
        got = [swap(item) for item in theirs]
        contract_total = grads_call([grad_turned], [acts[0]], info, got)
        contract_share = share_of(contract_total)
        if layer == 1:
            contract_pairs.append(pair_of(wholes[3], *theirs))
        grad_here = after(grad_low, contract_total)
        lifted = [
            lifted_call(
                grad_here,
                outward_pairs[layer][which],
                contract_pairs[layer][which],
                outward_at[layer],
                contract_at[layer],
                slopes[which],
                head_share,
                info,
            )
            for which in (0, 1)
        ]
        hidden_grads = [item[1] for item in lifted]
        offset_grads[layer] = [item[2][0] for item in lifted]
        first_turned, second_turned = normed[4:]

        def total_of(lefts, theirs, mine, cost=CHEAP):
            got = [swap(item) for item in grads_call(lefts, theirs, info, cost=cost)]
            return grads_call(lefts, mine, info, got, cost)

        out_grads = [item[0] for item in lifted]
        if layer == 1:
            expand_total = total_of([second_turned], [hidden_grads[1]], [hidden_grads[0]])
            expand_share = share_of(expand_total)
            out_grads = [after(item, expand_total) for item in out_grads]
        mixed_grads = heads_back(out_grads, saved)
        lefts = [first_turned, grad_turned]
        rights = [[mixed_grads[which], heads[which]] for which in (1, 0)]
        if layer == 0:
            hidden_here = [after(item, *shares[1], *mixed_grads) for item in hidden_grads]
            other_total = total_of(
                [second_turned] + lefts,
                [hidden_here[1]] + rights[0],
                [hidden_here[0]] + rights[1],
            )
            ahead = [other_total]
        else:
            ahead = [contract_share, *mixed_grads]
        pieces, norm_part = back_call(
            after(inputs[layer], *ahead),
            normed[2:4],
            vector_values[layer],
            mixed_grads,
            hidden_grads,
            inward_pairs[layer],
            expand_pairs[layer],
            expand_at[layer],
            place,
            peers,
            bits,
        )
        if layer == 1:
            lefts[0] = after(lefts[0], *pieces)
            flops = 8 * slots * width * head_share
            cost = pl.CostEstimate(
                flops=4 * flops, transcendentals=0, bytes_accessed=4 * flops // slots
            )
            shares[1] = (share_of(total_of(lefts, *rights, cost)), expand_share, contract_share)
        else:
            pieces = [after(item, contract_share) for item in pieces]
            shares[0] = (share_of(other_total), contract_share)
        upstream = block_of(grad_low)
        vector_grads[layer] = jnp.concatenate(
            [norm_part, jnp.sum(upstream, axis=0)[None]], axis=0
        )
        row_grads[layer] = upstream + summed(pieces)
        if layer == 1:
            block = row_grads[layer].astype(jnp.bfloat16)
            if bits:
                grad_low, grad_turned = assemble(
                    [after(item, expand_share) for item in spread(block)], peers, bits
                )
            else:
                grad_low = lax.all_gather(block, "tensor", axis=0, tiled=True)
                grad_turned = grad_low.T
            last = (heads, acts)
        else:
            pairs = [
                [after(item, other_total) for item in pair]
                for pair in (outward_pairs[1], contract_pairs[1])
            ]
            results.append(layer_output(1, *pairs, *last))

    activations = jnp.where(core == 0, results[0], results[1])
    got = swap(jnp.where(core == 0, results[1], results[0]))
    activations = jnp.where(
        core == 0, jnp.stack([activations, got]), jnp.stack([got, activations])
    )[None]
    gradients = jnp.where(core == 0, row_grads[0], row_grads[1])
    got = swap(jnp.where(core == 0, row_grads[1], row_grads[0]))
    gradients = jnp.where(core == 0, jnp.stack([gradients, got]), jnp.stack([got, gradients]))[None]

    def to_owner(first, second, *earlier):
        first = after(first, *earlier)
        from_first = lax.ppermute(first, "pipe", [(1, 0)])
        from_second = lax.ppermute(second, "pipe", [(0, 1)])
        return (first, from_first, from_second, second)

    vector_sum = added(jnp.stack(vector_grads), "tensor")
    offset_sum = jnp.stack([ordered(item[0], item[1], core) for item in offset_grads])
    small_sum = jnp.concatenate([vector_sum.reshape(2, -1), offset_sum], axis=1)
    small_sum = added(added(small_sum, "pipe"), "dp")
    small_sum = lax.dynamic_index_in_dim(small_sum, core, 0, keepdims=False)
    where = lax.axis_index("dp")
    vector_grad = lax.dynamic_slice_in_dim(
        small_sum[: 5 * width].reshape(5, width), where * depth, depth, 1
    )
    offset_size = offsets.shape[1]
    offset_grad = lax.dynamic_slice_in_dim(
        small_sum, 5 * width + where * offset_size, offset_size, 0
    )

    def viewed(*arrays):
        return [item[0] for item in arrays]

    def parts_first(*arrays):
        return [item[0].transpose(1, 0, 2) for item in arrays]

    which = core[None]
    contract_out = adam_rows(
        3,
        to_owner(shares[0][1], shares[1][2]),
        viewed(contract, contract_first, contract_second),
        (0, 0),
        head_share,
        which,
    )
    last_share = after(shares[0][0], contract_out[0])
    expand_out = adam_columns(
        2,
        to_owner(last_share, shares[1][1]),
        [expand, expand_first, expand_second],
        depth,
        (0, 0),
        which,
    )
    heads_grads = to_owner(last_share, shares[1][0])
    outward_out = adam_rows(
        1,
        heads_grads,
        viewed(outward, outward_first, outward_second),
        (count + 3, 3),
        head_share,
        which,
    )
    inward_out = adam_columns(
        0,
        heads_grads,
        parts_first(inward, inward_first, inward_second),
        depth,
        (count, 0),
        which,
    )
    outputs = [activations, gradients]
    outputs.extend([item.transpose(1, 0, 2)[None] for item in inward_out])
    outputs.extend([item[None] for item in outward_out])
    outputs.extend(expand_out)
    outputs.extend([item[None] for item in contract_out])
    outputs.extend(
        adam_update(vectors, vector_grad[None], vectors_first, vectors_second, RATES[4], DECAYS[4])
    )
    outputs.extend(
        adam_update(offsets, offset_grad[None], offsets_first, offsets_second, RATES[5], DECAYS[5])
    )
    return tuple(outputs)


def solution(mesh):
    return jax.shard_map(
        local,
        mesh=mesh,
        in_specs=(
            P("dp", None),
            P("dp", None),
            P("dp"),
            P("pipe", "dp", None, "tensor"),
            P("pipe", "tensor", "dp"),
            P("pipe", "dp", "tensor"),
            P("pipe", "tensor", "dp"),
            P("pipe", None, "dp"),
            P("pipe", ("tensor", "dp")),
            P("pipe", "dp", None, "tensor"),
            P("pipe", "dp", None, "tensor"),
            P("pipe", "tensor", "dp"),
            P("pipe", "tensor", "dp"),
            P("pipe", "dp", "tensor"),
            P("pipe", "dp", "tensor"),
            P("pipe", "tensor", "dp"),
            P("pipe", "tensor", "dp"),
            P("pipe", None, "dp"),
            P("pipe", None, "dp"),
            P("pipe", ("tensor", "dp")),
            P("pipe", ("tensor", "dp")),
        ),
        out_specs=(
            P("pipe", "dp", "tensor", None),
            P("pipe", "dp", "tensor", None),
            P("pipe", "dp", None, "tensor"),
            P("pipe", "dp", None, "tensor"),
            P("pipe", "dp", None, "tensor"),
            P("pipe", "tensor", "dp"),
            P("pipe", "tensor", "dp"),
            P("pipe", "tensor", "dp"),
            P("pipe", "dp", "tensor"),
            P("pipe", "dp", "tensor"),
            P("pipe", "dp", "tensor"),
            P("pipe", "tensor", "dp"),
            P("pipe", "tensor", "dp"),
            P("pipe", "tensor", "dp"),
            P("pipe", None, "dp"),
            P("pipe", None, "dp"),
            P("pipe", None, "dp"),
            P("pipe", ("tensor", "dp")),
            P("pipe", ("tensor", "dp")),
            P("pipe", ("tensor", "dp")),
        ),
        check_vma=False,
    )
```

time: 2540 us -> 1050 us (0.41)
  waiting for transfers between devices: 1570 us -> 383 us
  Pallas kernels: 0 us -> 465 us
  matrix products: 366 us -> 0 us
  other arithmetic: 308 us -> 53.4 us
  local copies, waits for them, and re-layouts: 189 us -> 37.6 us
  starting transfers between devices: 10.8 us -> 64.8 us
  blocking collectives: 55.7 us -> 26.8 us
    psum x5 -> x0, waiting for transfers between devices: 745 us -> none  [the longest x2 399 us: local(): lax.psum(row_part.astype(jnp.bfloat16), 'tensor').astype(jnp.float32)]
    pallas_call x0 -> x38, Pallas kernels: none -> 465 us  [call(): pl.pallas_call(body, grid_spec=pltpu.PrefetchScalarGridSpec(num_scalar_pr...]
    reduce_scatter x5, waiting for transfers between devices: 384 us -> 8.33 us  [share_of(): return lax.psum_scatter(total, 'dp', scatter_dimension=0, tiled=True)]
    dot_general x38 -> x0, matrix products: 366 us -> none  [the longest x2 67.5 us: forward_local(): jnp.dot(second_in, expand, preferred_element_type=jnp.float32)]
    all_gather x4, waiting for transfers between devices: 418 us -> 166 us  [whole_of(): return lax.all_gather(shard, 'dp', axis=0, tiled=True)]
    ppermute x4 -> x76, waiting for transfers between devices: 20 us -> 208 us  [the longest x36 161 us: flipped(): lax.ppermute(array, 'tensor', [(i, i ^ 1 << bit) for i in range(peers)])]
    convert_element_type x29 -> x3, other arithmetic: 137 us -> 3.43 us  [the longest x1 1.66 us: layer_output(): return block.astype(jnp.bfloat16)]
    another operation x26 -> x5, local copies, waits for them, and re-layouts: 79 us -> 5.1 us  [the longest x18 48.3 us: local(): stacked = jax.tree.map(lambda *items: jnp.stack(items), *kept)]
  transfers between devices with their start and end apart: 18 -> 85, of which waited for: 15 -> 55; matrix products, arithmetic and copies ran while one was open for 8% -> 7% of each run, Pallas kernels for 0% -> 42%
where the time goes in v1:
time: 1050 us
  Pallas kernels  465 us (44%)
  waiting for transfers between devices  383 us (36%)
  starting transfers between devices  64.8 us (6%)
  other arithmetic  53.4 us (5%)
  local copies, waits for them, and re-layouts  37.6 us (4%)
  blocking collectives  26.8 us (3%)
  between operations  15.2 us (1%)
    pallas_call x38, Pallas kernels, call(): pl.pallas_call(body, grid_spec=pltpu.PrefetchScalarGridSpec(num_scalar_pr...  465 us
    all_gather x4, waiting for transfers between devices, whole_of(): return lax.all_gather(shard, 'dp', axis=0, tiled=True)  166 us
    ppermute x36, waiting for transfers between devices, flipped(): lax.ppermute(array, 'tensor', [(i, i ^ 1 << bit) for i in range(peers)])  161 us
    ppermute x30, waiting for transfers between devices, swap(): return lax.ppermute(array, 'pipe', [(0, 1), (1, 0)])  43.4 us
    ppermute x36, starting transfers between devices, flipped(): lax.ppermute(array, 'tensor', [(i, i ^ 1 << bit) for i in range(peers)])  36.8 us
    all_gather x1, blocking collectives, local(): lax.all_gather(small, ('pipe', 'dp'), axis=0, tiled=False)  26.8 us
  transfers between devices with their start and end apart: 85, of which 55 were waited for; matrix products, arithmetic and copies ran while one was open for 7% of the time, Pallas kernels for 42%

profile of v1, /device:TPU:0, one launch (start us, length us, event | category | flops | bytes accessed | tf_op | source)
XLA Modules:
  0.0 1046.0 jit_solution(11737029989275511178)
XLA Ops:
  42.1 26.8 %all-gather = bf16[8,1,3072]{2,1,0:T(2,128)(2,1)S(1)} all-gather(bf16[1,1,3072]{2,1,0:T(2,128)(2,1)S(1)} %maximum_bitcast_fusion.2), channel_id=1, replica_groups=mesh['pipe'=2,'tensor'=4,'dp'=4] {'pipe','dp'}, dimensions={0}, use_global_device_ids=true | all-gather | bytes 55296 | tf_op jit(solution)/shard_map/all_gather | solution.py:1000
  74.7 10.5 %shard_map.356 = (bf16[1024,2048]{1,0:T(8,128)(2,1)}, bf16[1024,2048]{1,0:T(8,128)(2,1)}, f32[1024,1]{1,0:T(8,128)}, f32[1024,1]{1,0:T(8,128)}, bf16[2048,1024]{1,0:T(8,128)(2,1)}, /*index=5*/bf16[2048,1024]{1,0:T(8,128)(2,1)}) custom-call(s32[1]{0:T(128)} %dynamic_slice.109.info, bf16[1024,2048]{1,0:T(8,128)(2,1)} %constant_dynamic-slice_fusion.6.z_ref.refs_0_, ...), custom_call_target="tpu_custom_call" | custom-call | flops 1 | bytes 1 | tf_op jit(solution)/shard_map/pallas_call | solution.py:255
  89.9 12.3 %shard_map.358 = (bf16[1024,256]{1,0:T(8,128)(2,1)}, bf16[1024,768]{1,0:T(8,128)(2,1)}, f32[1024,1]{1,0:T(8,128)}) custom-call(s32[1]{0:T(128)} %dynamic_slice.109.info, bf16[1024,2048]{1,0:T(8,128)(2,1)} %get-tuple-element.207.x_ref, bf16[2048,768]{1,0:T(8,128)(2,1)} %all-gather.6.cloned.1.call-done.w_ref.refs_8_, f32[1024,128]{1,0:T(8,128)} %maximum_maximum_fusion.cos_ref, ...), custom_call_target="tpu_custom_call" | custom-call | flops 1 | bytes 1 | tf_op jit(solution)/shard_map/pallas_call | solution.py:255
  103.9 11.6 %shard_map.359 = (bf16[1024,256]{1,0:T(8,128)(2,1)}, bf16[1024,768]{1,0:T(8,128)(2,1)}, f32[1024,1]{1,0:T(8,128)}) custom-call(s32[1]{0:T(128)} %dynamic_slice.109.info, bf16[1024,2048]{1,0:T(8,128)(2,1)} %get-tuple-element.207.x_ref, bf16[2048,768]{1,0:T(8,128)(2,1)} %copy-done.4, f32[1024,128]{1,0:T(8,128)} %maximum_maximum_fusion.cos_ref, ...), custom_call_target="tpu_custom_call" | custom-call | flops 1 | bytes 1 | tf_op jit(solution)/shard_map/pallas_call | solution.py:255
  115.5 134.6 %all-gather.8.cloned.1.call-done.w_ref.refs_4_.refs_6_.outward_ref.contract_ref.refs_10_ = bf16[2048,2304]{1,0:T(8,128)(2,1)} async-done(((bf16[512,2304]{1,0:T(8,128)(2,1)}), bf16[2048,2304]{1,0:T(8,128)(2,1)}) %all-gather.8.cloned.1.call-update) | async-done | bytes 9437200 | tf_op jit(solution)/shard_map/all_gather | solution.py:1017
  253.7 10.9 %shard_map.360 = (bf16[1024,1024]{1,0:T(8,128)(2,1)}, bf16[1024,1024]{1,0:T(8,128)(2,1)}) custom-call(s32[1]{0:T(128)} %dynamic_slice.109.info, bf16[1024,2048]{1,0:T(8,128)(2,1)} %get-tuple-element.208.x_ref, bf16[2048,2304]{1,0:T(8,128)(2,1)} %all-gather.8.cloned.1.call-done.w_ref.refs_4_.refs_6_.outward_ref.contract_ref.refs_10_, f32[1,1024]{1,0:T(1,128)} %bitcast.246), custom_call_target="tpu_custom_call" | custom-call | flops 1 | bytes 1 | tf_op jit(solution)/shard_map/pallas_call | solution.py:255
  265.1 10.7 %shard_map.361 = (bf16[1024,1024]{1,0:T(8,128)(2,1)}, bf16[1024,1024]{1,0:T(8,128)(2,1)}) custom-call(s32[1]{0:T(128)} %dynamic_slice.109.info, bf16[1024,2048]{1,0:T(8,128)(2,1)} %get-tuple-element.208.x_ref, bf16[2048,2304]{1,0:T(8,128)(2,1)} %collective-permute-done.5.w_ref.refs_5_.refs_7_.outward_ref.contract_ref.refs_11_, f32[1,1024]{1,0:T(1,128)} %bitcast.245), custom_call_target="tpu_custom_call" | custom-call | flops 1 | bytes 1 | tf_op jit(solution)/shard_map/pallas_call | solution.py:255
  275.9 17.1 %shard_map.362 = (bf16[128,2048]{1,0:T(8,128)(2,1)}, bf16[128,2048]{1,0:T(8,128)(2,1)}, bf16[256,2048]{1,0:T(8,128)(2,1)}, bf16[128,2048]{1,0:T(8,128)(2,1)}, bf...) custom-call(s32[8]{0:T(128)} %stack.259.info, bf16[1024,256]{1,0:T(8,128)(2,1)} %get-tuple-element.211.refs_0_.refs_5_, ...), custom_call_target="tpu_custom_call" | custom-call | flops 1 | bytes 1 | tf_op jit(solution)/shard_map/pallas_call | solution.py:255
  297.1 10.9 %collective-permute-done.6 = bf16[128,2048]{1,0:T(8,128)(2,1)S(1)} collective-permute-done((bf16[128,2048]{1,0:T(8,128)(2,1)}, bf16[128,2048]{1,0:T(8,128)(2,1)S(1)}, u32[]{:S(2)}, u32[]{:S(2)}) %collective-permute-start.6) | collective-permute-done | bytes 524320 | tf_op jit(solution)/shard_map/ppermute | solution.py:112
  308.0 10.4 collective-permute-done.7
  326.4 9.1 collective-permute-done.10
  347.0 10.8 %collective-permute-done.13.refs_5_ = bf16[128,2048]{1,0:T(8,128)(2,1)S(1)} collective-permute-done((bf16[128,2048]{1,0:T(8,128)(2,1)S(1)}, bf16[128,2048]{1,0:T(8,128)(2,1)S(1)}, u32[]{:S(2)}, u32[]{:S(2)}) %collective-permute-start.13) | collective-permute-done | bytes 524320 | tf_op jit(solution)/shard_map/ppermute | solution.py:112
  361.6 8.8 collective-permute-done.16.refs_6_
  378.1 13.0 %shard_map.363 = (bf16[1024,2048]{1,0:T(8,128)(2,1)}, bf16[1024,2048]{1,0:T(8,128)(2,1)}, bf16[1024,2048]{1,0:T(8,128)(2,1)}, f32[1024,1]{1,0:T(8,128)}, f32[102...) custom-call(s32[8]{0:T(128)} %stack.276.info, bf16[128,2048]{1,0:T(8,128)(2,1)} %copy-done.9, ...), custom_call_target="tpu_custom_call" | custom-call | flops 1 | bytes 1 | tf_op jit(solution)/shard_map/pallas_call | solution.py:255
  391.1 8.8 all-gather.10.cloned.1.call-done.w_ref.outward_ref.refs_8_.refs_10_.refs_4_
  400.0 11.0 %shard_map.368 = (bf16[1024,1024]{1,0:T(8,128)(2,1)}, bf16[1024,1024]{1,0:T(8,128)(2,1)}) custom-call(s32[1]{0:T(128)} %dynamic_slice.109.info, bf16[1024,2048]{1,0:T(8,128)(2,1)} %get-tuple-element.236.x_ref, bf16[2048,2048]{1,0:T(8,128)(2,1)} %all-gather.10.cloned.1.call-done.w_ref.outward_ref.refs_8_.refs_10_.refs_4_, f32[1,1024]{1,0:T(1,128)} %bitcast.248), custom_call_target="tpu_custom_call" | custom-call | flops 1 | bytes 1 | tf_op jit(solution)/shard_map/pallas_call | solution.py:255
  413.4 10.8 %shard_map.364 = (bf16[1024,1024]{1,0:T(8,128)(2,1)}, bf16[1024,1024]{1,0:T(8,128)(2,1)}) custom-call(s32[1]{0:T(128)} %dynamic_slice.109.info, bf16[1024,2048]{1,0:T(8,128)(2,1)} %get-tuple-element.236.x_ref, bf16[2048,2048]{1,0:T(8,128)(2,1)} %collective-permute-done.18.w_ref.outward_ref.refs_9_.refs_11_.refs_5_, f32[1,1024]{1,0:T(1,128)} %bitcast.247), custom_call_target="tpu_custom_call" | custom-call | flops 1 | bytes 1 | tf_op jit(solution)/shard_map/pallas_call | solution.py:255
  424.2 10.3 shard_map.365
  434.5 11.6 %shard_map.366 = (bf16[1024,256]{1,0:T(8,128)(2,1)}, bf16[1024,768]{1,0:T(8,128)(2,1)}, f32[1024,1]{1,0:T(8,128)}) custom-call(s32[1]{0:T(128)} %dynamic_slice.109.info, bf16[1024,2048]{1,0:T(8,128)(2,1)} %get-tuple-element.244.x_ref, bf16[2048,2048]{1,0:T(8,128)(2,1)} %all-gather.10.cloned.1.call-done.w_ref.outward_ref.refs_8_.refs_10_.refs_4_, ...), custom_call_target="tpu_custom_call" | custom-call | flops 1 | bytes 1 | tf_op jit(solution)/shard_map/pallas_call | solution.py:255
  446.1 11.8 %shard_map.367 = (bf16[1024,256]{1,0:T(8,128)(2,1)}, bf16[1024,768]{1,0:T(8,128)(2,1)}, f32[1024,1]{1,0:T(8,128)}) custom-call(s32[1]{0:T(128)} %dynamic_slice.109.info, bf16[1024,2048]{1,0:T(8,128)(2,1)} %get-tuple-element.244.x_ref, bf16[2048,2048]{1,0:T(8,128)(2,1)} %collective-permute-done.18.w_ref.outward_ref.refs_9_.refs_11_.refs_5_, ...), custom_call_target="tpu_custom_call" | custom-call | flops 1 | bytes 1 | tf_op jit(solution)/shard_map/pallas_call | solution.py:255
  457.9 23.0 %all-gather.12.cloned.1.call-done.contract_ref.refs_6_ = bf16[2048,1024]{1,0:T(8,128)(2,1)} async-done(((bf16[512,1024]{1,0:T(8,128)(2,1)}), bf16[2048,1024]{1,0:T(8,128)(2,1)}) %all-gather.12.cloned.1.call-update) | async-done | bytes 4194320 | tf_op jit(solution)/shard_map/all_gather | solution.py:1017
  489.1 11.6 %shard_map.369 = bf16[2048,1024]{1,0:T(8,128)(2,1)} custom-call(s32[1]{0:T(128)} %dynamic_slice.109.info, bf16[2048,1024]{1,0:T(8,128)(2,1)} %get-tuple-element.209.refs_0_.refs_1_, bf16[1024,1024]{1,0:T(8,128)(2,1)} %get-tuple-element.247.refs_1_.refs_2_, bf16[2048,256]{1,0:T(8,128)(2,1)} %copy-done.24, bf16[2048,256]{1,0:T(8,128)(2,1)} %copy-done.27, ...), custom_call_target="tpu_custom_call" | custom-call | flops 1 | bytes 1 | tf_op jit(solution)/shard_map/pallas_call | solution.py:255
  510.1 10.9 %shard_map.371 = (bf16[1024,256]{1,0:T(8,128)(2,1)}, bf16[1024,1024]{1,0:T(8,128)(2,1)}, f32[1,1024]{1,0:T(1,128)}) custom-call(s32[1]{0:T(128)} %dynamic_slice.109.info, bf16[1024,2048]{1,0:T(8,128)(2,1)} %get-tuple-element.263.g_ref, bf16[2048,2048]{1,0:T(8,128)(2,1)} %collective-permute-done.18.w_ref.outward_ref.refs_9_.refs_11_.refs_5_, ...), custom_call_target="tpu_custom_call" | custom-call | flops 1 | bytes 1 | tf_op jit(solution)/shard_map/pallas_call | solution.py:255
  521.1 10.3 shard_map.372
  532.4 11.0 %shard_map.370 = (bf16[1024,256]{1,0:T(8,128)(2,1)}, bf16[1024,1024]{1,0:T(8,128)(2,1)}, f32[1,1024]{1,0:T(1,128)}) custom-call(s32[1]{0:T(128)} %dynamic_slice.109.info, bf16[1024,2048]{1,0:T(8,128)(2,1)} %get-tuple-element.263.g_ref, bf16[2048,2048]{1,0:T(8,128)(2,1)} %all-gather.10.cloned.1.call-done.w_ref.outward_ref.refs_8_.refs_10_.refs_4_, ...), custom_call_target="tpu_custom_call" | custom-call | flops 1 | bytes 1 | tf_op jit(solution)/shard_map/pallas_call | solution.py:255
  545.5 11.6 %shard_map.373 = bf16[2048,1024]{1,0:T(8,128)(2,1)} custom-call(s32[1]{0:T(128)} %dynamic_slice.109.info, bf16[2048,1024]{1,0:T(8,128)(2,1)} %get-tuple-element.267.refs_0_, bf16[1024,1024]{1,0:T(8,128)(2,1)} %get-tuple-element.268.refs_1_.refs_6_, bf16[2048,256]{1,0:T(8,128)(2,1)} %copy-done.20, bf16[2048,256]{1,0:T(8,128)(2,1)} %copy-done.21, ...), custom_call_target="tpu_custom_call" | custom-call | flops 1 | bytes 1 | tf_op jit(solution)/shard_map/pallas_call | solution.py:255
  557.8 8.2 shard_map.375.refs_5_.refs_2_
  576.1 30.8 %shard_map.376 = (bf16[128,2048]{1,0:T(8,128)(2,1)}, bf16[128,2048]{1,0:T(8,128)(2,1)}, bf16[256,2048]{1,0:T(8,128)(2,1)}, bf16[128,2048]{1,0:T(8,128)(2,1)}, bf...) custom-call(s32[16]{0:T(128)} %stack.282.info, ...), custom_call_target="tpu_custom_call" | custom-call | flops 1 | bytes 1 | tf_op jit(solution)/shard_map/pallas_call | solution.py:255
  606.9 11.0 %shard_map.381 = (bf16[2048,256]{1,0:T(8,128)(2,1)}, bf16[2048,256]{1,0:T(8,128)(2,1)}, bf16[2048,256]{1,0:T(8,128)(2,1)}, bf16[2048,256]{1,0:T(8,128)(2,1)}) custom-call(s32[1]{0:T(128)} %dynamic_slice.109.info, bf16[2048,1024]{1,0:T(8,128)(2,1)} %get-tuple-element.319.refs_0_, bf16[2048,1024]{1,0:T(8,128)(2,1)} %get-tuple-element.209.refs_0_.refs_1_, ...), custom_call_target="tpu_custom_call" | custom-call | flops 17179869184 | bytes 16777216 | tf_op jit(solution)/shard_map/pallas_call | solution.py:255
  626.3 12.5 %shard_map.382 = bf16[2048,1024]{1,0:T(8,128)(2,1)} custom-call(s32[1]{0:T(128)} %dynamic_slice.109.info, bf16[2048,1024]{1,0:T(8,128)(2,1)} %get-tuple-element.319.refs_0_, bf16[2048,1024]{1,0:T(8,128)(2,1)} %get-tuple-element.209.refs_0_.refs_1_, bf16[1024,768]{1,0:T(8,128)(2,1)} %shard_map.374.refs_4_.refs_2_, ...), custom_call_target="tpu_custom_call" | custom-call | flops 17179869184 | bytes 16777216 | tf_op jit(solution)/shard_map/pallas_call | solution.py:255
  643.0 10.9 %collective-permute-done.28 = bf16[128,2048]{1,0:T(8,128)(2,1)S(1)} collective-permute-done((bf16[128,2048]{1,0:T(8,128)(2,1)}, bf16[128,2048]{1,0:T(8,128)(2,1)S(1)}, u32[]{:S(2)}, u32[]{:S(2)}) %collective-permute-start.28) | collective-permute-done | bytes 524320 | tf_op jit(solution)/shard_map/ppermute | solution.py:112
  653.9 10.4 collective-permute-done.29
  669.9 8.9 collective-permute-done.32
  687.0 10.8 %collective-permute-done.35.refs_5_ = bf16[128,2048]{1,0:T(8,128)(2,1)S(1)} collective-permute-done((bf16[128,2048]{1,0:T(8,128)(2,1)S(1)}, bf16[128,2048]{1,0:T(8,128)(2,1)S(1)}, u32[]{:S(2)}, u32[]{:S(2)}) %collective-permute-start.35) | collective-permute-done | bytes 524320 | tf_op jit(solution)/shard_map/ppermute | solution.py:112
  700.5 10.1 collective-permute-done.38.refs_6_
  726.2 10.3 shard_map.378
  744.9 11.6 %shard_map.379 = bf16[2048,1024]{1,0:T(8,128)(2,1)} custom-call(s32[1]{0:T(128)} %dynamic_slice.109.info, bf16[2048,1024]{1,0:T(8,128)(2,1)} %get-tuple-element.309.refs_0_.refs_2_, bf16[1024,1024]{1,0:T(8,128)(2,1)} %get-tuple-element.215.refs_2_.refs_1_, bf16[2048,256]{1,0:T(8,128)(2,1)} %copy-done.23, bf16[2048,256]{1,0:T(8,128)(2,1)} %copy-done.25, ...), custom_call_target="tpu_custom_call" | custom-call | flops 1 | bytes 1 | tf_op jit(solution)/shard_map/pallas_call | solution.py:255
  756.5 11.0 %shard_map.380 = (bf16[1024,256]{1,0:T(8,128)(2,1)}, bf16[1024,1024]{1,0:T(8,128)(2,1)}, f32[1,1024]{1,0:T(1,128)}) custom-call(s32[1]{0:T(128)} %dynamic_slice.109.info, bf16[1024,2048]{1,0:T(8,128)(2,1)} %get-tuple-element.315.g_ref, bf16[2048,2304]{1,0:T(8,128)(2,1)} %all-gather.8.cloned.1.call-done.w_ref.refs_4_.refs_6_.outward_ref.contract_ref.refs_10_, ...), custom_call_target="tpu_custom_call" | custom-call | flops 1 | bytes 1 | tf_op jit(solution)/shard_map/pallas_call | solution.py:255
  767.6 10.9 %shard_map.384 = (bf16[1024,256]{1,0:T(8,128)(2,1)}, bf16[1024,1024]{1,0:T(8,128)(2,1)}, f32[1,1024]{1,0:T(1,128)}) custom-call(s32[1]{0:T(128)} %dynamic_slice.109.info, bf16[1024,2048]{1,0:T(8,128)(2,1)} %get-tuple-element.315.g_ref, bf16[2048,2304]{1,0:T(8,128)(2,1)} %collective-permute-done.5.w_ref.refs_5_.refs_7_.outward_ref.contract_ref.refs_11_, ...), custom_call_target="tpu_custom_call" | custom-call | flops 1 | bytes 1 | tf_op jit(solution)/shard_map/pallas_call | solution.py:255
  794.0 15.1 %shard_map.386 = (bf16[2048,512]{1,0:T(8,128)(2,1)}, bf16[2048,512]{1,0:T(8,128)(2,1)}, bf16[2048,512]{1,0:T(8,128)(2,1)}, bf16[2048,512]{1,0:T(8,128)(2,1)}) custom-call(s32[1]{0:T(128)} %dynamic_slice.109.info, bf16[2048,1024]{1,0:T(8,128)(2,1)} %get-tuple-element.248.refs_0_, bf16[2048,1024]{1,0:T(8,128)(2,1)} %get-tuple-element.249.refs_1_, ...), custom_call_target="tpu_custom_call" | custom-call | flops 1 | bytes 1 | tf_op jit(solution)/shard_map/pallas_call | solution.py:255
  822.6 18.0 %shard_map.387 = bf16[2048,2048]{1,0:T(8,128)(2,1)} custom-call(s32[1]{0:T(128)} %dynamic_slice.109.info, bf16[2048,1024]{1,0:T(8,128)(2,1)} %get-tuple-element.248.refs_0_, bf16[2048,1024]{1,0:T(8,128)(2,1)} %get-tuple-element.249.refs_1_, bf16[2048,1024]{1,0:T(8,128)(2,1)} %get-tuple-element.309.refs_0_.refs_2_, ...), custom_call_target="tpu_custom_call" | custom-call | flops 1 | bytes 1 | tf_op jit(solution)/shard_map/pallas_call | solution.py:255
  840.6 17.2 %shard_map.388 = (bf16[128,2048]{1,0:T(8,128)(2,1)}, bf16[128,2048]{1,0:T(8,128)(2,1)}, bf16[256,2048]{1,0:T(8,128)(2,1)}, bf16[128,2048]{1,0:T(8,128)(2,1)}, bf...) custom-call(s32[8]{0:T(128)} %stack.259.info, bf16[1024,256]{1,0:T(8,128)(2,1)} %get-tuple-element.245.refs_3_.refs_0_, ...), custom_call_target="tpu_custom_call" | custom-call | flops 1 | bytes 1 | tf_op jit(solution)/shard_map/pallas_call | solution.py:255
  864.9 31.4 %shard_map.389 = (bf16[128,2048]{1,0:T(8,128)(2,1)}, bf16[128,2048]{1,0:T(8,128)(2,1)}, bf16[256,2048]{1,0:T(8,128)(2,1)}, bf16[128,2048]{1,0:T(8,128)(2,1)}, bf...) custom-call(s32[16]{0:T(128)} %stack.282.info, ...), custom_call_target="tpu_custom_call" | custom-call | flops 1 | bytes 1 | tf_op jit(solution)/shard_map/pallas_call | solution.py:255
  904.9 8.7 collective-permute-done.62
  914.3 10.4 collective-permute-done.61
  965.1 13.5 %shard_map.390 = (f32[2048,512]{1,0:T(8,128)}, f32[2048,512]{1,0:T(8,128)}, f32[2048,512]{1,0:T(8,128)}) custom-call(s32[1]{0:T(128)} %bitcast.14.info, bf16[512,1024]{1,0:T(8,128)(2,1)} %reduce-scatter.12.cloned.1.call-done.refs_0_, bf16[512,1024]{1,0:T(8,128)(2,1)} %copy-done.19, bf16[512,1024]{1,0:T(8,128)(2,1)} %collective-permute-done.67.refs_2_, ...), custom_call_target="tpu_custom_call" | custom-call | flops 1 | bytes 1 | tf_op jit(solution)/shard_map/pallas_call | solution.py:255
  1015.3 12.7 %shard_map.391 = (f32[3,512,512]{2,1,0:T(8,128)}, f32[3,512,512]{2,1,0:T(8,128)}, f32[3,512,512]{2,1,0:T(8,128)}) custom-call(s32[1]{0:T(128)} %bitcast.14.info, bf16[512,2048]{1,0:T(8,128)(2,1)} %reduce-scatter.14.cloned.1.call-done.refs_0_, bf16[512,2048]{1,0:T(8,128)(2,1)} %copy-done, bf16[512,1024]{1,0:T(8,128)(2,1)} %collective-permute-done.69.refs_2_, ...), custom_call_target="tpu_custom_call" | custom-call | flops 1 | bytes 1 | tf_op jit(solution)/shard_map/pallas_call | solution.py:255
  1028.1 11.2 %shard_map.393 = (f32[1,512,2048]{2,1,0:T(8,128)}, f32[1,512,2048]{2,1,0:T(8,128)}, f32[1,512,2048]{2,1,0:T(8,128)}) custom-call(s32[1]{0:T(128)} %bitcast.14.info, bf16[512,2048]{1,0:T(8,128)(2,1)} %reduce-scatter.14.cloned.1.call-done.refs_0_, bf16[512,2048]{1,0:T(8,128)(2,1)} %copy-done, bf16[512,1024]{1,0:T(8,128)(2,1)} %collective-permute-done.70.refs_2_, ...), custom_call_target="tpu_custom_call" | custom-call | flops 1 | bytes 1 | tf_op jit(solution)/shard_map/pallas_call | solution.py:255
  (412 shorter events, 294.5 us)
Async XLA Ops:
  7.2 78.0 %all-gather.6.cloned.1.call-start = ((), (), s32[]{:S(2)}) async-start(), calls=%async_computation.5 | async-start | bytes 3932160 | tf_op jit(solution)/shard_map/all_gather | solution.py:1017
  14.6 235.6 %all-gather.8.cloned.1.call-start = ((), (), s32[]{:S(2)}) async-start(), calls=%async_computation.6 | async-start | bytes 11796480 | tf_op jit(solution)/shard_map/all_gather | solution.py:1017
  32.3 367.6 %all-gather.10.cloned.1.call-start = ((), (), s32[]{:S(2)}) async-start(), calls=%async_computation.7 | async-start | bytes 10485760 | tf_op jit(solution)/shard_map/all_gather | solution.py:1017
  85.2 17.0 %collective-permute-start.1 = (bf16[2048,768]{1,0:T(8,128)(2,1)}, bf16[2048,768]{1,0:T(8,128)(2,1)S(1)}, u32[]{:S(2)}, u32[]{:S(2)}) collective-permute-start(bf16[2048,768]{1,0:T(8,128)(2,1)} %all-gather.6.cloned.1.call-done.w_ref.refs_8_), channel_id=1, source_target_pairs={{0,16},{16,0},{1,17},{17,1},{2,18},{18,2},{3,19},{19,3},{4,20},{20... | collective-permute-start | bytes 9437192 | tf_op jit(solution)/shard_map/ppermute | solution.py:92
  250.1 15.0 %collective-permute-start.5 = (bf16[2048,2304]{1,0:T(8,128)(2,1)}, bf16[2048,2304]{1,0:T(8,128)(2,1)}, u32[]{:S(2)}, u32[]{:S(2)}) collective-permute-start(bf16[2048,2304]{1,0:T(8,128)(2,1)} %all-gather.8.cloned.1.call-done.w_ref.refs_4_.refs_6_.outward_ref.contract_ref.refs_10_), channel_id=1, source_target_pairs={{0,16},{16,0},{1,17},{17,1},{2,18},{18,2},{3,19},{19,3},{4,20},{20... | collective-permute-start | bytes 28311560 | tf_op jit(solution)/shard_map/ppermute | solution.py:92
  251.8 229.1 %all-gather.12.cloned.1.call-start = ((), (), s32[]{:S(2)}) async-start(), calls=%async_computation.8 | async-start | bytes 5242880 | tf_op jit(solution)/shard_map/all_gather | solution.py:1017
  293.0 15.0 %collective-permute-start.6 = (bf16[128,2048]{1,0:T(8,128)(2,1)}, bf16[128,2048]{1,0:T(8,128)(2,1)S(1)}, u32[]{:S(2)}, u32[]{:S(2)}) collective-permute-start(bf16[128,2048]{1,0:T(8,128)(2,1)} %get-tuple-element.218), channel_id=1, source_target_pairs={{0,4},{4,0},{8,12},{12,8},{1,5},{5,1},{9,13},{13,9},{2,6},{6,2},{1... | collective-permute-start | bytes 1572872 | tf_op jit(solution)/shard_map/ppermute | solution.py:112
  294.5 23.9 %collective-permute-start.7 = (bf16[128,2048]{1,0:T(8,128)(2,1)}, bf16[128,2048]{1,0:T(8,128)(2,1)S(1)}, u32[]{:S(2)}, u32[]{:S(2)}) collective-permute-start(bf16[128,2048]{1,0:T(8,128)(2,1)} %get-tuple-element.219), channel_id=1, source_target_pairs={{0,4},{4,0},{8,12},{12,8},{1,5},{5,1},{9,13},{13,9},{2,6},{6,2},{1... | collective-permute-start | bytes 1572872 | tf_op jit(solution)/shard_map/ppermute | solution.py:112
  295.1 23.4 %collective-permute-start.8 = (bf16[128,2048]{1,0:T(8,128)(2,1)}, bf16[128,2048]{1,0:T(8,128)(2,1)S(1)}, u32[]{:S(2)}, u32[]{:S(2)}) collective-permute-start(bf16[128,2048]{1,0:T(8,128)(2,1)} %get-tuple-element.220), channel_id=1, source_target_pairs={{0,8},{4,12},{8,0},{12,4},{1,9},{5,13},{9,1},{13,5},{2,10},{6,14},... | collective-permute-start | bytes 1572872 | tf_op jit(solution)/shard_map/ppermute | solution.py:112
  296.6 23.4 %collective-permute-start.9 = (bf16[128,2048]{1,0:T(8,128)(2,1)}, bf16[128,2048]{1,0:T(8,128)(2,1)S(1)}, u32[]{:S(2)}, u32[]{:S(2)}) collective-permute-start(bf16[128,2048]{1,0:T(8,128)(2,1)} %get-tuple-element.221), channel_id=1, source_target_pairs={{0,8},{4,12},{8,0},{12,4},{1,9},{5,13},{9,1},{13,5},{2,10},{6,14},... | collective-permute-start | bytes 1572872 | tf_op jit(solution)/shard_map/ppermute | solution.py:112
  342.9 14.9 %collective-permute-start.13 = (bf16[128,2048]{1,0:T(8,128)(2,1)S(1)}, bf16[128,2048]{1,0:T(8,128)(2,1)S(1)}, u32[]{:S(2)}, u32[]{:S(2)}) collective-permute-start(bf16[128,2048]{1,0:T(8,128)(2,1)S(1)} %get-tuple-element.490.refs_4_), channel_id=1, source_target_pairs={{0,4},{4,0},{8,12},{12,8},{1,5},{5,1},{9,13},{13,9},{2,6},{6,2},{1... | collective-permute-start | bytes 1572872 | tf_op jit(solution)/shard_map/ppermute | solution.py:112
  344.9 25.5 %collective-permute-start.16 = (bf16[128,2048]{1,0:T(8,128)(2,1)S(1)}, bf16[128,2048]{1,0:T(8,128)(2,1)S(1)}, u32[]{:S(2)}, u32[]{:S(2)}) collective-permute-start(bf16[128,2048]{1,0:T(8,128)(2,1)S(1)} %get-tuple-element.490.refs_4_), channel_id=1, source_target_pairs={{0,8},{4,12},{8,0},{12,4},{1,9},{5,13},{9,1},{13,5},{2,10},{6,14},... | collective-permute-start | bytes 1572872 | tf_op jit(solution)/shard_map/ppermute | solution.py:112
  346.4 24.1 %collective-permute-start.14 = (bf16[128,2048]{1,0:T(8,128)(2,1)S(1)}, bf16[128,2048]{1,0:T(8,128)(2,1)S(1)}, u32[]{:S(2)}, u32[]{:S(2)}) collective-permute-start(bf16[128,2048]{1,0:T(8,128)(2,1)S(1)} %get-tuple-element.491.refs_0_), channel_id=1, source_target_pairs={{0,4},{4,0},{8,12},{12,8},{1,5},{5,1},{9,13},{13,9},{2,6},{6,2},{1... | collective-permute-start | bytes 1572872 | tf_op jit(solution)/shard_map/ppermute | solution.py:112
  359.2 17.7 %collective-permute-start.15 = (bf16[128,2048]{1,0:T(8,128)(2,1)S(1)}, bf16[128,2048]{1,0:T(8,128)(2,1)}, u32[]{:S(2)}, u32[]{:S(2)}) collective-permute-start(bf16[128,2048]{1,0:T(8,128)(2,1)S(1)} %collective-permute-done.12.refs_1_), channel_id=1, source_target_pairs={{0,4},{4,0},{8,12},{12,8},{1,5},{5,1},{9,13},{13,9},{2,6},{6,2},{1... | collective-permute-start | bytes 1572872 | tf_op jit(solution)/shard_map/ppermute | solution.py:112
  359.8 18.2 %collective-permute-start.17 = (bf16[128,2048]{1,0:T(8,128)(2,1)S(1)}, bf16[128,2048]{1,0:T(8,128)(2,1)}, u32[]{:S(2)}, u32[]{:S(2)}) collective-permute-start(bf16[128,2048]{1,0:T(8,128)(2,1)S(1)} %collective-permute-done.13.refs_5_), channel_id=1, source_target_pairs={{0,8},{4,12},{8,0},{12,4},{1,9},{5,13},{9,1},{13,5},{2,10},{6,14},... | collective-permute-start | bytes 1572872 | tf_op jit(solution)/shard_map/ppermute | solution.py:112
  400.0 176.1 %reduce-scatter.6.cloned.1.call-start = ((), (), s32[]{:S(2)}) async-start(), calls=%async_computation.9 | async-start | bytes 5242880 | tf_op jit(solution)/shard_map/reduce_scatter | solution.py:875
  500.6 217.5 %reduce-scatter.8.cloned.1.call-start = ((), (), s32[]{:S(2)}) async-start(), calls=%async_computation.10 | async-start | bytes 5242880 | tf_op jit(solution)/shard_map/reduce_scatter | solution.py:875
  557.1 236.9 %reduce-scatter.10.cloned.1.call-start = ((), (), s32[]{:S(2)}) async-start(), calls=%async_computation.11 | async-start | bytes 5242880 | tf_op jit(solution)/shard_map/reduce_scatter | solution.py:875
  638.8 259.6 %reduce-scatter.12.cloned.1.call-start = ((), (), s32[]{:S(2)}) async-start(), calls=%async_computation.12 | async-start | bytes 5242880 | tf_op jit(solution)/shard_map/reduce_scatter | solution.py:875
  638.9 15.1 %collective-permute-start.28 = (bf16[128,2048]{1,0:T(8,128)(2,1)}, bf16[128,2048]{1,0:T(8,128)(2,1)S(1)}, u32[]{:S(2)}, u32[]{:S(2)}) collective-permute-start(bf16[128,2048]{1,0:T(8,128)(2,1)} %get-tuple-element.284), channel_id=1, source_target_pairs={{0,4},{4,0},{8,12},{12,8},{1,5},{5,1},{9,13},{13,9},{2,6},{6,2},{1... | collective-permute-start | bytes 1572872 | tf_op jit(solution)/shard_map/ppermute | solution.py:112
  640.4 23.9 %collective-permute-start.29 = (bf16[128,2048]{1,0:T(8,128)(2,1)}, bf16[128,2048]{1,0:T(8,128)(2,1)S(1)}, u32[]{:S(2)}, u32[]{:S(2)}) collective-permute-start(bf16[128,2048]{1,0:T(8,128)(2,1)} %get-tuple-element.285), channel_id=1, source_target_pairs={{0,4},{4,0},{8,12},{12,8},{1,5},{5,1},{9,13},{13,9},{2,6},{6,2},{1... | collective-permute-start | bytes 1572872 | tf_op jit(solution)/shard_map/ppermute | solution.py:112
  641.0 23.4 %collective-permute-start.30 = (bf16[128,2048]{1,0:T(8,128)(2,1)S(1)}, bf16[128,2048]{1,0:T(8,128)(2,1)S(1)}, u32[]{:S(2)}, u32[]{:S(2)}) collective-permute-start(bf16[128,2048]{1,0:T(8,128)(2,1)S(1)} %copy-done.68), channel_id=1, source_target_pairs={{0,8},{4,12},{8,0},{12,4},{1,9},{5,13},{9,1},{13,5},{2,10},{6,14},... | collective-permute-start | bytes 1572872 | tf_op jit(solution)/shard_map/ppermute | solution.py:112
  642.4 23.2 %collective-permute-start.31 = (bf16[128,2048]{1,0:T(8,128)(2,1)S(1)}, bf16[128,2048]{1,0:T(8,128)(2,1)S(1)}, u32[]{:S(2)}, u32[]{:S(2)}) collective-permute-start(bf16[128,2048]{1,0:T(8,128)(2,1)S(1)} %copy-done.67), channel_id=1, source_target_pairs={{0,8},{4,12},{8,0},{12,4},{1,9},{5,13},{9,1},{13,5},{2,10},{6,14},... | collective-permute-start | bytes 1572872 | tf_op jit(solution)/shard_map/ppermute | solution.py:112
  682.9 14.9 %collective-permute-start.35 = (bf16[128,2048]{1,0:T(8,128)(2,1)S(1)}, bf16[128,2048]{1,0:T(8,128)(2,1)S(1)}, u32[]{:S(2)}, u32[]{:S(2)}) collective-permute-start(bf16[128,2048]{1,0:T(8,128)(2,1)S(1)} %get-tuple-element.303.refs_4_), channel_id=1, source_target_pairs={{0,4},{4,0},{8,12},{12,8},{1,5},{5,1},{9,13},{13,9},{2,6},{6,2},{1... | collective-permute-start | bytes 1572872 | tf_op jit(solution)/shard_map/ppermute | solution.py:112
  685.0 25.5 %collective-permute-start.38 = (bf16[128,2048]{1,0:T(8,128)(2,1)S(1)}, bf16[128,2048]{1,0:T(8,128)(2,1)S(1)}, u32[]{:S(2)}, u32[]{:S(2)}) collective-permute-start(bf16[128,2048]{1,0:T(8,128)(2,1)S(1)} %get-tuple-element.303.refs_4_), channel_id=1, source_target_pairs={{0,8},{4,12},{8,0},{12,4},{1,9},{5,13},{9,1},{13,5},{2,10},{6,14},... | collective-permute-start | bytes 1572872 | tf_op jit(solution)/shard_map/ppermute | solution.py:112
  686.5 24.1 %collective-permute-start.36 = (bf16[128,2048]{1,0:T(8,128)(2,1)S(1)}, bf16[128,2048]{1,0:T(8,128)(2,1)S(1)}, u32[]{:S(2)}, u32[]{:S(2)}) collective-permute-start(bf16[128,2048]{1,0:T(8,128)(2,1)S(1)} %get-tuple-element.295.refs_0_), channel_id=1, source_target_pairs={{0,4},{4,0},{8,12},{12,8},{1,5},{5,1},{9,13},{13,9},{2,6},{6,2},{1... | collective-permute-start | bytes 1572872 | tf_op jit(solution)/shard_map/ppermute | solution.py:112
  699.3 17.6 %collective-permute-start.37 = (bf16[128,2048]{1,0:T(8,128)(2,1)S(1)}, bf16[128,2048]{1,0:T(8,128)(2,1)S(1)}, u32[]{:S(2)}, u32[]{:S(2)}) collective-permute-start(bf16[128,2048]{1,0:T(8,128)(2,1)S(1)} %collective-permute-done.34.refs_1_), channel_id=1, source_target_pairs={{0,4},{4,0},{8,12},{12,8},{1,5},{5,1},{9,13},{13,9},{2,6},{6,2},{1... | collective-permute-start | bytes 1572872 | tf_op jit(solution)/shard_map/ppermute | solution.py:112
  699.9 18.3 %collective-permute-start.39 = (bf16[128,2048]{1,0:T(8,128)(2,1)S(1)}, bf16[128,2048]{1,0:T(8,128)(2,1)}, u32[]{:S(2)}, u32[]{:S(2)}) collective-permute-start(bf16[128,2048]{1,0:T(8,128)(2,1)S(1)} %collective-permute-done.35.refs_5_), channel_id=1, source_target_pairs={{0,8},{4,12},{8,0},{12,4},{1,9},{5,13},{9,1},{13,5},{2,10},{6,14},... | collective-permute-start | bytes 1572872 | tf_op jit(solution)/shard_map/ppermute | solution.py:112
  756.5 228.1 %reduce-scatter.14.cloned.1.call-start = ((), (), s32[]{:S(2)}) async-start(), calls=%async_computation.13 | async-start | bytes 10485760 | tf_op jit(solution)/shard_map/reduce_scatter | solution.py:875
  857.8 38.6 %collective-permute-start.52 = (bf16[128,2048]{1,0:T(8,128)(2,1)}, bf16[128,2048]{1,0:T(8,128)(2,1)S(1)}, u32[]{:S(2)}, u32[]{:S(2)}) collective-permute-start(bf16[128,2048]{1,0:T(8,128)(2,1)} %get-tuple-element.343), channel_id=1, source_target_pairs={{0,4},{4,0},{8,12},{12,8},{1,5},{5,1},{9,13},{13,9},{2,6},{6,2},{1... | collective-permute-start | bytes 1572872 | tf_op jit(solution)/shard_map/ppermute | solution.py:112
  859.2 37.2 %collective-permute-start.53 = (bf16[128,2048]{1,0:T(8,128)(2,1)}, bf16[128,2048]{1,0:T(8,128)(2,1)S(1)}, u32[]{:S(2)}, u32[]{:S(2)}) collective-permute-start(bf16[128,2048]{1,0:T(8,128)(2,1)} %get-tuple-element.344), channel_id=1, source_target_pairs={{0,4},{4,0},{8,12},{12,8},{1,5},{5,1},{9,13},{13,9},{2,6},{6,2},{1... | collective-permute-start | bytes 1572872 | tf_op jit(solution)/shard_map/ppermute | solution.py:112
  859.9 36.5 %collective-permute-start.54 = (bf16[128,2048]{1,0:T(8,128)(2,1)}, bf16[128,2048]{1,0:T(8,128)(2,1)S(1)}, u32[]{:S(2)}, u32[]{:S(2)}) collective-permute-start(bf16[128,2048]{1,0:T(8,128)(2,1)} %get-tuple-element.345), channel_id=1, source_target_pairs={{0,8},{4,12},{8,0},{12,4},{1,9},{5,13},{9,1},{13,5},{2,10},{6,14},... | collective-permute-start | bytes 1572872 | tf_op jit(solution)/shard_map/ppermute | solution.py:112
  860.6 35.8 %collective-permute-start.55 = (bf16[128,2048]{1,0:T(8,128)(2,1)}, bf16[128,2048]{1,0:T(8,128)(2,1)S(1)}, u32[]{:S(2)}, u32[]{:S(2)}) collective-permute-start(bf16[128,2048]{1,0:T(8,128)(2,1)} %get-tuple-element.346), channel_id=1, source_target_pairs={{0,8},{4,12},{8,0},{12,4},{1,9},{5,13},{9,1},{13,5},{2,10},{6,14},... | collective-permute-start | bytes 1572872 | tf_op jit(solution)/shard_map/ppermute | solution.py:112
  862.6 101.3 %collective-permute-start.67 = (bf16[512,1024]{1,0:T(8,128)(2,1)}, bf16[512,1024]{1,0:T(8,128)(2,1)}, u32[]{:S(2)}, u32[]{:S(2)}) collective-permute-start(bf16[512,1024]{1,0:T(8,128)(2,1)} %reduce-scatter.6.cloned.1.call-done.refs_3_), channel_id=1, source_target_pairs={{0,16},{1,17},{2,18},{3,19},{4,20},{5,21},{6,22},{7,23},{8,24},{9,... | collective-permute-start | bytes 3145736 | tf_op jit(solution)/shard_map/ppermute | solution.py:1211
  898.4 15.1 %collective-permute-start.62 = (bf16[128,2048]{1,0:T(8,128)(2,1)}, bf16[128,2048]{1,0:T(8,128)(2,1)S(1)}, u32[]{:S(2)}, u32[]{:S(2)}) collective-permute-start(bf16[128,2048]{1,0:T(8,128)(2,1)} %get-tuple-element.366), channel_id=1, source_target_pairs={{0,8},{4,12},{8,0},{12,4},{1,9},{5,13},{9,1},{13,5},{2,10},{6,14},... | collective-permute-start | bytes 1572872 | tf_op jit(solution)/shard_map/ppermute | solution.py:112
  899.2 25.5 %collective-permute-start.61 = (bf16[128,2048]{1,0:T(8,128)(2,1)}, bf16[128,2048]{1,0:T(8,128)(2,1)S(1)}, u32[]{:S(2)}, u32[]{:S(2)}) collective-permute-start(bf16[128,2048]{1,0:T(8,128)(2,1)} %get-tuple-element.364), channel_id=1, source_target_pairs={{0,8},{4,12},{8,0},{12,4},{1,9},{5,13},{9,1},{13,5},{2,10},{6,14},... | collective-permute-start | bytes 1572872 | tf_op jit(solution)/shard_map/ppermute | solution.py:112
  900.5 25.6 %collective-permute-start.60 = (bf16[128,2048]{1,0:T(8,128)(2,1)}, bf16[128,2048]{1,0:T(8,128)(2,1)S(1)}, u32[]{:S(2)}, u32[]{:S(2)}) collective-permute-start(bf16[128,2048]{1,0:T(8,128)(2,1)} %get-tuple-element.362), channel_id=1, source_target_pairs={{0,4},{4,0},{8,12},{12,8},{1,5},{5,1},{9,13},{13,9},{2,6},{6,2},{1... | collective-permute-start | bytes 1572872 | tf_op jit(solution)/shard_map/ppermute | solution.py:112
  901.8 24.3 %collective-permute-start.59 = (bf16[128,2048]{1,0:T(8,128)(2,1)}, bf16[128,2048]{1,0:T(8,128)(2,1)S(1)}, u32[]{:S(2)}, u32[]{:S(2)}) collective-permute-start(bf16[128,2048]{1,0:T(8,128)(2,1)} %get-tuple-element.360), channel_id=1, source_target_pairs={{0,4},{4,0},{8,12},{12,8},{1,5},{5,1},{9,13},{13,9},{2,6},{6,2},{1... | collective-permute-start | bytes 1572872 | tf_op jit(solution)/shard_map/ppermute | solution.py:112
  913.5 22.5 %collective-permute-start.56 = (bf16[128,2048]{1,0:T(8,128)(2,1)S(1)}, bf16[128,2048]{1,0:T(8,128)(2,1)S(1)}, u32[]{:S(2)}, u32[]{:S(2)}) collective-permute-start(bf16[128,2048]{1,0:T(8,128)(2,1)S(1)} %fusion.36), channel_id=1, source_target_pairs={{0,8},{4,12},{8,0},{12,4},{1,9},{5,13},{9,1},{13,5},{2,10},{6,14},... | collective-permute-start | bytes 1572872 | tf_op jit(solution)/shard_map/ppermute | solution.py:112
  924.8 14.9 %collective-permute-start.57 = (bf16[128,2048]{1,0:T(8,128)(2,1)S(1)}, bf16[128,2048]{1,0:T(8,128)(2,1)S(1)}, u32[]{:S(2)}, u32[]{:S(2)}) collective-permute-start(bf16[128,2048]{1,0:T(8,128)(2,1)S(1)} %fusion.34), channel_id=1, source_target_pairs={{0,4},{4,0},{8,12},{12,8},{1,5},{5,1},{9,13},{13,9},{2,6},{6,2},{1... | collective-permute-start | bytes 1572872 | tf_op jit(solution)/shard_map/ppermute | solution.py:112
  926.7 17.7 %collective-permute-start.63 = (bf16[128,2048]{1,0:T(8,128)(2,1)S(1)}, bf16[128,2048]{1,0:T(8,128)(2,1)S(1)}, u32[]{:S(2)}, u32[]{:S(2)}) collective-permute-start(bf16[128,2048]{1,0:T(8,128)(2,1)S(1)} %fusion.28), channel_id=1, source_target_pairs={{0,8},{4,12},{8,0},{12,4},{1,9},{5,13},{9,1},{13,5},{2,10},{6,14},... | collective-permute-start | bytes 1572872 | tf_op jit(solution)/shard_map/ppermute | solution.py:112
  927.8 18.2 %collective-permute-start.64 = (bf16[128,2048]{1,0:T(8,128)(2,1)S(1)}, bf16[128,2048]{1,0:T(8,128)(2,1)S(1)}, u32[]{:S(2)}, u32[]{:S(2)}) collective-permute-start(bf16[128,2048]{1,0:T(8,128)(2,1)S(1)} %fusion.26), channel_id=1, source_target_pairs={{0,4},{4,0},{8,12},{12,8},{1,5},{5,1},{9,13},{13,9},{2,6},{6,2},{1... | collective-permute-start | bytes 1572872 | tf_op jit(solution)/shard_map/ppermute | solution.py:112
  961.3 24.8 %collective-permute-start.73 = (f32[2,12288]{1,0:T(2,128)S(1)}, f32[2,12288]{1,0:T(2,128)S(1)}, u32[]{:S(2)}, u32[]{:S(2)}) collective-permute-start(f32[2,12288]{1,0:T(2,128)S(1)} %maximum_maximum_fusion.3), channel_id=1, source_target_pairs={{0,16},{16,0},{1,17},{17,1},{2,18},{18,2},{3,19},{19,3},{4,20},{20... | collective-permute-start | bytes 294920 | tf_op jit(solution)/shard_map/ppermute | solution.py:87
  963.4 31.3 %collective-permute-start.58 = (bf16[256,2048]{1,0:T(8,128)(2,1)}, bf16[256,2048]{1,0:T(8,128)(2,1)}, u32[]{:S(2)}, u32[]{:S(2)}) collective-permute-start(bf16[256,2048]{1,0:T(8,128)(2,1)} %broadcast_select_fusion.2), channel_id=1, source_target_pairs={{0,16},{16,0},{1,17},{17,1},{2,18},{18,2},{3,19},{19,3},{4,20},{20... | collective-permute-start | bytes 3145736 | tf_op jit(solution)/shard_map/ppermute | solution.py:92
  963.4 40.1 %collective-permute-start.65 = (f32[256,2048]{1,0:T(8,128)}, f32[256,2048]{1,0:T(8,128)}, u32[]{:S(2)}, u32[]{:S(2)}) collective-permute-start(f32[256,2048]{1,0:T(8,128)} %get-tuple-element.463), channel_id=1, source_target_pairs={{0,16},{16,0},{1,17},{17,1},{2,18},{18,2},{3,19},{19,3},{4,20},{20... | collective-permute-start | bytes 6291464 | tf_op jit(solution)/shard_map/ppermute | solution.py:92
  984.6 25.5 %collective-permute-start.68 = (bf16[512,2048]{1,0:T(8,128)(2,1)}, bf16[512,2048]{1,0:T(8,128)(2,1)S(1)}, u32[]{:S(2)}, u32[]{:S(2)}) collective-permute-start(bf16[512,2048]{1,0:T(8,128)(2,1)} %reduce-scatter.14.cloned.1.call-done.refs_0_), channel_id=1, source_target_pairs={{16,0},{17,1},{18,2},{19,3},{20,4},{21,5},{22,6},{23,7},{24,8},{25... | collective-permute-start | bytes 6291464 | tf_op jit(solution)/shard_map/ppermute | solution.py:1210
  987.4 40.6 %collective-permute-start.70 = (bf16[512,1024]{1,0:T(8,128)(2,1)}, bf16[512,1024]{1,0:T(8,128)(2,1)}, u32[]{:S(2)}, u32[]{:S(2)}) collective-permute-start(bf16[512,1024]{1,0:T(8,128)(2,1)} %reduce-scatter.8.cloned.1.call-done.refs_3_), channel_id=1, source_target_pairs={{0,16},{1,17},{2,18},{3,19},{4,20},{5,21},{6,22},{7,23},{8,24},{9,... | collective-permute-start | bytes 3145736 | tf_op jit(solution)/shard_map/ppermute | solution.py:1211
  991.6 18.5 %collective-permute-start.69 = (bf16[512,1024]{1,0:T(8,128)(2,1)S(1)}, bf16[512,1024]{1,0:T(8,128)(2,1)}, u32[]{:S(2)}, u32[]{:S(2)}) collective-permute-start(bf16[512,1024]{1,0:T(8,128)(2,1)S(1)} %copy-done.5), channel_id=1, source_target_pairs={{0,16},{1,17},{2,18},{3,19},{4,20},{5,21},{6,22},{7,23},{8,24},{9,... | collective-permute-start | bytes 3145736 | tf_op jit(solution)/shard_map/ppermute | solution.py:1211
  (107 other events, 1272.8 us)
Sparse Core Ops, SparseCore 0:
  14.7 67.7 all-gather.5
  84.6 165.5 all-gather.7
  251.9 147.9 all-gather.9
  401.9 78.9 all-gather.11
  500.8 75.2 reduce-scatter.5
  578.9 77.2 reduce-scatter.7
  658.5 77.2 reduce-scatter.9
  756.6 75.9 reduce-scatter.11
  840.7 143.8 reduce-scatter.13

commit v2 on v1

--- a/solution.py
+++ b/solution.py
@@ -251,6 +251,10 @@
 SCALE = HEAD_DIM ** (-0.5)
 
 
+def work(flops):
+    return pl.CostEstimate(flops=4 * flops, transcendentals=0, bytes_accessed=flops // 256)
+
+
 def call(body, grid, in_specs, out_specs, out_shape, info, args, scratch=(), cost=CHEAP):
     return pl.pallas_call(
         body,
@@ -285,6 +289,10 @@
     return pl.BlockSpec(
         (width, columns), lambda i, info: (0, at), pipeline_mode=pl.Buffered(buffer_count=1)
     )
+
+
+def held_pieces(width, columns, start, size):
+    return [held(width, size, start // size + piece) for piece in range(columns // size)]
 
 
 def row_stats(rows):
@@ -454,15 +462,15 @@
 
 
 def heads_body(
-    steps, info, x_ref, w_ref, cos_ref, low_ref, high_ref, out_ref, qkv_ref, lse_ref, k_ref, v_ref
+    steps, info, x_ref, wq_ref, wk_ref, wv_ref, cos_ref, low_ref, high_ref, out_ref, qkv_ref, lse_ref, k_ref, v_ref
 ):
     step = pl.program_id(0)
     rows = x_ref.shape[0]
     tables = (cos_ref[...], low_ref[...], high_ref[...])
-    mixed = dot(x_ref[...], w_ref[...])
-    query = turned(mixed[:, :HEAD_DIM], tables, 1.0).astype(jnp.bfloat16)
-    keys = turned(mixed[:, HEAD_DIM : 2 * HEAD_DIM], tables, 1.0).astype(jnp.bfloat16)
-    values = mixed[:, 2 * HEAD_DIM :].astype(jnp.bfloat16)
+    rows_here = x_ref[...]
+    query = turned(dot(rows_here, wq_ref[...]), tables, 1.0).astype(jnp.bfloat16)
+    keys = turned(dot(rows_here, wk_ref[...]), tables, 1.0).astype(jnp.bfloat16)
+    values = dot(rows_here, wv_ref[...]).astype(jnp.bfloat16)
     qkv_ref[:, :HEAD_DIM] = query
     qkv_ref[:, HEAD_DIM : 2 * HEAD_DIM] = keys
     qkv_ref[:, 2 * HEAD_DIM :] = values
@@ -496,17 +504,11 @@
     out, qkv, lse = call(
         functools.partial(heads_body, steps),
         (steps,),
-        [
-            tall(width),
-            pl.BlockSpec(
-                (width, columns), lambda i, info: (0, 0), pipeline_mode=pl.Buffered(buffer_count=1)
-            ),
-        ]
-        + [tall(128)] * 3,
+        [tall(width)] + [held(width, HEAD_DIM, part) for part in range(3)] + [tall(128)] * 3,
         [tall(HEAD_DIM), tall(columns), tall(1)],
         [low_shape(slots, HEAD_DIM), low_shape(slots, columns), full_shape(slots, 1)],
         info,
-        (first_in, inward, *tables),
+        (first_in, inward, inward, inward, *tables),
         [pltpu.VMEM((slots, HEAD_DIM), jnp.bfloat16)] * 2,
     )
     return (out, (qkv, lse))
@@ -557,7 +559,7 @@
         out_ref[:, 2 * HEAD_DIM :] = dv_ref[...].astype(jnp.bfloat16)
 
 
-def heads_back_call(saved, out_grad, tables, info):
+def heads_back_call(saved, out_grad, tables, info, cost=CHEAP):
     qkv, lse = saved
     slots, columns = qkv.shape
     rows = min(slots, 256)
@@ -576,15 +578,16 @@
         info,
         (qkv, lse, out_grad, *tables),
         [pltpu.VMEM((slots, HEAD_DIM), jnp.float32)] * 2,
-    )
-
-
-def units_body(info, x_ref, w_ref, offset_ref, act_ref, slope_ref):
-    columns = w_ref.shape[1]
-    size = min(columns, 512)
-    for start in range(0, columns, size):
-        here = slice(start, start + size)
-        hidden = dot(x_ref[...], w_ref[:, here]) + offset_ref[:, here]
+        cost,
+    )
+
+
+def units_body(pieces, info, x_ref, *refs):
+    weights, (offset_ref, act_ref, slope_ref) = refs[:pieces], refs[pieces:]
+    size = weights[0].shape[1]
+    for piece in range(pieces):
+        here = slice(piece * size, (piece + 1) * size)
+        hidden = dot(x_ref[...], weights[piece][...]) + offset_ref[:, here]
         cdf = 0.5 * (1.0 + lax.erf(hidden * 0.7071067811865476))
         act_ref[:, here] = (hidden * cdf).astype(jnp.bfloat16)
         bell = jnp.exp(-0.5 * hidden * hidden) * 0.3989422804014327
@@ -596,18 +599,15 @@
     columns = offsets.shape[0]
     tall = min(slots, 256)
     spec = pl.BlockSpec((tall, columns), lambda i, info: (i, 0))
+    weights = held_pieces(width, columns, start * unit, unit)
     return call(
-        units_body,
+        functools.partial(units_body, len(weights)),
         (slots // tall,),
-        [
-            pl.BlockSpec((tall, width), lambda i, info: (i, 0)),
-            held(width, columns, start * unit // columns),
-            fixed((1, columns)),
-        ],
+        [pl.BlockSpec((tall, width), lambda i, info: (i, 0))] + weights + [fixed((1, columns))],
         [spec, spec],
         [low_shape(slots, columns)] * 2,
         info,
-        (second_in, expand, offsets[None]),
+        (second_in, *[expand] * len(weights), offsets[None]),
     )
 
 
@@ -627,127 +627,138 @@
                 outs[stream * (half + 1) + place][...] = rows
 
 
-def partial_body(half, tall, info, *refs):
-    value = None
-    for left, right in zip(refs[:4], refs[4:8]):
-        term = dot_nt(left[...], right[...])
-        value = term if value is None else value + term
-    outs, value_ref = refs[8:-1], refs[-1]
-    value_ref[...] = value.astype(jnp.bfloat16)
+def partial_body(half, tall, parts, info, *refs):
+    lefts, rights = [refs[k * parts : (k + 1) * parts] for k in range(4)], refs[4 * parts :][:4]
+    outs, value_ref = refs[4 * parts + 4 : -1], refs[-1]
+    rows = lefts[0][0].shape[0]
+    for part in range(parts):
+        value = None
+        for left, right in zip(lefts, rights):
+            term = dot_nt(left[part][...], right[...])
+            value = term if value is None else value + term
+        value_ref[part * rows : (part + 1) * rows] = value.astype(jnp.bfloat16)
     if half:
         place_rows(info, value_ref, outs, half, tall)
     else:
         outs[0][...] = value_ref[...]
 
 
-def partial_call(heads, acts, outward, contract, outward_at, contract_at, places):
+def partial_call(heads, acts, outward, contract, outward_at, contract_at, places, cost=CHEAP):
     slots, unit = heads[0].shape
     wide = acts[0].shape[1]
     width = outward[0].shape[0]
     block = min(width, 512)
+    parts = max(slots // 256, 1)
+    rows = slots // parts
     half = len(places) // 4
     tall = slots // (4 * half) if half else 0
     heights = halving_blocks(half, tall) if half else [slots]
     info = jnp.stack([jnp.asarray(item, jnp.int32) for item in (places or [0])])
+
+    def row_blocks(columns):
+        return [
+            pl.BlockSpec(
+                (rows, columns),
+                lambda j, info, part=part: (part, 0),
+                pipeline_mode=pl.Buffered(buffer_count=1),
+            )
+            for part in range(parts)
+        ]
+
     return call(
-        functools.partial(partial_body, half, tall),
+        functools.partial(partial_body, half, tall, parts),
         (width // block,),
-        [fixed(item.shape) for item in (*heads, *acts)]
+        row_blocks(unit) * 2
+        + row_blocks(wide) * 2
         + [pl.BlockSpec((block, unit), lambda j, info: (j, outward_at))] * 2
         + [pl.BlockSpec((block, wide), lambda j, info: (j, contract_at * unit // wide))] * 2,
         [pl.BlockSpec((height, block), lambda j, info: (0, j)) for height in heights],
         [low_shape(height, width) for height in heights],
         info,
-        (*heads, *acts, *outward, *contract),
+        [item for item in (*heads, *acts) for part in range(parts)] + [*outward, *contract],
         [pltpu.VMEM((slots, block), jnp.bfloat16)],
-    )
-
-
-PIECES = 4
-
-
-def grads_body(count, split, info, *refs):
-    lefts, rights, rest = refs[:count], refs[count : 2 * count], refs[2 * count :]
-    got, outs = ((), rest) if split else (rest[:PIECES], rest[PIECES:])
-    size = (outs[0].shape[1]) if split else got[0].shape[1]
-    start = 0
-    for left, right in zip(lefts, rights):
-        value = dot(left[...], right[...])
-        for piece in range(PIECES):
-            low = max(start, piece * size)
-            high = min(start + right.shape[1], (piece + 1) * size)
-            if low >= high:
-                continue
-            term = value[:, low - start : high - start]
-            inner = slice(low - piece * size, high - piece * size)
-            if split:
-                outs[piece][:, inner] = term.astype(jnp.bfloat16)
-            else:
-                term = term + got[piece][:, inner].astype(jnp.float32)
-                outs[0][:, low:high] = term.astype(jnp.bfloat16)
-        start = start + right.shape[1]
-
-
-def grads_call(lefts, rights, info, got=None, cost=CHEAP):
+        cost,
+    )
+
+
+def grads_body(plan, split, info, *refs):
+    lefts = refs[: max(plan) + 1]
+    rights = refs[len(lefts) : len(lefts) + len(plan)]
+    rest = refs[len(lefts) + len(plan) :]
+    got, outs = ((), rest) if split else (rest[:-1], rest[-1:])
+    size = rights[0].shape[1]
+    for place, right in enumerate(rights):
+        value = dot(lefts[plan[place]][...], right[...])
+        if split:
+            outs[place][...] = value.astype(jnp.bfloat16)
+        else:
+            value = value + got[place][...].astype(jnp.float32)
+            outs[0][:, place * size : (place + 1) * size] = value.astype(jnp.bfloat16)
+
+
+def grads_call(lefts, rights, size, info, got=None, cost=CHEAP):
     width, slots = lefts[0].shape
     columns = sum(item.shape[1] for item in rights)
     block = min(width, 256)
     split = got is None
     spec = pl.BlockSpec((block, columns), lambda j, info: (j, 0))
-    piece_specs = [pl.BlockSpec((block, columns // PIECES), lambda j, info: (j, 0))] * PIECES
-    out = call(
-        functools.partial(grads_body, len(lefts), split),
+    pieces = columns // size
+    piece_specs = [pl.BlockSpec((block, size), lambda j, info: (j, 0))] * pieces
+    plan, specs, args = [], [], []
+    for which, right in enumerate(rights):
+        for piece in held_pieces(slots, right.shape[1], 0, size):
+            plan.append(which)
+            specs.append(piece)
+            args.append(right)
+    return call(
+        functools.partial(grads_body, plan, split),
         (width // block,),
         [pl.BlockSpec((block, slots), lambda j, info: (j, 0))] * len(lefts)
-        + [fixed(item.shape) for item in rights]
+        + specs
         + ([] if split else piece_specs),
         piece_specs if split else spec,
-        [low_shape(width, columns // PIECES)] * PIECES if split else low_shape(width, columns),
+        [low_shape(width, size)] * pieces if split else low_shape(width, columns),
         info,
-        (*lefts, *rights, *(got or ())),
+        (*lefts, *args, *(got or ())),
         cost=cost,
     )
-    return out
-
-
-def lifted_body(info, g_ref, outward_ref, contract_ref, slope_ref, out_ref, hidden_ref, sum_ref):
-    columns = contract_ref.shape[1]
-    size = min(columns, 512)
+
+
+def lifted_body(pieces, info, g_ref, outward_ref, *refs):
+    weights, (slope_ref, out_ref, hidden_ref, sum_ref) = refs[:pieces], refs[pieces:]
+    size = weights[0].shape[1]
 
     @pl.when(pl.program_id(0) == 0)
     def _():
         sum_ref[...] = jnp.zeros_like(sum_ref)
 
-    for start in range(0, columns, size):
-        here = slice(start, start + size)
-        value = dot(g_ref[...], contract_ref[:, here]) * slope_ref[:, here].astype(jnp.float32)
+    for piece in range(pieces):
+        here = slice(piece * size, (piece + 1) * size)
+        value = dot(g_ref[...], weights[piece][...]) * slope_ref[:, here].astype(jnp.float32)
         value = value.astype(jnp.bfloat16)
         hidden_ref[:, here] = value
         sum_ref[:, here] += jnp.sum(value.astype(jnp.float32), axis=0, keepdims=True)
     out_ref[...] = dot(g_ref[...], outward_ref[...]).astype(jnp.bfloat16)
 
 
-def lifted_call(grad, outward, contract, outward_at, contract_at, slope, unit, info):
+def lifted_call(grad, outward, contract, outward_at, contract_at, slope, unit, info, cost=CHEAP):
     slots, width = grad.shape
     columns = slope.shape[1]
     tall = min(slots, 256)
+    weights = held_pieces(width, columns, contract_at * unit, unit)
 
     def rows(size):
         return pl.BlockSpec((tall, size), lambda i, info: (i, 0))
 
     return call(
-        lifted_body,
+        functools.partial(lifted_body, len(weights)),
         (slots // tall,),
-        [
-            rows(width),
-            held(width, unit, outward_at),
-            held(width, columns, contract_at * unit // columns),
-            rows(columns),
-        ],
+        [rows(width), held(width, unit, outward_at)] + weights + [rows(columns)],
         [rows(unit), rows(columns), pl.BlockSpec((1, columns), lambda i, info: (0, 0))],
         [low_shape(slots, unit), low_shape(slots, columns), full_shape(1, columns)],
         info,
-        (grad, outward, contract, slope),
+        (grad, outward, *[contract] * len(weights), slope),
+        cost=cost,
     )
 
 
@@ -891,7 +902,7 @@
 def adam_columns(index, grads, arrays, depth, starts, core):
     parts, _, columns = arrays[0].shape
     half = columns // 2
-    tall = depth // 4
+    tall = depth // 2
 
     def arrange(run):
         for which in (0, 1):
@@ -912,7 +923,7 @@
     )
 
 
-def adam_rows(index, grads, arrays, starts, block, core):
+def adam_rows(index, grads, arrays, starts, block, core, cost=CHEAP):
     units, depth = arrays[0].shape
     each = units // 2 // block
 
@@ -938,6 +949,7 @@
         [jax.ShapeDtypeStruct(arrays[0].shape, jnp.float32)] * 3,
         core,
         (*grads, *arrays),
+        cost=cost,
     )
 
 
@@ -1044,12 +1056,12 @@
         out, saved = attend(mixed, length, tables)
         return (list(halves(out, core)), saved)
 
-    def heads_back(out_grads, saved):
+    def heads_back(which, out_grads, saved, cost=CHEAP):
         if lone:
-            return [heads_back_call(kept, grad, turns, info) for grad, kept in zip(out_grads, saved)]
+            return heads_back_call(saved[which], out_grads[which], turns, info, cost)
         grad = ordered(out_grads[0], out_grads[1], core)
         mixed_grad = attend_back(grad, saved, length, tables).reshape(slots, 3, -1)
-        return [item.reshape(slots, -1) for item in halves(mixed_grad, core)]
+        return halves(mixed_grad, core)[which].reshape(slots, -1)
 
     def units_of(second_in, expand_pair, start, layer):
         done = [
@@ -1060,9 +1072,16 @@
         ]
         return ([item[0] for item in done], [item[1] for item in done])
 
-    def layer_output(layer, outward_pair, contract_pair, heads, acts):
+    def layer_output(layer, outward_pair, contract_pair, heads, acts, cost=CHEAP):
         pieces = partial_call(
-            heads, acts, outward_pair, contract_pair, outward_at[layer], contract_at[layer], places
+            heads,
+            acts,
+            outward_pair,
+            contract_pair,
+            outward_at[layer],
+            contract_at[layer],
+            places,
+            cost,
         )
         block = summed(pieces) + block_of(inputs[layer]) + vector_values[layer][4]
         return block.astype(jnp.bfloat16)
@@ -1102,19 +1121,18 @@
     for layer in (1, 0):
         if layer == 0:
             normed, heads, saved, acts, slopes = kept[0]
-        theirs = grads_call([grad_turned], [acts[1]], info)
+        dense = 2 * slots * width * unit_share
+        theirs = grads_call([grad_turned], [acts[1]], head_share, info)
         if layer == 1:
-            heads, saved = heads_of(after(first_in, *theirs), rest_pair)
-            theirs = [after(after(item, acts[0], *heads), wholes[3]) for item in theirs]
+            mine = grads_call([grad_turned], [acts[0]], head_share, info)
+            heads, saved = heads_of(after(first_in, *theirs, *mine), rest_pair)
+            theirs = [after(after(item, *mine, *heads), wholes[3]) for item in theirs]
+            contract_pairs.append(pair_of(wholes[3], *theirs))
         got = [swap(item) for item in theirs]
-        contract_total = grads_call([grad_turned], [acts[0]], info, got)
-        contract_share = share_of(contract_total)
-        if layer == 1:
-            contract_pairs.append(pair_of(wholes[3], *theirs))
-        grad_here = after(grad_low, contract_total)
-        lifted = [
-            lifted_call(
-                grad_here,
+
+        def lift(which, grad, cost=CHEAP):
+            return lifted_call(
+                grad,
                 outward_pairs[layer][which],
                 contract_pairs[layer][which],
                 outward_at[layer],
@@ -1122,35 +1140,58 @@
                 slopes[which],
                 head_share,
                 info,
+                cost,
             )
-            for which in (0, 1)
-        ]
+
+        def total_of(lefts, theirs, mine, cost=CHEAP, between=None):
+            got = [swap(item) for item in grads_call(lefts, theirs, head_share, info, cost=cost)]
+            if between is not None:
+                mine = [after(mine[0], between), *mine[1:]]
+            return grads_call(lefts, mine, head_share, info, got, cost)
+
+        lifted = [lift(0, after(grad_low, *theirs), work(dense))]
+        if layer == 1:
+            mine = [after(item, lifted[0][1]) for item in mine]
+            contract_total = jnp.concatenate(
+                [
+                    (own.astype(jnp.float32) + item.astype(jnp.float32)).astype(jnp.bfloat16)
+                    for own, item in zip(mine, got)
+                ],
+                axis=1,
+            )
+        else:
+            contract_total = grads_call(
+                [grad_turned], [after(acts[0], lifted[0][1])], head_share, info, got
+            )
+        contract_share = share_of(contract_total)
+        lifted.append(lift(1, after(grad_low, contract_total)))
+        out_grads = [item[0] for item in lifted]
         hidden_grads = [item[1] for item in lifted]
         offset_grads[layer] = [item[2][0] for item in lifted]
         first_turned, second_turned = normed[4:]
-
-        def total_of(lefts, theirs, mine, cost=CHEAP):
-            got = [swap(item) for item in grads_call(lefts, theirs, info, cost=cost)]
-            return grads_call(lefts, mine, info, got, cost)
-
-        out_grads = [item[0] for item in lifted]
+        lefts = [first_turned, grad_turned]
+        small_work = work(dense // 2)
         if layer == 1:
-            expand_total = total_of([second_turned], [hidden_grads[1]], [hidden_grads[0]])
+            mixed_first = heads_back(0, out_grads, saved, small_work)
+            expand_total = total_of(
+                [second_turned], [hidden_grads[1]], [hidden_grads[0]], between=mixed_first
+            )
             expand_share = share_of(expand_total)
             out_grads = [after(item, expand_total) for item in out_grads]
-        mixed_grads = heads_back(out_grads, saved)
-        lefts = [first_turned, grad_turned]
-        rights = [[mixed_grads[which], heads[which]] for which in (1, 0)]
-        if layer == 0:
-            hidden_here = [after(item, *shares[1], *mixed_grads) for item in hidden_grads]
+            mixed_grads = [mixed_first, heads_back(1, out_grads, saved)]
+            ahead = [contract_share, *mixed_grads]
+        else:
+            mixed_last = heads_back(1, out_grads, saved)
+            mixed_first = heads_back(0, out_grads, saved, small_work)
+            mixed_grads = [mixed_first, mixed_last]
+            hidden_here = [after(item, *shares[1]) for item in hidden_grads]
             other_total = total_of(
-                [second_turned] + lefts,
-                [hidden_here[1]] + rights[0],
-                [hidden_here[0]] + rights[1],
+                [second_turned, first_turned],
+                [hidden_here[1], mixed_last],
+                [hidden_here[0], mixed_first],
+                between=mixed_first,
             )
             ahead = [other_total]
-        else:
-            ahead = [contract_share, *mixed_grads]
         pieces, norm_part = back_call(
             after(inputs[layer], *ahead),
             normed[2:4],
@@ -1164,16 +1205,21 @@
             peers,
             bits,
         )
+        rights = [[mixed_grads[which], heads[which]] for which in (1, 0)]
         if layer == 1:
             lefts[0] = after(lefts[0], *pieces)
-            flops = 8 * slots * width * head_share
-            cost = pl.CostEstimate(
-                flops=4 * flops, transcendentals=0, bytes_accessed=4 * flops // slots
+            shares[1] = (share_of(total_of(lefts, *rights, work(dense))), expand_share, contract_share)
+        else:
+            outward_total = total_of(
+                [after(grad_turned, other_total)], [rights[0][1]], [rights[1][1]]
             )
-            shares[1] = (share_of(total_of(lefts, *rights, cost)), expand_share, contract_share)
-        else:
+            pairs = [
+                [after(item, outward_total) for item in pair]
+                for pair in (outward_pairs[1], contract_pairs[1])
+            ]
             pieces = [after(item, contract_share) for item in pieces]
-            shares[0] = (share_of(other_total), contract_share)
+            shares[0] = (share_of(other_total), share_of(outward_total), contract_share)
+            results.append(layer_output(1, *pairs, *last))
         upstream = block_of(grad_low)
         vector_grads[layer] = jnp.concatenate(
             [norm_part, jnp.sum(upstream, axis=0)[None]], axis=0
@@ -1189,12 +1235,6 @@
                 grad_low = lax.all_gather(block, "tensor", axis=0, tiled=True)
                 grad_turned = grad_low.T
             last = (heads, acts)
-        else:
-            pairs = [
-                [after(item, other_total) for item in pair]
-                for pair in (outward_pairs[1], contract_pairs[1])
-            ]
-            results.append(layer_output(1, *pairs, *last))
 
     activations = jnp.where(core == 0, results[0], results[1])
     got = swap(jnp.where(core == 0, results[1], results[0]))
@@ -1205,11 +1245,8 @@
     got = swap(jnp.where(core == 0, row_grads[1], row_grads[0]))
     gradients = jnp.where(core == 0, jnp.stack([gradients, got]), jnp.stack([got, gradients]))[None]
 
-    def to_owner(first, second, *earlier):
-        first = after(first, *earlier)
-        from_first = lax.ppermute(first, "pipe", [(1, 0)])
-        from_second = lax.ppermute(second, "pipe", [(0, 1)])
-        return (first, from_first, from_second, second)
+    def to_owner(first, second):
+        return (first, swap(first), swap(second), second)
 
     vector_sum = added(jnp.stack(vector_grads), "tensor")
     offset_sum = jnp.stack([ordered(item[0], item[1], core) for item in offset_grads])
@@ -1232,38 +1269,46 @@
         return [item[0].transpose(1, 0, 2) for item in arrays]
 
     which = core[None]
+    expand_1, heads_1 = swap(shares[1][1]), swap(shares[1][0])
     contract_out = adam_rows(
         3,
-        to_owner(shares[0][1], shares[1][2]),
+        to_owner(shares[0][2], shares[1][2]),
         viewed(contract, contract_first, contract_second),
         (0, 0),
         head_share,
         which,
     )
-    last_share = after(shares[0][0], contract_out[0])
+    vectors_out = adam_update(
+        vectors, vector_grad[None], vectors_first, vectors_second, RATES[4], DECAYS[4]
+    )
+    offsets_out = adam_update(
+        offsets, offset_grad[None], offsets_first, offsets_second, RATES[5], DECAYS[5]
+    )
+    other_share = after(shares[0][0], contract_out[0])
+    other_0 = swap(other_share)
     expand_out = adam_columns(
         2,
-        to_owner(last_share, shares[1][1]),
+        (other_share, other_0, expand_1, shares[1][1]),
         [expand, expand_first, expand_second],
         depth,
         (0, 0),
         which,
     )
-    heads_grads = to_owner(last_share, shares[1][0])
-    outward_out = adam_rows(
-        1,
-        heads_grads,
-        viewed(outward, outward_first, outward_second),
-        (count + 3, 3),
-        head_share,
-        which,
-    )
     inward_out = adam_columns(
         0,
-        heads_grads,
+        (other_share, other_0, heads_1, shares[1][0]),
         parts_first(inward, inward_first, inward_second),
         depth,
         (count, 0),
+        which,
+    )
+    outward_share = after(shares[0][1], expand_out[0], inward_out[0])
+    outward_out = adam_rows(
+        1,
+        (outward_share, swap(outward_share), heads_1, shares[1][0]),
+        viewed(outward, outward_first, outward_second),
+        (0, 3),
+        head_share,
         which,
     )
     outputs = [activations, gradients]
@@ -1271,12 +1316,8 @@
     outputs.extend([item[None] for item in outward_out])
     outputs.extend(expand_out)
     outputs.extend([item[None] for item in contract_out])
-    outputs.extend(
-        adam_update(vectors, vector_grad[None], vectors_first, vectors_second, RATES[4], DECAYS[4])
-    )
-    outputs.extend(
-        adam_update(offsets, offset_grad[None], offsets_first, offsets_second, RATES[5], DECAYS[5])
-    )
+    outputs.extend(vectors_out)
+    outputs.extend(offsets_out)
     return tuple(outputs)
 
 

time: 1050 us -> 1050 us (level)
  starting transfers between devices: 64.8 us -> 50.5 us
    ppermute x30 -> x40, waiting for transfers between devices: 43.4 us -> 24.6 us  [swap(): return lax.ppermute(array, 'pipe', [(0, 1), (1, 0)])]
    ppermute x5 -> x0, starting transfers between devices: 11.9 us -> none  [the longest x3 9.17 us: to_owner(): from_second = lax.ppermute(second, 'pipe', [(0, 1)])]
    ppermute x5, waiting for transfers between devices: 3.87 us -> 15.8 us  [added(): lax.ppermute(array, axis, [(i, i ^ 1 << bit) for i in range(peers)])]
    pallas_call x38 -> x40, Pallas kernels: 465 us -> 473 us  [call(): pl.pallas_call(body, grid_spec=pltpu.PrefetchScalarGridSpec(num_scalar_pr...]
    unnamed x156 -> x190, local copies, waits for them, and re-layouts: 20.6 us -> 24.8 us
  transfers between devices with their start and end apart: 85 -> 91, of which waited for: 55 -> 48; matrix products, arithmetic and copies ran while one was open for 7% -> 7% of each run, Pallas kernels for 42% -> 45%
where the time goes in v2:
time: 1050 us; the launch traced here: 1040 us
  Pallas kernels  473 us (45%)
  waiting for transfers between devices  374 us (36%)
  other arithmetic  62.7 us (6%)
  starting transfers between devices  50.5 us (5%)
  local copies, waits for them, and re-layouts  41.7 us (4%)
  blocking collectives  26.9 us (3%)
  between operations  16.1 us (2%)
    pallas_call x40, Pallas kernels, call(): pl.pallas_call(body, grid_spec=pltpu.PrefetchScalarGridSpec(num_scalar_pr...  473 us
    ppermute x36, waiting for transfers between devices, flipped(): lax.ppermute(array, 'tensor', [(i, i ^ 1 << bit) for i in range(peers)])  161 us
    all_gather x4, waiting for transfers between devices, whole_of(): return lax.all_gather(shard, 'dp', axis=0, tiled=True)  159 us
    ppermute x36, starting transfers between devices, flipped(): lax.ppermute(array, 'tensor', [(i, i ^ 1 << bit) for i in range(peers)])  35.4 us
    all_gather x1, blocking collectives, local(): lax.all_gather(small, ('pipe', 'dp'), axis=0, tiled=False)  26.9 us
    unnamed x190, local copies, waits for them, and re-layouts  24.8 us
    ppermute x40, waiting for transfers between devices, swap(): return lax.ppermute(array, 'pipe', [(0, 1), (1, 0)])  24.6 us
  transfers between devices with their start and end apart: 91, of which 48 were waited for; matrix products, arithmetic and copies ran while one was open for 7% of the time, Pallas kernels for 45%

profile of v2, /device:TPU:0, one launch (start us, length us, event | category | flops | bytes accessed | tf_op | source)
XLA Modules:
  0.0 1044.6 jit_solution(4992010204619749076)
XLA Ops:
  41.5 26.9 %all-gather = bf16[8,1,3072]{2,1,0:T(2,128)(2,1)S(1)} all-gather(bf16[1,1,3072]{2,1,0:T(2,128)(2,1)S(1)} %maximum_bitcast_fusion.2), channel_id=1, replica_groups=mesh['pipe'=2,'tensor'=4,'dp'=4] {'pipe','dp'}, dimensions={0}, use_global_device_ids=true | all-gather | bytes 55296 | tf_op jit(solution)/shard_map/all_gather | solution.py:1012
  74.2 10.5 %shard_map.356 = (bf16[1024,2048]{1,0:T(8,128)(2,1)}, bf16[1024,2048]{1,0:T(8,128)(2,1)}, f32[1024,1]{1,0:T(8,128)}, f32[1024,1]{1,0:T(8,128)}, bf16[2048,1024]{1,0:T(8,128)(2,1)}, /*index=5*/bf16[2048,1024]{1,0:T(8,128)(2,1)}) custom-call(s32[1]{0:T(128)} %dynamic_slice.109.info, bf16[1024,2048]{1,0:T(8,128)(2,1)} %constant_dynamic-slice_fusion.6.z_ref.refs_0_, ...), custom_call_target="tpu_custom_call" | custom-call | flops 1 | bytes 1 | tf_op jit(solution)/shard_map/pallas_call | solution.py:259
  89.5 12.3 %shard_map.358 = (bf16[1024,256]{1,0:T(8,128)(2,1)}, bf16[1024,768]{1,0:T(8,128)(2,1)}, f32[1024,1]{1,0:T(8,128)}) custom-call(s32[1]{0:T(128)} %dynamic_slice.109.info, bf16[1024,2048]{1,0:T(8,128)(2,1)} %get-tuple-element.224.x_ref, bf16[2048,768]{1,0:T(8,128)(2,1)} %all-gather.6.cloned.1.call-done.wq_ref.wk_ref.wv_ref.refs_8_, ...), custom_call_target="tpu_custom_call" | custom-call | flops 1 | bytes 1 | tf_op jit(solution)/shard_map/pallas_call | solution.py:259
  103.5 11.6 %shard_map.359 = (bf16[1024,256]{1,0:T(8,128)(2,1)}, bf16[1024,768]{1,0:T(8,128)(2,1)}, f32[1024,1]{1,0:T(8,128)}) custom-call(s32[1]{0:T(128)} %dynamic_slice.109.info, bf16[1024,2048]{1,0:T(8,128)(2,1)} %get-tuple-element.224.x_ref, bf16[2048,768]{1,0:T(8,128)(2,1)} %copy-done.1, bf16[2048,768]{1,0:T(8,128)(2,1)} %copy-done.1, ...), custom_call_target="tpu_custom_call" | custom-call | flops 1 | bytes 1 | tf_op jit(solution)/shard_map/pallas_call | solution.py:259
  115.1 135.0 %all-gather.8.cloned.1.call-done.refs_0_.refs_1_.refs_2_.refs_3_.refs_16_.refs_18_.outward_ref.refs_10_ = bf16[2048,2304]{1,0:T(8,128)(2,1)} async-done(((bf16[512,2304]{1,0:T(8,128)(2,1)}), bf16[2048,2304]{1,0:T(8,128)(2,1)}) %all-gather.8.cloned.1.call-update) | async-done | bytes 9437200 | tf_op jit(solution)/shard_map/all_gather | solution.py:1029
  253.6 10.9 %shard_map.360 = (bf16[1024,1024]{1,0:T(8,128)(2,1)}, bf16[1024,1024]{1,0:T(8,128)(2,1)}) custom-call(s32[1]{0:T(128)} %dynamic_slice.109.info, bf16[1024,2048]{1,0:T(8,128)(2,1)} %get-tuple-element.225.x_ref, bf16[2048,2304]{1,0:T(8,128)(2,1)} %all-gather.8.cloned.1.call-done.refs_0_.refs_1_.refs_2_.refs_3_.refs_16_.refs_18_.outward_ref.refs_10_, ...), custom_call_target="tpu_custom_call" | custom-call | flops 1 | bytes 1 | tf_op jit(solution)/shard_map/pallas_call | solution.py:259
  265.2 10.7 %shard_map.361 = (bf16[1024,1024]{1,0:T(8,128)(2,1)}, bf16[1024,1024]{1,0:T(8,128)(2,1)}) custom-call(s32[1]{0:T(128)} %dynamic_slice.109.info, bf16[1024,2048]{1,0:T(8,128)(2,1)} %get-tuple-element.225.x_ref, bf16[2048,2304]{1,0:T(8,128)(2,1)} %collective-permute-done.5.refs_0_.refs_1_.refs_2_.refs_3_.refs_17_.refs_19_.outward_ref.refs_11_, ...), custom_call_target="tpu_custom_call" | custom-call | flops 1 | bytes 1 | tf_op jit(solution)/shard_map/pallas_call | solution.py:259
  275.9 17.2 %shard_map.362 = (bf16[128,2048]{1,0:T(8,128)(2,1)}, bf16[128,2048]{1,0:T(8,128)(2,1)}, bf16[256,2048]{1,0:T(8,128)(2,1)}, bf16[128,2048]{1,0:T(8,128)(2,1)}, bf...) custom-call(s32[8]{0:T(128)} %stack.259.info, bf16[1024,256]{1,0:T(8,128)(2,1)} %get-tuple-element.228.refs_0_.refs_1_.refs_2_.refs_3_, ...), custom_call_target="tpu_custom_call" | custom-call | flops 1 | bytes 1 | tf_op jit(solution)/shard_map/pallas_call | solution.py:259
  297.2 10.9 %collective-permute-done.6 = bf16[128,2048]{1,0:T(8,128)(2,1)S(1)} collective-permute-done((bf16[128,2048]{1,0:T(8,128)(2,1)}, bf16[128,2048]{1,0:T(8,128)(2,1)S(1)}, u32[]{:S(2)}, u32[]{:S(2)}) %collective-permute-start.6) | collective-permute-done | bytes 524320 | tf_op jit(solution)/shard_map/ppermute | solution.py:112
  308.1 10.4 collective-permute-done.7
  327.1 9.3 collective-permute-done.10
  346.6 10.8 %collective-permute-done.13.refs_5_ = bf16[128,2048]{1,0:T(8,128)(2,1)S(1)} collective-permute-done((bf16[128,2048]{1,0:T(8,128)(2,1)S(1)}, bf16[128,2048]{1,0:T(8,128)(2,1)S(1)}, u32[]{:S(2)}, u32[]{:S(2)}) %collective-permute-start.13) | collective-permute-done | bytes 524320 | tf_op jit(solution)/shard_map/ppermute | solution.py:112
  361.3 8.8 collective-permute-done.16.refs_6_
  377.8 13.1 %shard_map.363 = (bf16[1024,2048]{1,0:T(8,128)(2,1)}, bf16[1024,2048]{1,0:T(8,128)(2,1)}, bf16[1024,2048]{1,0:T(8,128)(2,1)}, f32[1024,1]{1,0:T(8,128)}, f32[102...) custom-call(s32[8]{0:T(128)} %stack.276.info, bf16[128,2048]{1,0:T(8,128)(2,1)} %copy-done.16, ...), custom_call_target="tpu_custom_call" | custom-call | flops 1 | bytes 1 | tf_op jit(solution)/shard_map/pallas_call | solution.py:259
  391.0 9.0 all-gather.10.cloned.1.call-done.refs_0_.refs_1_.refs_2_.refs_3_.wq_ref.wk_ref.wv_ref.outward_ref.refs_8_.refs_10_.refs_16_
  400.1 11.0 %shard_map.366 = (bf16[1024,1024]{1,0:T(8,128)(2,1)}, bf16[1024,1024]{1,0:T(8,128)(2,1)}) custom-call(s32[1]{0:T(128)} %dynamic_slice.109.info, bf16[1024,2048]{1,0:T(8,128)(2,1)} %get-tuple-element.253.x_ref, bf16[2048,2048]{1,0:T(8,128)(2,1)} %all-gather.10.cloned.1.call-done.refs_0_.refs_1_.refs_2_.refs_3_.wq_ref.wk_ref.wv_ref.outward_ref.refs_8_.refs_10_.refs_16_, ...), custom_call_target="tpu_custom_call" | custom-call | flops 1 | bytes 1 | tf_op jit(solution)/shard_map/pallas_call | solution.py:259
  411.0 10.2 shard_map.367
  421.3 10.7 %shard_map.364 = (bf16[1024,1024]{1,0:T(8,128)(2,1)}, bf16[1024,1024]{1,0:T(8,128)(2,1)}) custom-call(s32[1]{0:T(128)} %dynamic_slice.109.info, bf16[1024,2048]{1,0:T(8,128)(2,1)} %get-tuple-element.253.x_ref, bf16[2048,2048]{1,0:T(8,128)(2,1)} %collective-permute-done.18.refs_0_.refs_1_.refs_2_.refs_3_.wq_ref.wk_ref.wv_ref.outward_ref.refs_9_.refs_11_.refs_17_, ...), custom_call_target="tpu_custom_call" | custom-call | flops 1 | bytes 1 | tf_op jit(solution)/shard_map/pallas_call | solution.py:259
  432.0 10.2 shard_map.365
  442.2 11.6 %shard_map.368 = (bf16[1024,256]{1,0:T(8,128)(2,1)}, bf16[1024,768]{1,0:T(8,128)(2,1)}, f32[1024,1]{1,0:T(8,128)}) custom-call(s32[1]{0:T(128)} %dynamic_slice.109.info, bf16[1024,2048]{1,0:T(8,128)(2,1)} %get-tuple-element.266.x_ref, ...), custom_call_target="tpu_custom_call" | custom-call | flops 1 | bytes 1 | tf_op jit(solution)/shard_map/pallas_call | solution.py:259
  453.9 11.8 %shard_map.369 = (bf16[1024,256]{1,0:T(8,128)(2,1)}, bf16[1024,768]{1,0:T(8,128)(2,1)}, f32[1024,1]{1,0:T(8,128)}) custom-call(s32[1]{0:T(128)} %dynamic_slice.109.info, bf16[1024,2048]{1,0:T(8,128)(2,1)} %get-tuple-element.266.x_ref, ...), custom_call_target="tpu_custom_call" | custom-call | flops 1 | bytes 1 | tf_op jit(solution)/shard_map/pallas_call | solution.py:259
  465.6 15.3 %all-gather.12.cloned.1.call-done.refs_0_.refs_1_.refs_2_.refs_3_.refs_18_ = bf16[2048,1024]{1,0:T(8,128)(2,1)} async-done(((bf16[512,1024]{1,0:T(8,128)(2,1)}), bf16[2048,1024]{1,0:T(8,128)(2,1)}) %all-gather.12.cloned.1.call-update) | async-done | bytes 4194320 | tf_op jit(solution)/shard_map/all_gather | solution.py:1029
  481.5 11.3 %shard_map.370 = (bf16[1024,256]{1,0:T(8,128)(2,1)}, bf16[1024,1024]{1,0:T(8,128)(2,1)}, f32[1,1024]{1,0:T(1,128)}) custom-call(s32[1]{0:T(128)} %dynamic_slice.109.info, bf16[1024,2048]{1,0:T(8,128)(2,1)} %get-tuple-element.293.g_ref, ...), custom_call_target="tpu_custom_call" | custom-call | flops 17179869184 | bytes 16777216 | tf_op jit(solution)/shard_map/pallas_call | solution.py:259
  509.1 10.9 %shard_map.372 = (bf16[1024,256]{1,0:T(8,128)(2,1)}, bf16[1024,1024]{1,0:T(8,128)(2,1)}, f32[1,1024]{1,0:T(1,128)}) custom-call(s32[1]{0:T(128)} %dynamic_slice.109.info, bf16[1024,2048]{1,0:T(8,128)(2,1)} %get-tuple-element.293.g_ref, ...), custom_call_target="tpu_custom_call" | custom-call | flops 1 | bytes 1 | tf_op jit(solution)/shard_map/pallas_call | solution.py:259
  520.0 10.2 shard_map.373
  541.7 11.5 %shard_map.374 = bf16[2048,1024]{1,0:T(8,128)(2,1)} custom-call(s32[1]{0:T(128)} %dynamic_slice.109.info, bf16[2048,1024]{1,0:T(8,128)(2,1)} %get-tuple-element.296.refs_0_, bf16[1024,1024]{1,0:T(8,128)(2,1)} %get-tuple-element.297.refs_1_.refs_2_.refs_3_.refs_4_.refs_6_, bf16[1024,1024]{1,0:T(8,128)(2,1)} %get-tuple-element.297.refs_1_.refs_2_.refs_3_.refs_4_.refs_6_, ...), custom_call_target="tpu_custom_call" | custom-call | flops 1 | bytes 1 | tf_op jit(solution)/shard_map/pallas_call | solution.py:259
  553.9 8.0 shard_map.375.refs_5_.refs_2_.refs_3_.refs_4_
  561.8 13.2 %reduce-scatter.7.cloned.1.call-done.refs_3_ = bf16[512,1024]{1,0:T(8,128)(2,1)} async-done(((bf16[2048,1024]{1,0:T(8,128)(2,1)}), bf16[512,1024]{1,0:T(8,128)(2,1)}) %reduce-scatter.7.cloned.1.call-update) | async-done | bytes 1048592 | tf_op jit(solution)/shard_map/reduce_scatter | solution.py:886
  575.1 30.9 %shard_map.376 = (bf16[128,2048]{1,0:T(8,128)(2,1)}, bf16[128,2048]{1,0:T(8,128)(2,1)}, bf16[256,2048]{1,0:T(8,128)(2,1)}, bf16[128,2048]{1,0:T(8,128)(2,1)}, bf...) custom-call(s32[16]{0:T(128)} %stack.282.info, ...), custom_call_target="tpu_custom_call" | custom-call | flops 1 | bytes 1 | tf_op jit(solution)/shard_map/pallas_call | solution.py:259
  605.9 11.0 %shard_map.380 = (bf16[2048,256]{1,0:T(8,128)(2,1)}, bf16[2048,256]{1,0:T(8,128)(2,1)}, bf16[2048,256]{1,0:T(8,128)(2,1)}, bf16[2048,256]{1,0:T(8,128)(2,1)}) custom-call(s32[1]{0:T(128)} %dynamic_slice.109.info, bf16[2048,1024]{1,0:T(8,128)(2,1)} %get-tuple-element.345.refs_0_, bf16[2048,1024]{1,0:T(8,128)(2,1)} %get-tuple-element.226.refs_0_.refs_1_, ...), custom_call_target="tpu_custom_call" | custom-call | flops 17179869184 | bytes 16777216 | tf_op jit(solution)/shard_map/pallas_call | solution.py:259
  625.3 12.3 %shard_map.381 = bf16[2048,1024]{1,0:T(8,128)(2,1)} custom-call(s32[1]{0:T(128)} %dynamic_slice.109.info, bf16[2048,1024]{1,0:T(8,128)(2,1)} %get-tuple-element.345.refs_0_, bf16[2048,1024]{1,0:T(8,128)(2,1)} %get-tuple-element.226.refs_0_.refs_1_, bf16[1024,768]{1,0:T(8,128)(2,1)} %shard_map.371.refs_4_.refs_2_.refs_3_, ...), custom_call_target="tpu_custom_call" | custom-call | flops 17179869184 | bytes 16777216 | tf_op jit(solution)/shard_map/pallas_call | solution.py:259
  642.3 10.9 %collective-permute-done.28 = bf16[128,2048]{1,0:T(8,128)(2,1)S(1)} collective-permute-done((bf16[128,2048]{1,0:T(8,128)(2,1)}, bf16[128,2048]{1,0:T(8,128)(2,1)S(1)}, u32[]{:S(2)}, u32[]{:S(2)}) %collective-permute-start.28) | collective-permute-done | bytes 524320 | tf_op jit(solution)/shard_map/ppermute | solution.py:112
  653.2 10.4 collective-permute-done.29
  669.2 8.9 collective-permute-done.32
  686.4 10.8 %collective-permute-done.35.refs_5_ = bf16[128,2048]{1,0:T(8,128)(2,1)S(1)} collective-permute-done((bf16[128,2048]{1,0:T(8,128)(2,1)S(1)}, bf16[128,2048]{1,0:T(8,128)(2,1)S(1)}, u32[]{:S(2)}, u32[]{:S(2)}) %collective-permute-start.35) | collective-permute-done | bytes 524320 | tf_op jit(solution)/shard_map/ppermute | solution.py:112
  699.8 10.1 collective-permute-done.38.refs_6_
  725.5 10.2 shard_map.378
  736.7 10.8 %shard_map.379 = (bf16[1024,256]{1,0:T(8,128)(2,1)}, bf16[1024,1024]{1,0:T(8,128)(2,1)}, f32[1,1024]{1,0:T(1,128)}) custom-call(s32[1]{0:T(128)} %dynamic_slice.109.info, bf16[1024,2048]{1,0:T(8,128)(2,1)} %get-tuple-element.356.g_ref, bf16[2048,2304]{1,0:T(8,128)(2,1)} %all-gather.8.cloned.1.call-done.refs_0_.refs_1_.refs_2_.refs_3_.refs_16_.refs_18_.outward_ref.refs_10_, ...), custom_call_target="tpu_custom_call" | custom-call | flops 17179869184 | bytes 16777216 | tf_op jit(solution)/shard_map/pallas_call | solution.py:259
  750.2 11.5 %shard_map.383 = bf16[2048,1024]{1,0:T(8,128)(2,1)} custom-call(s32[1]{0:T(128)} %dynamic_slice.109.info, bf16[2048,1024]{1,0:T(8,128)(2,1)} %get-tuple-element.370.refs_0_, bf16[1024,1024]{1,0:T(8,128)(2,1)} %get-tuple-element.355.refs_8_.refs_9_.refs_10_.refs_11_.refs_1_.refs_2_.refs_3_.refs_4_, ...), custom_call_target="tpu_custom_call" | custom-call | flops 1 | bytes 1 | tf_op jit(solution)/shard_map/pallas_call | solution.py:259
  762.0 10.9 %shard_map.384 = (bf16[1024,256]{1,0:T(8,128)(2,1)}, bf16[1024,1024]{1,0:T(8,128)(2,1)}, f32[1,1024]{1,0:T(1,128)}) custom-call(s32[1]{0:T(128)} %dynamic_slice.109.info, bf16[1024,2048]{1,0:T(8,128)(2,1)} %get-tuple-element.356.g_ref, bf16[2048,2304]{1,0:T(8,128)(2,1)} %collective-permute-done.5.refs_0_.refs_1_.refs_2_.refs_3_.refs_17_.refs_19_.outward_ref.refs_11_, ...), custom_call_target="tpu_custom_call" | custom-call | flops 1 | bytes 1 | tf_op jit(solution)/shard_map/pallas_call | solution.py:259
  780.5 13.4 %shard_map.386 = (bf16[2048,256]{1,0:T(8,128)(2,1)}, bf16[2048,256]{1,0:T(8,128)(2,1)}, bf16[2048,256]{1,0:T(8,128)(2,1)}, bf16[2048,256]{1,0:T(8,128)(2,1)}, bf...) custom-call(s32[1]{0:T(128)} %dynamic_slice.109.info, ...), custom_call_target="tpu_custom_call" | custom-call | flops 1 | bytes 1 | tf_op jit(solution)/shard_map/pallas_call | solution.py:259
  808.0 16.0 %shard_map.387 = bf16[2048,1792]{1,0:T(8,128)(2,1)} custom-call(s32[1]{0:T(128)} %dynamic_slice.109.info, bf16[2048,1024]{1,0:T(8,128)(2,1)} %get-tuple-element.334.refs_0_, bf16[2048,1024]{1,0:T(8,128)(2,1)} %get-tuple-element.335.refs_1_, bf16[1024,1024]{1,0:T(8,128)(2,1)} %get-tuple-element.354.refs_2_.refs_3_.refs_4_.refs_5_.refs_6_, ...), custom_call_target="tpu_custom_call" | custom-call | flops 1 | bytes 1 | tf_op jit(solution)/shard_map/pallas_call | solution.py:259
  843.7 18.5 %shard_map.390 = (bf16[128,2048]{1,0:T(8,128)(2,1)}, bf16[128,2048]{1,0:T(8,128)(2,1)}, bf16[256,2048]{1,0:T(8,128)(2,1)}, bf16[128,2048]{1,0:T(8,128)(2,1)}, bf...) custom-call(s32[8]{0:T(128)} %stack.259.info, ...), custom_call_target="tpu_custom_call" | custom-call | flops 1 | bytes 1 | tf_op jit(solution)/shard_map/pallas_call | solution.py:259
  867.2 31.4 %shard_map.391 = (bf16[128,2048]{1,0:T(8,128)(2,1)}, bf16[128,2048]{1,0:T(8,128)(2,1)}, bf16[256,2048]{1,0:T(8,128)(2,1)}, bf16[128,2048]{1,0:T(8,128)(2,1)}, bf...) custom-call(s32[16]{0:T(128)} %stack.282.info, ...), custom_call_target="tpu_custom_call" | custom-call | flops 1 | bytes 1 | tf_op jit(solution)/shard_map/pallas_call | solution.py:259
  915.8 11.1 %collective-permute-done.65 = bf16[128,2048]{1,0:T(8,128)(2,1)S(1)} collective-permute-done((bf16[128,2048]{1,0:T(8,128)(2,1)}, bf16[128,2048]{1,0:T(8,128)(2,1)S(1)}, u32[]{:S(2)}, u32[]{:S(2)}) %collective-permute-start.65) | collective-permute-done | bytes 524320 | tf_op jit(solution)/shard_map/ppermute | solution.py:112
  971.7 13.5 %shard_map.392 = (f32[2048,512]{1,0:T(8,128)}, f32[2048,512]{1,0:T(8,128)}, f32[2048,512]{1,0:T(8,128)}) custom-call(s32[1]{0:T(128)} %bitcast.14.info, bf16[512,1024]{1,0:T(8,128)(2,1)} %reduce-scatter.13.cloned.1.call-done.refs_0_, bf16[512,1024]{1,0:T(8,128)(2,1)} %copy-done.35, bf16[512,1024]{1,0:T(8,128)(2,1)} %collective-permute-done.71.refs_2_, ...), custom_call_target="tpu_custom_call" | custom-call | flops 1 | bytes 1 | tf_op jit(solution)/shard_map/pallas_call | solution.py:259
  1006.9 10.1 shard_map.394
  1017.0 10.6 %shard_map.393 = (f32[3,512,512]{2,1,0:T(8,128)}, f32[3,512,512]{2,1,0:T(8,128)}, f32[3,512,512]{2,1,0:T(8,128)}) custom-call(s32[1]{0:T(128)} %bitcast.14.info, bf16[512,1792]{1,0:T(8,128)(2,1)} %reduce-scatter.15.cloned.1.call-done.refs_0_, bf16[512,1792]{1,0:T(8,128)(2,1)} %copy-done.5, bf16[512,1024]{1,0:T(8,128)(2,1)} %collective-permute-done.73.refs_2_, ...), custom_call_target="tpu_custom_call" | custom-call | flops 1 | bytes 1 | tf_op jit(solution)/shard_map/pallas_call | solution.py:259
  (466 shorter events, 301.6 us)
Async XLA Ops:
  7.2 77.4 %all-gather.6.cloned.1.call-start = ((), (), s32[]{:S(2)}) async-start(), calls=%async_computation.6 | async-start | bytes 3932160 | tf_op jit(solution)/shard_map/all_gather | solution.py:1029
  14.6 235.6 %all-gather.8.cloned.1.call-start = ((), (), s32[]{:S(2)}) async-start(), calls=%async_computation.7 | async-start | bytes 11796480 | tf_op jit(solution)/shard_map/all_gather | solution.py:1029
  32.3 367.7 %all-gather.10.cloned.1.call-start = ((), (), s32[]{:S(2)}) async-start(), calls=%async_computation.8 | async-start | bytes 10485760 | tf_op jit(solution)/shard_map/all_gather | solution.py:1029
  84.6 17.2 %collective-permute-start.1 = (bf16[2048,768]{1,0:T(8,128)(2,1)}, bf16[2048,768]{1,0:T(8,128)(2,1)S(1)}, u32[]{:S(2)}, u32[]{:S(2)}) collective-permute-start(bf16[2048,768]{1,0:T(8,128)(2,1)} %all-gather.6.cloned.1.call-done.wq_ref.wk_ref.wv_ref.refs_8_), channel_id=1, source_target_pairs={{0,16},{16,0},{1,17},{17,1},{2,18},{18,2},{3,19},{19,3},{4,20},{20... | collective-permute-start | bytes 9437192 | tf_op jit(solution)/shard_map/ppermute | solution.py:92
  250.2 15.0 %collective-permute-start.5 = (bf16[2048,2304]{1,0:T(8,128)(2,1)}, bf16[2048,2304]{1,0:T(8,128)(2,1)}, u32[]{:S(2)}, u32[]{:S(2)}) collective-permute-start(bf16[2048,2304]{1,0:T(8,128)(2,1)} %all-gather.8.cloned.1.call-done.refs_0_.refs_1_.refs_2_.refs_3_.refs_16_.refs_18_.outward_ref.refs_10_), channel_id=1, source_target_pairs={{0,16},{16,0},{1,17},{17,1},{2,18},{18,2},{3,19},{19,3},{4,20},{20... | collective-permute-start | bytes 28311560 | tf_op jit(solution)/shard_map/ppermute | solution.py:92
  251.9 229.1 %all-gather.12.cloned.1.call-start = ((), (), s32[]{:S(2)}) async-start(), calls=%async_computation.9 | async-start | bytes 5242880 | tf_op jit(solution)/shard_map/all_gather | solution.py:1029
  293.1 15.1 %collective-permute-start.6 = (bf16[128,2048]{1,0:T(8,128)(2,1)}, bf16[128,2048]{1,0:T(8,128)(2,1)S(1)}, u32[]{:S(2)}, u32[]{:S(2)}) collective-permute-start(bf16[128,2048]{1,0:T(8,128)(2,1)} %get-tuple-element.235), channel_id=1, source_target_pairs={{0,4},{4,0},{8,12},{12,8},{1,5},{5,1},{9,13},{13,9},{2,6},{6,2},{1... | collective-permute-start | bytes 1572872 | tf_op jit(solution)/shard_map/ppermute | solution.py:112
  294.6 23.9 %collective-permute-start.7 = (bf16[128,2048]{1,0:T(8,128)(2,1)}, bf16[128,2048]{1,0:T(8,128)(2,1)S(1)}, u32[]{:S(2)}, u32[]{:S(2)}) collective-permute-start(bf16[128,2048]{1,0:T(8,128)(2,1)} %get-tuple-element.236), channel_id=1, source_target_pairs={{0,4},{4,0},{8,12},{12,8},{1,5},{5,1},{9,13},{13,9},{2,6},{6,2},{1... | collective-permute-start | bytes 1572872 | tf_op jit(solution)/shard_map/ppermute | solution.py:112
  295.2 23.4 %collective-permute-start.8 = (bf16[128,2048]{1,0:T(8,128)(2,1)}, bf16[128,2048]{1,0:T(8,128)(2,1)S(1)}, u32[]{:S(2)}, u32[]{:S(2)}) collective-permute-start(bf16[128,2048]{1,0:T(8,128)(2,1)} %get-tuple-element.237), channel_id=1, source_target_pairs={{0,8},{4,12},{8,0},{12,4},{1,9},{5,13},{9,1},{13,5},{2,10},{6,14},... | collective-permute-start | bytes 1572872 | tf_op jit(solution)/shard_map/ppermute | solution.py:112
  296.6 23.4 %collective-permute-start.9 = (bf16[128,2048]{1,0:T(8,128)(2,1)}, bf16[128,2048]{1,0:T(8,128)(2,1)S(1)}, u32[]{:S(2)}, u32[]{:S(2)}) collective-permute-start(bf16[128,2048]{1,0:T(8,128)(2,1)} %get-tuple-element.238), channel_id=1, source_target_pairs={{0,8},{4,12},{8,0},{12,4},{1,9},{5,13},{9,1},{13,5},{2,10},{6,14},... | collective-permute-start | bytes 1572872 | tf_op jit(solution)/shard_map/ppermute | solution.py:112
  344.5 25.6 %collective-permute-start.16 = (bf16[128,2048]{1,0:T(8,128)(2,1)S(1)}, bf16[128,2048]{1,0:T(8,128)(2,1)S(1)}, u32[]{:S(2)}, u32[]{:S(2)}) collective-permute-start(bf16[128,2048]{1,0:T(8,128)(2,1)S(1)} %get-tuple-element.524.refs_4_), channel_id=1, source_target_pairs={{0,8},{4,12},{8,0},{12,4},{1,9},{5,13},{9,1},{13,5},{2,10},{6,14},... | collective-permute-start | bytes 1572872 | tf_op jit(solution)/shard_map/ppermute | solution.py:112
  346.0 24.1 %collective-permute-start.14 = (bf16[128,2048]{1,0:T(8,128)(2,1)S(1)}, bf16[128,2048]{1,0:T(8,128)(2,1)S(1)}, u32[]{:S(2)}, u32[]{:S(2)}) collective-permute-start(bf16[128,2048]{1,0:T(8,128)(2,1)S(1)} %get-tuple-element.525.refs_0_), channel_id=1, source_target_pairs={{0,4},{4,0},{8,12},{12,8},{1,5},{5,1},{9,13},{13,9},{2,6},{6,2},{1... | collective-permute-start | bytes 1572872 | tf_op jit(solution)/shard_map/ppermute | solution.py:112
  358.8 17.8 %collective-permute-start.15 = (bf16[128,2048]{1,0:T(8,128)(2,1)S(1)}, bf16[128,2048]{1,0:T(8,128)(2,1)}, u32[]{:S(2)}, u32[]{:S(2)}) collective-permute-start(bf16[128,2048]{1,0:T(8,128)(2,1)S(1)} %collective-permute-done.12.refs_1_), channel_id=1, source_target_pairs={{0,4},{4,0},{8,12},{12,8},{1,5},{5,1},{9,13},{13,9},{2,6},{6,2},{1... | collective-permute-start | bytes 1572872 | tf_op jit(solution)/shard_map/ppermute | solution.py:112
  359.4 18.4 %collective-permute-start.17 = (bf16[128,2048]{1,0:T(8,128)(2,1)S(1)}, bf16[128,2048]{1,0:T(8,128)(2,1)}, u32[]{:S(2)}, u32[]{:S(2)}) collective-permute-start(bf16[128,2048]{1,0:T(8,128)(2,1)S(1)} %collective-permute-done.13.refs_5_), channel_id=1, source_target_pairs={{0,8},{4,12},{8,0},{12,4},{1,9},{5,13},{9,1},{13,5},{2,10},{6,14},... | collective-permute-start | bytes 1572872 | tf_op jit(solution)/shard_map/ppermute | solution.py:112
  399.9 21.3 %collective-permute-start.18 = (bf16[2048,2048]{1,0:T(8,128)(2,1)}, bf16[2048,2048]{1,0:T(8,128)(2,1)}, u32[]{:S(2)}, u32[]{:S(2)}) collective-permute-start(bf16[2048,2048]{1,0:T(8,128)(2,1)} %all-gather.10.cloned.1.call-done.refs_0_.refs_1_.refs_2_.refs_3_.wq_ref.wk_ref.wv_ref.outward_ref.refs_8_.refs_10_.r, ...), channel_id=1, source_target_pairs={{0,16},{16,0},{1,17},{17,1},{2,18},{18,2},{3,19},{19,3},{4,20},{20... | collective-permute-start | bytes 25165832 | tf_op jit(solution)/shard_map/ppermute | solution.py:92
  400.0 175.1 %reduce-scatter.7.cloned.1.call-start = ((), (), s32[]{:S(2)}) async-start(), calls=%async_computation.10 | async-start | bytes 5242880 | tf_op jit(solution)/shard_map/reduce_scatter | solution.py:886
  499.6 217.9 %reduce-scatter.9.cloned.1.call-start = ((), (), s32[]{:S(2)}) async-start(), calls=%async_computation.11 | async-start | bytes 5242880 | tf_op jit(solution)/shard_map/reduce_scatter | solution.py:886
  553.2 227.4 %reduce-scatter.11.cloned.1.call-start = ((), (), s32[]{:S(2)}) async-start(), calls=%async_computation.12 | async-start | bytes 5242880 | tf_op jit(solution)/shard_map/reduce_scatter | solution.py:886
  637.6 263.0 %reduce-scatter.13.cloned.1.call-start = ((), (), s32[]{:S(2)}) async-start(), calls=%async_computation.13 | async-start | bytes 5242880 | tf_op jit(solution)/shard_map/reduce_scatter | solution.py:886
  638.1 15.0 %collective-permute-start.28 = (bf16[128,2048]{1,0:T(8,128)(2,1)}, bf16[128,2048]{1,0:T(8,128)(2,1)S(1)}, u32[]{:S(2)}, u32[]{:S(2)}) collective-permute-start(bf16[128,2048]{1,0:T(8,128)(2,1)} %get-tuple-element.308), channel_id=1, source_target_pairs={{0,4},{4,0},{8,12},{12,8},{1,5},{5,1},{9,13},{13,9},{2,6},{6,2},{1... | collective-permute-start | bytes 1572872 | tf_op jit(solution)/shard_map/ppermute | solution.py:112
  639.7 24.0 %collective-permute-start.29 = (bf16[128,2048]{1,0:T(8,128)(2,1)}, bf16[128,2048]{1,0:T(8,128)(2,1)S(1)}, u32[]{:S(2)}, u32[]{:S(2)}) collective-permute-start(bf16[128,2048]{1,0:T(8,128)(2,1)} %get-tuple-element.309), channel_id=1, source_target_pairs={{0,4},{4,0},{8,12},{12,8},{1,5},{5,1},{9,13},{13,9},{2,6},{6,2},{1... | collective-permute-start | bytes 1572872 | tf_op jit(solution)/shard_map/ppermute | solution.py:112
  640.2 23.4 %collective-permute-start.30 = (bf16[128,2048]{1,0:T(8,128)(2,1)S(1)}, bf16[128,2048]{1,0:T(8,128)(2,1)S(1)}, u32[]{:S(2)}, u32[]{:S(2)}) collective-permute-start(bf16[128,2048]{1,0:T(8,128)(2,1)S(1)} %copy-done.85), channel_id=1, source_target_pairs={{0,8},{4,12},{8,0},{12,4},{1,9},{5,13},{9,1},{13,5},{2,10},{6,14},... | collective-permute-start | bytes 1572872 | tf_op jit(solution)/shard_map/ppermute | solution.py:112
  641.7 23.2 %collective-permute-start.31 = (bf16[128,2048]{1,0:T(8,128)(2,1)S(1)}, bf16[128,2048]{1,0:T(8,128)(2,1)S(1)}, u32[]{:S(2)}, u32[]{:S(2)}) collective-permute-start(bf16[128,2048]{1,0:T(8,128)(2,1)S(1)} %copy-done.84), channel_id=1, source_target_pairs={{0,8},{4,12},{8,0},{12,4},{1,9},{5,13},{9,1},{13,5},{2,10},{6,14},... | collective-permute-start | bytes 1572872 | tf_op jit(solution)/shard_map/ppermute | solution.py:112
  684.3 25.5 %collective-permute-start.38 = (bf16[128,2048]{1,0:T(8,128)(2,1)S(1)}, bf16[128,2048]{1,0:T(8,128)(2,1)S(1)}, u32[]{:S(2)}, u32[]{:S(2)}) collective-permute-start(bf16[128,2048]{1,0:T(8,128)(2,1)S(1)} %get-tuple-element.327.refs_4_), channel_id=1, source_target_pairs={{0,8},{4,12},{8,0},{12,4},{1,9},{5,13},{9,1},{13,5},{2,10},{6,14},... | collective-permute-start | bytes 1572872 | tf_op jit(solution)/shard_map/ppermute | solution.py:112
  685.8 24.1 %collective-permute-start.36 = (bf16[128,2048]{1,0:T(8,128)(2,1)S(1)}, bf16[128,2048]{1,0:T(8,128)(2,1)S(1)}, u32[]{:S(2)}, u32[]{:S(2)}) collective-permute-start(bf16[128,2048]{1,0:T(8,128)(2,1)S(1)} %get-tuple-element.319.refs_0_), channel_id=1, source_target_pairs={{0,4},{4,0},{8,12},{12,8},{1,5},{5,1},{9,13},{13,9},{2,6},{6,2},{1... | collective-permute-start | bytes 1572872 | tf_op jit(solution)/shard_map/ppermute | solution.py:112
  698.6 17.6 %collective-permute-start.37 = (bf16[128,2048]{1,0:T(8,128)(2,1)S(1)}, bf16[128,2048]{1,0:T(8,128)(2,1)S(1)}, u32[]{:S(2)}, u32[]{:S(2)}) collective-permute-start(bf16[128,2048]{1,0:T(8,128)(2,1)S(1)} %collective-permute-done.34.refs_1_), channel_id=1, source_target_pairs={{0,4},{4,0},{8,12},{12,8},{1,5},{5,1},{9,13},{13,9},{2,6},{6,2},{1... | collective-permute-start | bytes 1572872 | tf_op jit(solution)/shard_map/ppermute | solution.py:112
  699.2 18.3 %collective-permute-start.39 = (bf16[128,2048]{1,0:T(8,128)(2,1)S(1)}, bf16[128,2048]{1,0:T(8,128)(2,1)}, u32[]{:S(2)}, u32[]{:S(2)}) collective-permute-start(bf16[128,2048]{1,0:T(8,128)(2,1)S(1)} %collective-permute-done.35.refs_5_), channel_id=1, source_target_pairs={{0,8},{4,12},{8,0},{12,4},{1,9},{5,13},{9,1},{13,5},{2,10},{6,14},... | collective-permute-start | bytes 1572872 | tf_op jit(solution)/shard_map/ppermute | solution.py:112
  761.7 223.6 %reduce-scatter.15.cloned.1.call-start = ((), (), s32[]{:S(2)}) async-start(), calls=%async_computation.14 | async-start | bytes 9175040 | tf_op jit(solution)/shard_map/reduce_scatter | solution.py:886
  824.0 203.7 %reduce-scatter.17.cloned.1.call-start = ((), (), s32[]{:S(2)}) async-start(), calls=%async_computation.15 | async-start | bytes 1310720 | tf_op jit(solution)/shard_map/reduce_scatter | solution.py:886
  862.3 36.3 %collective-permute-start.56 = (bf16[128,2048]{1,0:T(8,128)(2,1)}, bf16[128,2048]{1,0:T(8,128)(2,1)S(1)}, u32[]{:S(2)}, u32[]{:S(2)}) collective-permute-start(bf16[128,2048]{1,0:T(8,128)(2,1)} %get-tuple-element.376), channel_id=1, source_target_pairs={{0,4},{4,0},{8,12},{12,8},{1,5},{5,1},{9,13},{13,9},{2,6},{6,2},{1... | collective-permute-start | bytes 1572872 | tf_op jit(solution)/shard_map/ppermute | solution.py:112
  863.3 35.3 %collective-permute-start.57 = (bf16[128,2048]{1,0:T(8,128)(2,1)}, bf16[128,2048]{1,0:T(8,128)(2,1)S(1)}, u32[]{:S(2)}, u32[]{:S(2)}) collective-permute-start(bf16[128,2048]{1,0:T(8,128)(2,1)} %get-tuple-element.377), channel_id=1, source_target_pairs={{0,4},{4,0},{8,12},{12,8},{1,5},{5,1},{9,13},{13,9},{2,6},{6,2},{1... | collective-permute-start | bytes 1572872 | tf_op jit(solution)/shard_map/ppermute | solution.py:112
  864.4 34.2 %collective-permute-start.58 = (bf16[128,2048]{1,0:T(8,128)(2,1)}, bf16[128,2048]{1,0:T(8,128)(2,1)S(1)}, u32[]{:S(2)}, u32[]{:S(2)}) collective-permute-start(bf16[128,2048]{1,0:T(8,128)(2,1)} %get-tuple-element.378), channel_id=1, source_target_pairs={{0,8},{4,12},{8,0},{12,4},{1,9},{5,13},{9,1},{13,5},{2,10},{6,14},... | collective-permute-start | bytes 1572872 | tf_op jit(solution)/shard_map/ppermute | solution.py:112
  864.6 34.0 %collective-permute-start.59 = (bf16[128,2048]{1,0:T(8,128)(2,1)}, bf16[128,2048]{1,0:T(8,128)(2,1)S(1)}, u32[]{:S(2)}, u32[]{:S(2)}) collective-permute-start(bf16[128,2048]{1,0:T(8,128)(2,1)} %get-tuple-element.379), channel_id=1, source_target_pairs={{0,8},{4,12},{8,0},{12,4},{1,9},{5,13},{9,1},{13,5},{2,10},{6,14},... | collective-permute-start | bytes 1572872 | tf_op jit(solution)/shard_map/ppermute | solution.py:112
  867.1 103.7 %collective-permute-start.71 = (bf16[512,1024]{1,0:T(8,128)(2,1)}, bf16[512,1024]{1,0:T(8,128)(2,1)}, u32[]{:S(2)}, u32[]{:S(2)}) collective-permute-start(bf16[512,1024]{1,0:T(8,128)(2,1)} %reduce-scatter.7.cloned.1.call-done.refs_3_), channel_id=1, source_target_pairs={{0,16},{16,0},{1,17},{17,1},{2,18},{18,2},{3,19},{19,3},{4,20},{20... | collective-permute-start | bytes 3145736 | tf_op jit(solution)/shard_map/ppermute | solution.py:92
  900.6 15.0 %collective-permute-start.66 = (bf16[128,2048]{1,0:T(8,128)(2,1)}, bf16[128,2048]{1,0:T(8,128)(2,1)S(1)}, u32[]{:S(2)}, u32[]{:S(2)}) collective-permute-start(bf16[128,2048]{1,0:T(8,128)(2,1)} %get-tuple-element.399), channel_id=1, source_target_pairs={{0,8},{4,12},{8,0},{12,4},{1,9},{5,13},{9,1},{13,5},{2,10},{6,14},... | collective-permute-start | bytes 1572872 | tf_op jit(solution)/shard_map/ppermute | solution.py:112
  900.9 26.0 %collective-permute-start.65 = (bf16[128,2048]{1,0:T(8,128)(2,1)}, bf16[128,2048]{1,0:T(8,128)(2,1)S(1)}, u32[]{:S(2)}, u32[]{:S(2)}) collective-permute-start(bf16[128,2048]{1,0:T(8,128)(2,1)} %get-tuple-element.397), channel_id=1, source_target_pairs={{0,8},{4,12},{8,0},{12,4},{1,9},{5,13},{9,1},{13,5},{2,10},{6,14},... | collective-permute-start | bytes 1572872 | tf_op jit(solution)/shard_map/ppermute | solution.py:112
  902.7 25.1 %collective-permute-start.64 = (bf16[128,2048]{1,0:T(8,128)(2,1)}, bf16[128,2048]{1,0:T(8,128)(2,1)S(1)}, u32[]{:S(2)}, u32[]{:S(2)}) collective-permute-start(bf16[128,2048]{1,0:T(8,128)(2,1)} %get-tuple-element.395), channel_id=1, source_target_pairs={{0,4},{4,0},{8,12},{12,8},{1,5},{5,1},{9,13},{13,9},{2,6},{6,2},{1... | collective-permute-start | bytes 1572872 | tf_op jit(solution)/shard_map/ppermute | solution.py:112
  903.7 24.2 %collective-permute-start.63 = (bf16[128,2048]{1,0:T(8,128)(2,1)}, bf16[128,2048]{1,0:T(8,128)(2,1)S(1)}, u32[]{:S(2)}, u32[]{:S(2)}) collective-permute-start(bf16[128,2048]{1,0:T(8,128)(2,1)} %get-tuple-element.393), channel_id=1, source_target_pairs={{0,4},{4,0},{8,12},{12,8},{1,5},{5,1},{9,13},{13,9},{2,6},{6,2},{1... | collective-permute-start | bytes 1572872 | tf_op jit(solution)/shard_map/ppermute | solution.py:112
  915.6 22.6 %collective-permute-start.60 = (bf16[128,2048]{1,0:T(8,128)(2,1)}, bf16[128,2048]{1,0:T(8,128)(2,1)}, u32[]{:S(2)}, u32[]{:S(2)}) collective-permute-start(bf16[128,2048]{1,0:T(8,128)(2,1)} %fusion.36), channel_id=1, source_target_pairs={{0,8},{4,12},{8,0},{12,4},{1,9},{5,13},{9,1},{13,5},{2,10},{6,14},... | collective-permute-start | bytes 1572872 | tf_op jit(solution)/shard_map/ppermute | solution.py:112
  926.9 15.2 %collective-permute-start.61 = (bf16[128,2048]{1,0:T(8,128)(2,1)}, bf16[128,2048]{1,0:T(8,128)(2,1)}, u32[]{:S(2)}, u32[]{:S(2)}) collective-permute-start(bf16[128,2048]{1,0:T(8,128)(2,1)} %fusion.34), channel_id=1, source_target_pairs={{0,4},{4,0},{8,12},{12,8},{1,5},{5,1},{9,13},{13,9},{2,6},{6,2},{1... | collective-permute-start | bytes 1572872 | tf_op jit(solution)/shard_map/ppermute | solution.py:112
  929.5 19.6 %collective-permute-start.67 = (bf16[128,2048]{1,0:T(8,128)(2,1)}, bf16[128,2048]{1,0:T(8,128)(2,1)}, u32[]{:S(2)}, u32[]{:S(2)}) collective-permute-start(bf16[128,2048]{1,0:T(8,128)(2,1)} %fusion.28), channel_id=1, source_target_pairs={{0,8},{4,12},{8,0},{12,4},{1,9},{5,13},{9,1},{13,5},{2,10},{6,14},... | collective-permute-start | bytes 1572872 | tf_op jit(solution)/shard_map/ppermute | solution.py:112
  931.4 20.2 %collective-permute-start.68 = (bf16[128,2048]{1,0:T(8,128)(2,1)}, bf16[128,2048]{1,0:T(8,128)(2,1)}, u32[]{:S(2)}, u32[]{:S(2)}) collective-permute-start(bf16[128,2048]{1,0:T(8,128)(2,1)} %fusion.26), channel_id=1, source_target_pairs={{0,4},{4,0},{8,12},{12,8},{1,5},{5,1},{9,13},{13,9},{2,6},{6,2},{1... | collective-permute-start | bytes 1572872 | tf_op jit(solution)/shard_map/ppermute | solution.py:112
  969.1 16.8 %collective-permute-start.78 = (f32[2,12288]{1,0:T(2,128)S(1)}, f32[2,12288]{1,0:T(2,128)S(1)}, u32[]{:S(2)}, u32[]{:S(2)}) collective-permute-start(f32[2,12288]{1,0:T(2,128)S(1)} %maximum_maximum_fusion.3), channel_id=1, source_target_pairs={{0,16},{16,0},{1,17},{17,1},{2,18},{18,2},{3,19},{19,3},{4,20},{20... | collective-permute-start | bytes 294920 | tf_op jit(solution)/shard_map/ppermute | solution.py:87
  970.3 25.4 %collective-permute-start.62 = (bf16[256,2048]{1,0:T(8,128)(2,1)}, bf16[256,2048]{1,0:T(8,128)(2,1)}, u32[]{:S(2)}, u32[]{:S(2)}) collective-permute-start(bf16[256,2048]{1,0:T(8,128)(2,1)} %broadcast_select_fusion.2), channel_id=1, source_target_pairs={{0,16},{16,0},{1,17},{17,1},{2,18},{18,2},{3,19},{19,3},{4,20},{20... | collective-permute-start | bytes 3145736 | tf_op jit(solution)/shard_map/ppermute | solution.py:92
  970.7 57.0 %collective-permute-start.69 = (f32[256,2048]{1,0:T(8,128)}, f32[256,2048]{1,0:T(8,128)}, u32[]{:S(2)}, u32[]{:S(2)}) collective-permute-start(f32[256,2048]{1,0:T(8,128)} %get-tuple-element.497), channel_id=1, source_target_pairs={{0,16},{16,0},{1,17},{17,1},{2,18},{18,2},{3,19},{19,3},{4,20},{20... | collective-permute-start | bytes 6291464 | tf_op jit(solution)/shard_map/ppermute | solution.py:92
  985.3 20.3 %collective-permute-start.72 = (bf16[512,1792]{1,0:T(8,128)(2,1)}, bf16[512,1792]{1,0:T(8,128)(2,1)S(1)}, u32[]{:S(2)}, u32[]{:S(2)}) collective-permute-start(bf16[512,1792]{1,0:T(8,128)(2,1)} %reduce-scatter.15.cloned.1.call-done.refs_0_), channel_id=1, source_target_pairs={{0,16},{16,0},{1,17},{17,1},{2,18},{18,2},{3,19},{19,3},{4,20},{20... | collective-permute-start | bytes 5505032 | tf_op jit(solution)/shard_map/ppermute | solution.py:92
  987.7 17.9 %collective-permute-start.74 = (bf16[512,1024]{1,0:T(8,128)(2,1)}, bf16[512,1024]{1,0:T(8,128)(2,1)}, u32[]{:S(2)}, u32[]{:S(2)}) collective-permute-start(bf16[512,1024]{1,0:T(8,128)(2,1)} %reduce-scatter.9.cloned.1.call-done.refs_3_), channel_id=1, source_target_pairs={{0,16},{16,0},{1,17},{17,1},{2,18},{18,2},{3,19},{19,3},{4,20},{20... | collective-permute-start | bytes 3145736 | tf_op jit(solution)/shard_map/ppermute | solution.py:92
  995.6 21.4 %collective-permute-start.73 = (bf16[512,1024]{1,0:T(8,128)(2,1)S(1)}, bf16[512,1024]{1,0:T(8,128)(2,1)}, u32[]{:S(2)}, u32[]{:S(2)}) collective-permute-start(bf16[512,1024]{1,0:T(8,128)(2,1)S(1)} %copy-done.14), channel_id=1, source_target_pairs={{0,16},{16,0},{1,17},{17,1},{2,18},{18,2},{3,19},{19,3},{4,20},{20... | collective-permute-start | bytes 3145736 | tf_op jit(solution)/shard_map/ppermute | solution.py:92
  (130 other events, 1562.9 us)
Sparse Core Ops, SparseCore 0:
  14.7 67.7 all-gather.5
  84.6 165.5 all-gather.7
  252.0 147.9 all-gather.9
  401.9 78.9 all-gather.11
  499.8 75.2 reduce-scatter.6
  577.9 77.2 reduce-scatter.8
  657.5 77.2 reduce-scatter.10
  761.9 75.8 reduce-scatter.12
  840.1 128.2 reduce-scatter.14
  970.5 29.7 reduce-scatter.16

commit v3 on v2

--- a/solution.py
+++ b/solution.py
@@ -142,7 +142,7 @@
     return places
 
 
-def sum_scatter(pieces, peers, bits):
+def sum_scatter(pieces, peers, bits, beside=()):
     me = lax.axis_index("tensor")
     half = peers // 2
     width = pieces[0].shape[1]
@@ -150,8 +150,14 @@
     keeps = [pieces[k * (half + 1) + half] for k in (0, 1)]
     left = [[b for b in reversed(range(bits)) if b != step_bits(bits, k)[0]] for k in (0, 1)]
     for step in range(bits):
-        arrived = lax.optimization_barrier(
-            [[flipped(item, peers, step_bits(bits, k)[step]) for item in sends[k]] for k in (0, 1)]
+        arrived, unused = lax.optimization_barrier(
+            (
+                [
+                    [flipped(item, peers, step_bits(bits, k)[step]) for item in sends[k]]
+                    for k in (0, 1)
+                ],
+                list(beside) if step == bits - 1 else [],
+            )
         )
         for k in (0, 1):
             got = arrived[k]
@@ -1036,9 +1042,9 @@
         block = lax.dynamic_slice_in_dim(array, place * row_share, row_share, 0)
         return block.astype(jnp.float32)
 
-    def summed(pieces):
+    def summed(pieces, beside=()):
         if bits:
-            return jnp.concatenate(sum_scatter(pieces, peers, bits), axis=0)
+            return jnp.concatenate(sum_scatter(pieces, peers, bits, beside), axis=0)
         return lax.psum_scatter(pieces[0], "tensor", scatter_dimension=0, tiled=True).astype(
             jnp.float32
         )
@@ -1149,8 +1155,8 @@
                 mine = [after(mine[0], between), *mine[1:]]
             return grads_call(lefts, mine, head_share, info, got, cost)
 
-        lifted = [lift(0, after(grad_low, *theirs), work(dense))]
         if layer == 1:
+            lifted = [lift(0, after(grad_low, *theirs), work(dense))]
             mine = [after(item, lifted[0][1]) for item in mine]
             contract_total = jnp.concatenate(
                 [
@@ -1160,9 +1166,8 @@
                 axis=1,
             )
         else:
-            contract_total = grads_call(
-                [grad_turned], [after(acts[0], lifted[0][1])], head_share, info, got
-            )
+            contract_total = grads_call([grad_turned], [acts[0]], head_share, info, got)
+            lifted = [lift(0, after(grad_low, contract_total))]
         contract_share = share_of(contract_total)
         lifted.append(lift(1, after(grad_low, contract_total)))
         out_grads = [item[0] for item in lifted]
@@ -1179,16 +1184,16 @@
             expand_share = share_of(expand_total)
             out_grads = [after(item, expand_total) for item in out_grads]
             mixed_grads = [mixed_first, heads_back(1, out_grads, saved)]
-            ahead = [contract_share, *mixed_grads]
+            ahead = mixed_grads
         else:
             mixed_last = heads_back(1, out_grads, saved)
             mixed_first = heads_back(0, out_grads, saved, small_work)
             mixed_grads = [mixed_first, mixed_last]
             hidden_here = [after(item, *shares[1]) for item in hidden_grads]
             other_total = total_of(
-                [second_turned, first_turned],
-                [hidden_here[1], mixed_last],
-                [hidden_here[0], mixed_first],
+                [second_turned, first_turned, grad_turned],
+                [hidden_here[1], mixed_last, heads[1]],
+                [hidden_here[0], mixed_first, heads[0]],
                 between=mixed_first,
             )
             ahead = [other_total]
@@ -1208,23 +1213,30 @@
         rights = [[mixed_grads[which], heads[which]] for which in (1, 0)]
         if layer == 1:
             lefts[0] = after(lefts[0], *pieces)
-            shares[1] = (share_of(total_of(lefts, *rights, work(dense))), expand_share, contract_share)
+            heads_total = total_of(lefts, *rights, work(dense))
+            shares[1] = (share_of(heads_total), expand_share, contract_share)
+            pieces = [after(item, contract_share) for item in pieces]
         else:
-            outward_total = total_of(
-                [after(grad_turned, other_total)], [rights[0][1]], [rights[1][1]]
+            shares[0] = share_of(other_total)
+            contract_here = after(contract_share, *pieces)
+            contract_out = adam_rows(
+                3,
+                (contract_here, swap(contract_here), swap(shares[1][2]), shares[1][2]),
+                [item[0] for item in (contract, contract_first, contract_second)],
+                (0, 0),
+                head_share,
+                core[None],
             )
             pairs = [
-                [after(item, outward_total) for item in pair]
+                [after(item, *pieces) for item in pair]
                 for pair in (outward_pairs[1], contract_pairs[1])
             ]
-            pieces = [after(item, contract_share) for item in pieces]
-            shares[0] = (share_of(other_total), share_of(outward_total), contract_share)
             results.append(layer_output(1, *pairs, *last))
         upstream = block_of(grad_low)
         vector_grads[layer] = jnp.concatenate(
             [norm_part, jnp.sum(upstream, axis=0)[None]], axis=0
         )
-        row_grads[layer] = upstream + summed(pieces)
+        row_grads[layer] = upstream + summed(pieces, contract_out[:1] if layer == 0 else ())
         if layer == 1:
             block = row_grads[layer].astype(jnp.bfloat16)
             if bits:
@@ -1245,9 +1257,6 @@
     got = swap(jnp.where(core == 0, row_grads[1], row_grads[0]))
     gradients = jnp.where(core == 0, jnp.stack([gradients, got]), jnp.stack([got, gradients]))[None]
 
-    def to_owner(first, second):
-        return (first, swap(first), swap(second), second)
-
     vector_sum = added(jnp.stack(vector_grads), "tensor")
     offset_sum = jnp.stack([ordered(item[0], item[1], core) for item in offset_grads])
     small_sum = jnp.concatenate([vector_sum.reshape(2, -1), offset_sum], axis=1)
@@ -1270,21 +1279,13 @@
 
     which = core[None]
     expand_1, heads_1 = swap(shares[1][1]), swap(shares[1][0])
-    contract_out = adam_rows(
-        3,
-        to_owner(shares[0][2], shares[1][2]),
-        viewed(contract, contract_first, contract_second),
-        (0, 0),
-        head_share,
-        which,
-    )
     vectors_out = adam_update(
         vectors, vector_grad[None], vectors_first, vectors_second, RATES[4], DECAYS[4]
     )
     offsets_out = adam_update(
         offsets, offset_grad[None], offsets_first, offsets_second, RATES[5], DECAYS[5]
     )
-    other_share = after(shares[0][0], contract_out[0])
+    other_share = after(shares[0], contract_out[0], expand_1, heads_1)
     other_0 = swap(other_share)
     expand_out = adam_columns(
         2,
@@ -1302,12 +1303,11 @@
         (count, 0),
         which,
     )
-    outward_share = after(shares[0][1], expand_out[0], inward_out[0])
     outward_out = adam_rows(
         1,
-        (outward_share, swap(outward_share), heads_1, shares[1][0]),
+        (other_share, other_0, heads_1, shares[1][0]),
         viewed(outward, outward_first, outward_second),
-        (0, 3),
+        (count + 3, 3),
         head_share,
         which,
     )

time: 1050 us -> 1040 us (level)
  Pallas kernels: 473 us -> 461 us
    reduce_scatter x6 -> x5, waiting for transfers between devices: 13.3 us -> 0.03 us  [share_of(): return lax.psum_scatter(total, 'dp', scatter_dimension=0, tiled=True)]
    pallas_call x40 -> x38, Pallas kernels: 473 us -> 461 us  [call(): pl.pallas_call(body, grid_spec=pltpu.PrefetchScalarGridSpec(num_scalar_pr...]
    ppermute x40 -> x39, waiting for transfers between devices: 24.6 us -> 31 us  [swap(): return lax.ppermute(array, 'pipe', [(0, 1), (1, 0)])]
    unnamed x190 -> x188, local copies, waits for them, and re-layouts: 24.8 us -> 20.6 us
  transfers between devices with their start and end apart: 91 -> 89, of which waited for: 48 -> 50; matrix products, arithmetic and copies ran while one was open for 7% -> 8% of each run, Pallas kernels for 45% -> 43%
where the time goes in v3:
time: 1040 us; the launch traced here: 1030 us
  Pallas kernels  461 us (44%)
  waiting for transfers between devices  374 us (36%)
  other arithmetic  62.6 us (6%)
  starting transfers between devices  49.1 us (5%)
  local copies, waits for them, and re-layouts  37.7 us (4%)
  blocking collectives  26.9 us (3%)
  between operations  15.6 us (2%)
    pallas_call x38, Pallas kernels, call(): pl.pallas_call(body, grid_spec=pltpu.PrefetchScalarGridSpec(num_scalar_pr...  461 us
    ppermute x36, waiting for transfers between devices, flipped(): lax.ppermute(array, 'tensor', [(i, i ^ 1 << bit) for i in range(peers)])  171 us
    all_gather x4, waiting for transfers between devices, whole_of(): return lax.all_gather(shard, 'dp', axis=0, tiled=True)  159 us
    ppermute x36, starting transfers between devices, flipped(): lax.ppermute(array, 'tensor', [(i, i ^ 1 << bit) for i in range(peers)])  35.5 us
    ppermute x39, waiting for transfers between devices, swap(): return lax.ppermute(array, 'pipe', [(0, 1), (1, 0)])  31 us
    all_gather x1, blocking collectives, local(): lax.all_gather(small, ('pipe', 'dp'), axis=0, tiled=False)  26.9 us
  transfers between devices with their start and end apart: 89, of which 50 were waited for; matrix products, arithmetic and copies ran while one was open for 8% of the time, Pallas kernels for 43%

profile of v3, /device:TPU:0, one launch (start us, length us, event | category | flops | bytes accessed | tf_op | source)
XLA Modules:
  0.0 1027.2 jit_solution(11733856248306557085)
XLA Ops:
  41.6 26.9 %all-gather = bf16[8,1,3072]{2,1,0:T(2,128)(2,1)S(1)} all-gather(bf16[1,1,3072]{2,1,0:T(2,128)(2,1)S(1)} %maximum_bitcast_fusion.2), channel_id=1, replica_groups=mesh['pipe'=2,'tensor'=4,'dp'=4] {'pipe','dp'}, dimensions={0}, use_global_device_ids=true | all-gather | bytes 55296 | tf_op jit(solution)/shard_map/all_gather | solution.py:1018
  74.3 10.5 %shard_map.356 = (bf16[1024,2048]{1,0:T(8,128)(2,1)}, bf16[1024,2048]{1,0:T(8,128)(2,1)}, f32[1024,1]{1,0:T(8,128)}, f32[1024,1]{1,0:T(8,128)}, bf16[2048,1024]{1,0:T(8,128)(2,1)}, /*index=5*/bf16[2048,1024]{1,0:T(8,128)(2,1)}) custom-call(s32[1]{0:T(128)} %dynamic_slice.109.info, bf16[1024,2048]{1,0:T(8,128)(2,1)} %constant_dynamic-slice_fusion.6.z_ref.refs_0_, ...), custom_call_target="tpu_custom_call" | custom-call | flops 1 | bytes 1 | tf_op jit(solution)/shard_map/pallas_call | solution.py:265
  89.5 12.4 %shard_map.358 = (bf16[1024,256]{1,0:T(8,128)(2,1)}, bf16[1024,768]{1,0:T(8,128)(2,1)}, f32[1024,1]{1,0:T(8,128)}) custom-call(s32[1]{0:T(128)} %dynamic_slice.109.info, bf16[1024,2048]{1,0:T(8,128)(2,1)} %get-tuple-element.222.x_ref, bf16[2048,768]{1,0:T(8,128)(2,1)} %all-gather.6.cloned.1.call-done.wq_ref.wk_ref.wv_ref.refs_8_, ...), custom_call_target="tpu_custom_call" | custom-call | flops 1 | bytes 1 | tf_op jit(solution)/shard_map/pallas_call | solution.py:265
  103.6 11.7 %shard_map.359 = (bf16[1024,256]{1,0:T(8,128)(2,1)}, bf16[1024,768]{1,0:T(8,128)(2,1)}, f32[1024,1]{1,0:T(8,128)}) custom-call(s32[1]{0:T(128)} %dynamic_slice.109.info, bf16[1024,2048]{1,0:T(8,128)(2,1)} %get-tuple-element.222.x_ref, bf16[2048,768]{1,0:T(8,128)(2,1)} %copy-done.1, bf16[2048,768]{1,0:T(8,128)(2,1)} %copy-done.1, ...), custom_call_target="tpu_custom_call" | custom-call | flops 1 | bytes 1 | tf_op jit(solution)/shard_map/pallas_call | solution.py:265
  115.3 134.9 %all-gather.8.cloned.1.call-done.refs_0_.refs_1_.refs_2_.refs_3_.refs_16_.refs_18_.outward_ref.refs_10_ = bf16[2048,2304]{1,0:T(8,128)(2,1)} async-done(((bf16[512,2304]{1,0:T(8,128)(2,1)}), bf16[2048,2304]{1,0:T(8,128)(2,1)}) %all-gather.8.cloned.1.call-update) | async-done | bytes 9437200 | tf_op jit(solution)/shard_map/all_gather | solution.py:1035
  253.7 10.9 %shard_map.360 = (bf16[1024,1024]{1,0:T(8,128)(2,1)}, bf16[1024,1024]{1,0:T(8,128)(2,1)}) custom-call(s32[1]{0:T(128)} %dynamic_slice.109.info, bf16[1024,2048]{1,0:T(8,128)(2,1)} %get-tuple-element.223.x_ref, bf16[2048,2304]{1,0:T(8,128)(2,1)} %all-gather.8.cloned.1.call-done.refs_0_.refs_1_.refs_2_.refs_3_.refs_16_.refs_18_.outward_ref.refs_10_, ...), custom_call_target="tpu_custom_call" | custom-call | flops 1 | bytes 1 | tf_op jit(solution)/shard_map/pallas_call | solution.py:265
  265.2 10.8 %shard_map.361 = (bf16[1024,1024]{1,0:T(8,128)(2,1)}, bf16[1024,1024]{1,0:T(8,128)(2,1)}) custom-call(s32[1]{0:T(128)} %dynamic_slice.109.info, bf16[1024,2048]{1,0:T(8,128)(2,1)} %get-tuple-element.223.x_ref, bf16[2048,2304]{1,0:T(8,128)(2,1)} %collective-permute-done.5.refs_0_.refs_1_.refs_2_.refs_3_.refs_17_.refs_19_.outward_ref.refs_11_, ...), custom_call_target="tpu_custom_call" | custom-call | flops 1 | bytes 1 | tf_op jit(solution)/shard_map/pallas_call | solution.py:265
  276.0 17.1 %shard_map.362 = (bf16[128,2048]{1,0:T(8,128)(2,1)}, bf16[128,2048]{1,0:T(8,128)(2,1)}, bf16[256,2048]{1,0:T(8,128)(2,1)}, bf16[128,2048]{1,0:T(8,128)(2,1)}, bf...) custom-call(s32[8]{0:T(128)} %stack.259.info, ...), custom_call_target="tpu_custom_call" | custom-call | flops 1 | bytes 1 | tf_op jit(solution)/shard_map/pallas_call | solution.py:265
  297.2 10.9 %collective-permute-done.6 = bf16[128,2048]{1,0:T(8,128)(2,1)S(1)} collective-permute-done((bf16[128,2048]{1,0:T(8,128)(2,1)}, bf16[128,2048]{1,0:T(8,128)(2,1)S(1)}, u32[]{:S(2)}, u32[]{:S(2)}) %collective-permute-start.6) | collective-permute-done | bytes 524320 | tf_op jit(solution)/shard_map/ppermute | solution.py:112
  308.2 10.4 %collective-permute-done.7 = bf16[128,2048]{1,0:T(8,128)(2,1)S(1)} collective-permute-done((bf16[128,2048]{1,0:T(8,128)(2,1)}, bf16[128,2048]{1,0:T(8,128)(2,1)S(1)}, u32[]{:S(2)}, u32[]{:S(2)}) %collective-permute-start.7) | collective-permute-done | bytes 524320 | tf_op jit(solution)/shard_map/ppermute | solution.py:112
  327.2 9.3 collective-permute-done.10
  346.7 10.8 %collective-permute-done.13.refs_5_ = bf16[128,2048]{1,0:T(8,128)(2,1)S(1)} collective-permute-done((bf16[128,2048]{1,0:T(8,128)(2,1)S(1)}, bf16[128,2048]{1,0:T(8,128)(2,1)S(1)}, u32[]{:S(2)}, u32[]{:S(2)}) %collective-permute-start.13) | collective-permute-done | bytes 524320 | tf_op jit(solution)/shard_map/ppermute | solution.py:112
  361.4 8.7 collective-permute-done.16.refs_6_
  377.9 13.0 %shard_map.363 = (bf16[1024,2048]{1,0:T(8,128)(2,1)}, bf16[1024,2048]{1,0:T(8,128)(2,1)}, bf16[1024,2048]{1,0:T(8,128)(2,1)}, f32[1024,1]{1,0:T(8,128)}, f32[102...) custom-call(s32[8]{0:T(128)} %stack.276.info, bf16[128,2048]{1,0:T(8,128)(2,1)} %copy-done.15, ...), custom_call_target="tpu_custom_call" | custom-call | flops 1 | bytes 1 | tf_op jit(solution)/shard_map/pallas_call | solution.py:265
  390.9 9.0 all-gather.10.cloned.1.call-done.refs_0_.refs_1_.refs_2_.refs_3_.wq_ref.wk_ref.wv_ref.outward_ref.refs_8_.refs_10_.refs_16_
  400.1 11.0 %shard_map.366 = (bf16[1024,1024]{1,0:T(8,128)(2,1)}, bf16[1024,1024]{1,0:T(8,128)(2,1)}) custom-call(s32[1]{0:T(128)} %dynamic_slice.109.info, bf16[1024,2048]{1,0:T(8,128)(2,1)} %get-tuple-element.251.x_ref, bf16[2048,2048]{1,0:T(8,128)(2,1)} %all-gather.10.cloned.1.call-done.refs_0_.refs_1_.refs_2_.refs_3_.wq_ref.wk_ref.wv_ref.outward_ref.refs_8_.refs_10_.refs_16_, ...), custom_call_target="tpu_custom_call" | custom-call | flops 1 | bytes 1 | tf_op jit(solution)/shard_map/pallas_call | solution.py:265
  411.0 10.3 %shard_map.367 = (bf16[2048,256]{1,0:T(8,128)(2,1)}, bf16[2048,256]{1,0:T(8,128)(2,1)}, bf16[2048,256]{1,0:T(8,128)(2,1)}, bf16[2048,256]{1,0:T(8,128)(2,1)}) custom-call(s32[1]{0:T(128)} %dynamic_slice.109.info, bf16[2048,1024]{1,0:T(8,128)(2,1)} %get-tuple-element.224.refs_0_.refs_1_, ...), custom_call_target="tpu_custom_call" | custom-call | flops 1 | bytes 1 | tf_op jit(solution)/shard_map/pallas_call | solution.py:265
  421.3 10.8 %shard_map.364 = (bf16[1024,1024]{1,0:T(8,128)(2,1)}, bf16[1024,1024]{1,0:T(8,128)(2,1)}) custom-call(s32[1]{0:T(128)} %dynamic_slice.109.info, bf16[1024,2048]{1,0:T(8,128)(2,1)} %get-tuple-element.251.x_ref, bf16[2048,2048]{1,0:T(8,128)(2,1)} %collective-permute-done.18.refs_0_.refs_1_.refs_2_.refs_3_.wq_ref.wk_ref.wv_ref.outward_ref.refs_9_.refs_11_.refs_17_, ...), custom_call_target="tpu_custom_call" | custom-call | flops 1 | bytes 1 | tf_op jit(solution)/shard_map/pallas_call | solution.py:265
  432.1 10.3 %shard_map.365 = (bf16[2048,256]{1,0:T(8,128)(2,1)}, bf16[2048,256]{1,0:T(8,128)(2,1)}, bf16[2048,256]{1,0:T(8,128)(2,1)}, bf16[2048,256]{1,0:T(8,128)(2,1)}) custom-call(s32[1]{0:T(128)} %dynamic_slice.109.info, bf16[2048,1024]{1,0:T(8,128)(2,1)} %get-tuple-element.224.refs_0_.refs_1_, ...), custom_call_target="tpu_custom_call" | custom-call | flops 1 | bytes 1 | tf_op jit(solution)/shard_map/pallas_call | solution.py:265
  442.4 11.6 %shard_map.368 = (bf16[1024,256]{1,0:T(8,128)(2,1)}, bf16[1024,768]{1,0:T(8,128)(2,1)}, f32[1024,1]{1,0:T(8,128)}) custom-call(s32[1]{0:T(128)} %dynamic_slice.109.info, bf16[1024,2048]{1,0:T(8,128)(2,1)} %get-tuple-element.264.x_ref, ...), custom_call_target="tpu_custom_call" | custom-call | flops 1 | bytes 1 | tf_op jit(solution)/shard_map/pallas_call | solution.py:265
  454.1 11.9 %shard_map.369 = (bf16[1024,256]{1,0:T(8,128)(2,1)}, bf16[1024,768]{1,0:T(8,128)(2,1)}, f32[1024,1]{1,0:T(8,128)}) custom-call(s32[1]{0:T(128)} %dynamic_slice.109.info, bf16[1024,2048]{1,0:T(8,128)(2,1)} %get-tuple-element.264.x_ref, ...), custom_call_target="tpu_custom_call" | custom-call | flops 1 | bytes 1 | tf_op jit(solution)/shard_map/pallas_call | solution.py:265
  465.9 15.0 %all-gather.12.cloned.1.call-done.refs_0_.refs_1_.refs_2_.refs_3_.refs_18_ = bf16[2048,1024]{1,0:T(8,128)(2,1)} async-done(((bf16[512,1024]{1,0:T(8,128)(2,1)}), bf16[2048,1024]{1,0:T(8,128)(2,1)}) %all-gather.12.cloned.1.call-update) | async-done | bytes 4194320 | tf_op jit(solution)/shard_map/all_gather | solution.py:1035
  481.5 11.3 %shard_map.370 = (bf16[1024,256]{1,0:T(8,128)(2,1)}, bf16[1024,1024]{1,0:T(8,128)(2,1)}, f32[1,1024]{1,0:T(1,128)}) custom-call(s32[1]{0:T(128)} %dynamic_slice.109.info, bf16[1024,2048]{1,0:T(8,128)(2,1)} %get-tuple-element.293.g_ref, ...), custom_call_target="tpu_custom_call" | custom-call | flops 17179869184 | bytes 16777216 | tf_op jit(solution)/shard_map/pallas_call | solution.py:265
  509.2 10.9 %shard_map.372 = (bf16[1024,256]{1,0:T(8,128)(2,1)}, bf16[1024,1024]{1,0:T(8,128)(2,1)}, f32[1,1024]{1,0:T(1,128)}) custom-call(s32[1]{0:T(128)} %dynamic_slice.109.info, bf16[1024,2048]{1,0:T(8,128)(2,1)} %get-tuple-element.293.g_ref, ...), custom_call_target="tpu_custom_call" | custom-call | flops 1 | bytes 1 | tf_op jit(solution)/shard_map/pallas_call | solution.py:265
  520.1 10.3 %shard_map.373 = (bf16[2048,256]{1,0:T(8,128)(2,1)}, bf16[2048,256]{1,0:T(8,128)(2,1)}, bf16[2048,256]{1,0:T(8,128)(2,1)}, bf16[2048,256]{1,0:T(8,128)(2,1)}) custom-call(s32[1]{0:T(128)} %dynamic_slice.109.info, bf16[2048,1024]{1,0:T(8,128)(2,1)} %get-tuple-element.296.refs_0_, ...), custom_call_target="tpu_custom_call" | custom-call | flops 1 | bytes 1 | tf_op jit(solution)/shard_map/pallas_call | solution.py:265
  541.8 11.5 %shard_map.374 = bf16[2048,1024]{1,0:T(8,128)(2,1)} custom-call(s32[1]{0:T(128)} %dynamic_slice.109.info, bf16[2048,1024]{1,0:T(8,128)(2,1)} %get-tuple-element.296.refs_0_, bf16[1024,1024]{1,0:T(8,128)(2,1)} %get-tuple-element.297.refs_1_.refs_2_.refs_3_.refs_4_.refs_6_, bf16[1024,1024]{1,0:T(8,128)(2,1)} %get-tuple-element.297.refs_1_.refs_2_.refs_3_.refs_4_.refs_6_, ...), custom_call_target="tpu_custom_call" | custom-call | flops 1 | bytes 1 | tf_op jit(solution)/shard_map/pallas_call | solution.py:265
  562.1 31.0 %shard_map.376 = (bf16[128,2048]{1,0:T(8,128)(2,1)}, bf16[128,2048]{1,0:T(8,128)(2,1)}, bf16[256,2048]{1,0:T(8,128)(2,1)}, bf16[128,2048]{1,0:T(8,128)(2,1)}, bf...) custom-call(s32[16]{0:T(128)} %stack.282.info, ...), custom_call_target="tpu_custom_call" | custom-call | flops 1 | bytes 1 | tf_op jit(solution)/shard_map/pallas_call | solution.py:265
  593.0 11.1 %shard_map.381 = (bf16[2048,256]{1,0:T(8,128)(2,1)}, bf16[2048,256]{1,0:T(8,128)(2,1)}, bf16[2048,256]{1,0:T(8,128)(2,1)}, bf16[2048,256]{1,0:T(8,128)(2,1)}) custom-call(s32[1]{0:T(128)} %dynamic_slice.109.info, bf16[2048,1024]{1,0:T(8,128)(2,1)} %get-tuple-element.349.refs_0_, bf16[2048,1024]{1,0:T(8,128)(2,1)} %get-tuple-element.224.refs_0_.refs_1_, ...), custom_call_target="tpu_custom_call" | custom-call | flops 17179869184 | bytes 16777216 | tf_op jit(solution)/shard_map/pallas_call | solution.py:265
  612.4 12.4 %shard_map.382 = bf16[2048,1024]{1,0:T(8,128)(2,1)} custom-call(s32[1]{0:T(128)} %dynamic_slice.109.info, bf16[2048,1024]{1,0:T(8,128)(2,1)} %get-tuple-element.349.refs_0_, bf16[2048,1024]{1,0:T(8,128)(2,1)} %get-tuple-element.224.refs_0_.refs_1_, bf16[1024,768]{1,0:T(8,128)(2,1)} %shard_map.371.refs_4_.refs_2_.refs_3_, ...), custom_call_target="tpu_custom_call" | custom-call | flops 17179869184 | bytes 16777216 | tf_op jit(solution)/shard_map/pallas_call | solution.py:265
  629.5 10.9 %collective-permute-done.31 = bf16[128,2048]{1,0:T(8,128)(2,1)S(1)} collective-permute-done((bf16[128,2048]{1,0:T(8,128)(2,1)}, bf16[128,2048]{1,0:T(8,128)(2,1)S(1)}, u32[]{:S(2)}, u32[]{:S(2)}) %collective-permute-start.31) | collective-permute-done | bytes 524320 | tf_op jit(solution)/shard_map/ppermute | solution.py:112
  640.5 10.4 %collective-permute-done.30 = bf16[128,2048]{1,0:T(8,128)(2,1)S(1)} collective-permute-done((bf16[128,2048]{1,0:T(8,128)(2,1)}, bf16[128,2048]{1,0:T(8,128)(2,1)S(1)}, u32[]{:S(2)}, u32[]{:S(2)}) %collective-permute-start.30) | collective-permute-done | bytes 524320 | tf_op jit(solution)/shard_map/ppermute | solution.py:112
  656.5 8.9 collective-permute-done.32
  673.7 10.8 %collective-permute-done.35.refs_5_ = bf16[128,2048]{1,0:T(8,128)(2,1)S(1)} collective-permute-done((bf16[128,2048]{1,0:T(8,128)(2,1)S(1)}, bf16[128,2048]{1,0:T(8,128)(2,1)S(1)}, u32[]{:S(2)}, u32[]{:S(2)}) %collective-permute-start.35) | collective-permute-done | bytes 524320 | tf_op jit(solution)/shard_map/ppermute | solution.py:112
  687.1 10.1 collective-permute-done.38.refs_6_
  712.7 10.3 shard_map.378
  731.4 11.5 %shard_map.379 = bf16[2048,1024]{1,0:T(8,128)(2,1)} custom-call(s32[1]{0:T(128)} %dynamic_slice.109.info, bf16[2048,1024]{1,0:T(8,128)(2,1)} %get-tuple-element.339.refs_0_.refs_2_, bf16[1024,1024]{1,0:T(8,128)(2,1)} %get-tuple-element.230.refs_8_.refs_9_.refs_10_.refs_11_.refs_1_.refs_2_.refs_3_.refs_4_, ...), custom_call_target="tpu_custom_call" | custom-call | flops 1 | bytes 1 | tf_op jit(solution)/shard_map/pallas_call | solution.py:265
  743.1 10.9 %shard_map.384 = (bf16[1024,256]{1,0:T(8,128)(2,1)}, bf16[1024,1024]{1,0:T(8,128)(2,1)}, f32[1,1024]{1,0:T(1,128)}) custom-call(s32[1]{0:T(128)} %dynamic_slice.109.info, bf16[1024,2048]{1,0:T(8,128)(2,1)} %get-tuple-element.345.g_ref, bf16[2048,2304]{1,0:T(8,128)(2,1)} %collective-permute-done.5.refs_0_.refs_1_.refs_2_.refs_3_.refs_17_.refs_19_.outward_ref.refs_11_, ...), custom_call_target="tpu_custom_call" | custom-call | flops 1 | bytes 1 | tf_op jit(solution)/shard_map/pallas_call | solution.py:265
  761.8 15.2 %shard_map.386 = (bf16[2048,256]{1,0:T(8,128)(2,1)}, bf16[2048,256]{1,0:T(8,128)(2,1)}, bf16[2048,256]{1,0:T(8,128)(2,1)}, bf16[2048,256]{1,0:T(8,128)(2,1)}, bf...) custom-call(s32[1]{0:T(128)} %dynamic_slice.109.info, ...), custom_call_target="tpu_custom_call" | custom-call | flops 1 | bytes 1 | tf_op jit(solution)/shard_map/pallas_call | solution.py:265
  784.6 11.0 %shard_map.380 = (bf16[1024,256]{1,0:T(8,128)(2,1)}, bf16[1024,1024]{1,0:T(8,128)(2,1)}, f32[1,1024]{1,0:T(1,128)}) custom-call(s32[1]{0:T(128)} %dynamic_slice.109.info, bf16[1024,2048]{1,0:T(8,128)(2,1)} %get-tuple-element.345.g_ref, bf16[2048,2304]{1,0:T(8,128)(2,1)} %all-gather.8.cloned.1.call-done.refs_0_.refs_1_.refs_2_.refs_3_.refs_16_.refs_18_.outward_ref.refs_10_, ...), custom_call_target="tpu_custom_call" | custom-call | flops 1 | bytes 1 | tf_op jit(solution)/shard_map/pallas_call | solution.py:265
  804.7 18.2 %shard_map.387 = bf16[2048,2048]{1,0:T(8,128)(2,1)} custom-call(s32[1]{0:T(128)} %dynamic_slice.109.info, bf16[2048,1024]{1,0:T(8,128)(2,1)} %get-tuple-element.267.refs_0_, bf16[2048,1024]{1,0:T(8,128)(2,1)} %get-tuple-element.268.refs_1_, bf16[2048,1024]{1,0:T(8,128)(2,1)} %get-tuple-element.339.refs_0_.refs_2_, ...), custom_call_target="tpu_custom_call" | custom-call | flops 1 | bytes 1 | tf_op jit(solution)/shard_map/pallas_call | solution.py:265
  823.0 31.2 %shard_map.388 = (bf16[128,2048]{1,0:T(8,128)(2,1)}, bf16[128,2048]{1,0:T(8,128)(2,1)}, bf16[256,2048]{1,0:T(8,128)(2,1)}, bf16[128,2048]{1,0:T(8,128)(2,1)}, bf...) custom-call(s32[16]{0:T(128)} %stack.282.info, ...), custom_call_target="tpu_custom_call" | custom-call | flops 1 | bytes 1 | tf_op jit(solution)/shard_map/pallas_call | solution.py:265
  854.2 17.3 %shard_map.389 = (bf16[128,2048]{1,0:T(8,128)(2,1)}, bf16[128,2048]{1,0:T(8,128)(2,1)}, bf16[256,2048]{1,0:T(8,128)(2,1)}, bf16[128,2048]{1,0:T(8,128)(2,1)}, bf...) custom-call(s32[8]{0:T(128)} %stack.259.info, ...), custom_call_target="tpu_custom_call" | custom-call | flops 1 | bytes 1 | tf_op jit(solution)/shard_map/pallas_call | solution.py:265
  876.5 10.1 collective-permute-done.56
  887.2 10.6 %collective-permute-done.57 = bf16[128,2048]{1,0:T(8,128)(2,1)S(1)} collective-permute-done((bf16[128,2048]{1,0:T(8,128)(2,1)}, bf16[128,2048]{1,0:T(8,128)(2,1)S(1)}, u32[]{:S(2)}, u32[]{:S(2)}) %collective-permute-start.57) | collective-permute-done | bytes 524320 | tf_op jit(solution)/shard_map/ppermute | solution.py:112
  909.5 10.2 collective-permute-done.64
  940.3 13.8 %shard_map.390 = (f32[2048,512]{1,0:T(8,128)}, f32[2048,512]{1,0:T(8,128)}, f32[2048,512]{1,0:T(8,128)}) custom-call(s32[1]{0:T(128)} %bitcast.14.info, bf16[512,1024]{1,0:T(8,128)(2,1)} %reduce-scatter.12.cloned.1.call-done.refs_0_, bf16[512,1024]{1,0:T(8,128)(2,1)} %copy-done.32, bf16[512,1024]{1,0:T(8,128)(2,1)} %collective-permute-done.70.refs_2_, ...), custom_call_target="tpu_custom_call" | custom-call | flops 1 | bytes 1 | tf_op jit(solution)/shard_map/pallas_call | solution.py:265
  996.1 10.1 shard_map.393
  1010.1 10.2 shard_map.391
  (457 shorter events, 283.0 us)
Async XLA Ops:
  7.2 77.6 %all-gather.6.cloned.1.call-start = ((), (), s32[]{:S(2)}) async-start(), calls=%async_computation.5 | async-start | bytes 3932160 | tf_op jit(solution)/shard_map/all_gather | solution.py:1035
  14.6 235.6 %all-gather.8.cloned.1.call-start = ((), (), s32[]{:S(2)}) async-start(), calls=%async_computation.6 | async-start | bytes 11796480 | tf_op jit(solution)/shard_map/all_gather | solution.py:1035
  32.3 367.7 %all-gather.10.cloned.1.call-start = ((), (), s32[]{:S(2)}) async-start(), calls=%async_computation.7 | async-start | bytes 10485760 | tf_op jit(solution)/shard_map/all_gather | solution.py:1035
  84.8 17.2 %collective-permute-start.1 = (bf16[2048,768]{1,0:T(8,128)(2,1)}, bf16[2048,768]{1,0:T(8,128)(2,1)S(1)}, u32[]{:S(2)}, u32[]{:S(2)}) collective-permute-start(bf16[2048,768]{1,0:T(8,128)(2,1)} %all-gather.6.cloned.1.call-done.wq_ref.wk_ref.wv_ref.refs_8_), channel_id=1, source_target_pairs={{0,16},{16,0},{1,17},{17,1},{2,18},{18,2},{3,19},{19,3},{4,20},{20... | collective-permute-start | bytes 9437192 | tf_op jit(solution)/shard_map/ppermute | solution.py:92
  251.9 229.1 %all-gather.12.cloned.1.call-start = ((), (), s32[]{:S(2)}) async-start(), calls=%async_computation.8 | async-start | bytes 5242880 | tf_op jit(solution)/shard_map/all_gather | solution.py:1035
  293.1 15.0 %collective-permute-start.6 = (bf16[128,2048]{1,0:T(8,128)(2,1)}, bf16[128,2048]{1,0:T(8,128)(2,1)S(1)}, u32[]{:S(2)}, u32[]{:S(2)}) collective-permute-start(bf16[128,2048]{1,0:T(8,128)(2,1)} %get-tuple-element.233), channel_id=1, source_target_pairs={{0,4},{4,0},{8,12},{12,8},{1,5},{5,1},{9,13},{13,9},{2,6},{6,2},{1... | collective-permute-start | bytes 1572872 | tf_op jit(solution)/shard_map/ppermute | solution.py:112
  294.7 23.9 %collective-permute-start.7 = (bf16[128,2048]{1,0:T(8,128)(2,1)}, bf16[128,2048]{1,0:T(8,128)(2,1)S(1)}, u32[]{:S(2)}, u32[]{:S(2)}) collective-permute-start(bf16[128,2048]{1,0:T(8,128)(2,1)} %get-tuple-element.234), channel_id=1, source_target_pairs={{0,4},{4,0},{8,12},{12,8},{1,5},{5,1},{9,13},{13,9},{2,6},{6,2},{1... | collective-permute-start | bytes 1572872 | tf_op jit(solution)/shard_map/ppermute | solution.py:112
  295.2 23.4 %collective-permute-start.8 = (bf16[128,2048]{1,0:T(8,128)(2,1)}, bf16[128,2048]{1,0:T(8,128)(2,1)S(1)}, u32[]{:S(2)}, u32[]{:S(2)}) collective-permute-start(bf16[128,2048]{1,0:T(8,128)(2,1)} %get-tuple-element.235), channel_id=1, source_target_pairs={{0,8},{4,12},{8,0},{12,4},{1,9},{5,13},{9,1},{13,5},{2,10},{6,14},... | collective-permute-start | bytes 1572872 | tf_op jit(solution)/shard_map/ppermute | solution.py:112
  296.7 23.4 %collective-permute-start.9 = (bf16[128,2048]{1,0:T(8,128)(2,1)}, bf16[128,2048]{1,0:T(8,128)(2,1)S(1)}, u32[]{:S(2)}, u32[]{:S(2)}) collective-permute-start(bf16[128,2048]{1,0:T(8,128)(2,1)} %get-tuple-element.236), channel_id=1, source_target_pairs={{0,8},{4,12},{8,0},{12,4},{1,9},{5,13},{9,1},{13,5},{2,10},{6,14},... | collective-permute-start | bytes 1572872 | tf_op jit(solution)/shard_map/ppermute | solution.py:112
  344.6 25.5 %collective-permute-start.16 = (bf16[128,2048]{1,0:T(8,128)(2,1)S(1)}, bf16[128,2048]{1,0:T(8,128)(2,1)S(1)}, u32[]{:S(2)}, u32[]{:S(2)}) collective-permute-start(bf16[128,2048]{1,0:T(8,128)(2,1)S(1)} %get-tuple-element.520.refs_4_), channel_id=1, source_target_pairs={{0,8},{4,12},{8,0},{12,4},{1,9},{5,13},{9,1},{13,5},{2,10},{6,14},... | collective-permute-start | bytes 1572872 | tf_op jit(solution)/shard_map/ppermute | solution.py:112
  346.0 24.1 %collective-permute-start.14 = (bf16[128,2048]{1,0:T(8,128)(2,1)S(1)}, bf16[128,2048]{1,0:T(8,128)(2,1)S(1)}, u32[]{:S(2)}, u32[]{:S(2)}) collective-permute-start(bf16[128,2048]{1,0:T(8,128)(2,1)S(1)} %get-tuple-element.521.refs_0_), channel_id=1, source_target_pairs={{0,4},{4,0},{8,12},{12,8},{1,5},{5,1},{9,13},{13,9},{2,6},{6,2},{1... | collective-permute-start | bytes 1572872 | tf_op jit(solution)/shard_map/ppermute | solution.py:112
  358.9 17.8 %collective-permute-start.15 = (bf16[128,2048]{1,0:T(8,128)(2,1)S(1)}, bf16[128,2048]{1,0:T(8,128)(2,1)}, u32[]{:S(2)}, u32[]{:S(2)}) collective-permute-start(bf16[128,2048]{1,0:T(8,128)(2,1)S(1)} %collective-permute-done.12.refs_1_), channel_id=1, source_target_pairs={{0,4},{4,0},{8,12},{12,8},{1,5},{5,1},{9,13},{13,9},{2,6},{6,2},{1... | collective-permute-start | bytes 1572872 | tf_op jit(solution)/shard_map/ppermute | solution.py:112
  359.5 18.3 %collective-permute-start.17 = (bf16[128,2048]{1,0:T(8,128)(2,1)S(1)}, bf16[128,2048]{1,0:T(8,128)(2,1)}, u32[]{:S(2)}, u32[]{:S(2)}) collective-permute-start(bf16[128,2048]{1,0:T(8,128)(2,1)S(1)} %collective-permute-done.13.refs_5_), channel_id=1, source_target_pairs={{0,8},{4,12},{8,0},{12,4},{1,9},{5,13},{9,1},{13,5},{2,10},{6,14},... | collective-permute-start | bytes 1572872 | tf_op jit(solution)/shard_map/ppermute | solution.py:112
  399.9 21.4 %collective-permute-start.18 = (bf16[2048,2048]{1,0:T(8,128)(2,1)}, bf16[2048,2048]{1,0:T(8,128)(2,1)}, u32[]{:S(2)}, u32[]{:S(2)}) collective-permute-start(bf16[2048,2048]{1,0:T(8,128)(2,1)} %all-gather.10.cloned.1.call-done.refs_0_.refs_1_.refs_2_.refs_3_.wq_ref.wk_ref.wv_ref.outward_ref.refs_8_.refs_10_.r, ...), channel_id=1, source_target_pairs={{0,16},{16,0},{1,17},{17,1},{2,18},{18,2},{3,19},{19,3},{4,20},{20... | collective-permute-start | bytes 25165832 | tf_op jit(solution)/shard_map/ppermute | solution.py:92
  400.0 225.4 %reduce-scatter.6.cloned.1.call-start = ((), (), s32[]{:S(2)}) async-start(), calls=%async_computation.9 | async-start | bytes 5242880 | tf_op jit(solution)/shard_map/reduce_scatter | solution.py:892
  499.7 205.1 %reduce-scatter.8.cloned.1.call-start = ((), (), s32[]{:S(2)}) async-start(), calls=%async_computation.10 | async-start | bytes 5242880 | tf_op jit(solution)/shard_map/reduce_scatter | solution.py:892
  553.4 208.5 %reduce-scatter.10.cloned.1.call-start = ((), (), s32[]{:S(2)}) async-start(), calls=%async_computation.11 | async-start | bytes 5242880 | tf_op jit(solution)/shard_map/reduce_scatter | solution.py:892
  624.9 302.7 %reduce-scatter.12.cloned.1.call-start = ((), (), s32[]{:S(2)}) async-start(), calls=%async_computation.12 | async-start | bytes 5242880 | tf_op jit(solution)/shard_map/reduce_scatter | solution.py:892
  625.4 15.1 %collective-permute-start.31 = (bf16[128,2048]{1,0:T(8,128)(2,1)}, bf16[128,2048]{1,0:T(8,128)(2,1)S(1)}, u32[]{:S(2)}, u32[]{:S(2)}) collective-permute-start(bf16[128,2048]{1,0:T(8,128)(2,1)} %get-tuple-element.316), channel_id=1, source_target_pairs={{0,8},{4,12},{8,0},{12,4},{1,9},{5,13},{9,1},{13,5},{2,10},{6,14},... | collective-permute-start | bytes 1572872 | tf_op jit(solution)/shard_map/ppermute | solution.py:112
  627.0 23.9 %collective-permute-start.30 = (bf16[128,2048]{1,0:T(8,128)(2,1)}, bf16[128,2048]{1,0:T(8,128)(2,1)S(1)}, u32[]{:S(2)}, u32[]{:S(2)}) collective-permute-start(bf16[128,2048]{1,0:T(8,128)(2,1)} %get-tuple-element.314), channel_id=1, source_target_pairs={{0,8},{4,12},{8,0},{12,4},{1,9},{5,13},{9,1},{13,5},{2,10},{6,14},... | collective-permute-start | bytes 1572872 | tf_op jit(solution)/shard_map/ppermute | solution.py:112
  627.5 23.4 %collective-permute-start.29 = (bf16[128,2048]{1,0:T(8,128)(2,1)S(1)}, bf16[128,2048]{1,0:T(8,128)(2,1)S(1)}, u32[]{:S(2)}, u32[]{:S(2)}) collective-permute-start(bf16[128,2048]{1,0:T(8,128)(2,1)S(1)} %copy-done.84), channel_id=1, source_target_pairs={{0,4},{4,0},{8,12},{12,8},{1,5},{5,1},{9,13},{13,9},{2,6},{6,2},{1... | collective-permute-start | bytes 1572872 | tf_op jit(solution)/shard_map/ppermute | solution.py:112
  629.1 23.1 %collective-permute-start.28 = (bf16[128,2048]{1,0:T(8,128)(2,1)S(1)}, bf16[128,2048]{1,0:T(8,128)(2,1)S(1)}, u32[]{:S(2)}, u32[]{:S(2)}) collective-permute-start(bf16[128,2048]{1,0:T(8,128)(2,1)S(1)} %copy-done.83), channel_id=1, source_target_pairs={{0,4},{4,0},{8,12},{12,8},{1,5},{5,1},{9,13},{13,9},{2,6},{6,2},{1... | collective-permute-start | bytes 1572872 | tf_op jit(solution)/shard_map/ppermute | solution.py:112
  671.7 25.5 %collective-permute-start.38 = (bf16[128,2048]{1,0:T(8,128)(2,1)S(1)}, bf16[128,2048]{1,0:T(8,128)(2,1)S(1)}, u32[]{:S(2)}, u32[]{:S(2)}) collective-permute-start(bf16[128,2048]{1,0:T(8,128)(2,1)S(1)} %get-tuple-element.333.refs_4_), channel_id=1, source_target_pairs={{0,8},{4,12},{8,0},{12,4},{1,9},{5,13},{9,1},{13,5},{2,10},{6,14},... | collective-permute-start | bytes 1572872 | tf_op jit(solution)/shard_map/ppermute | solution.py:112
  673.1 24.1 %collective-permute-start.36 = (bf16[128,2048]{1,0:T(8,128)(2,1)S(1)}, bf16[128,2048]{1,0:T(8,128)(2,1)S(1)}, u32[]{:S(2)}, u32[]{:S(2)}) collective-permute-start(bf16[128,2048]{1,0:T(8,128)(2,1)S(1)} %get-tuple-element.325.refs_0_), channel_id=1, source_target_pairs={{0,4},{4,0},{8,12},{12,8},{1,5},{5,1},{9,13},{13,9},{2,6},{6,2},{1... | collective-permute-start | bytes 1572872 | tf_op jit(solution)/shard_map/ppermute | solution.py:112
  686.0 17.5 %collective-permute-start.37 = (bf16[128,2048]{1,0:T(8,128)(2,1)S(1)}, bf16[128,2048]{1,0:T(8,128)(2,1)S(1)}, u32[]{:S(2)}, u32[]{:S(2)}) collective-permute-start(bf16[128,2048]{1,0:T(8,128)(2,1)S(1)} %collective-permute-done.34.refs_1_), channel_id=1, source_target_pairs={{0,4},{4,0},{8,12},{12,8},{1,5},{5,1},{9,13},{13,9},{2,6},{6,2},{1... | collective-permute-start | bytes 1572872 | tf_op jit(solution)/shard_map/ppermute | solution.py:112
  686.5 18.2 %collective-permute-start.39 = (bf16[128,2048]{1,0:T(8,128)(2,1)S(1)}, bf16[128,2048]{1,0:T(8,128)(2,1)}, u32[]{:S(2)}, u32[]{:S(2)}) collective-permute-start(bf16[128,2048]{1,0:T(8,128)(2,1)S(1)} %collective-permute-done.35.refs_5_), channel_id=1, source_target_pairs={{0,8},{4,12},{8,0},{12,4},{1,9},{5,13},{9,1},{13,5},{2,10},{6,14},... | collective-permute-start | bytes 1572872 | tf_op jit(solution)/shard_map/ppermute | solution.py:112
  742.9 231.1 %reduce-scatter.14.cloned.1.call-start = ((), (), s32[]{:S(2)}) async-start(), calls=%async_computation.13 | async-start | bytes 10485760 | tf_op jit(solution)/shard_map/reduce_scatter | solution.py:892
  777.7 25.7 %collective-permute-start.51 = (bf16[2048,256]{1,0:T(8,128)(2,1)}, bf16[2048,256]{1,0:T(8,128)(2,1)S(1)}, u32[]{:S(2)}, u32[]{:S(2)}) collective-permute-start(bf16[2048,256]{1,0:T(8,128)(2,1)} %get-tuple-element.368), channel_id=1, source_target_pairs={{0,16},{16,0},{1,17},{17,1},{2,18},{18,2},{3,19},{19,3},{4,20},{20... | collective-permute-start | bytes 3145736 | tf_op jit(solution)/shard_map/ppermute | solution.py:92
  778.1 25.2 %collective-permute-start.52 = (bf16[2048,256]{1,0:T(8,128)(2,1)}, bf16[2048,256]{1,0:T(8,128)(2,1)S(1)}, u32[]{:S(2)}, u32[]{:S(2)}) collective-permute-start(bf16[2048,256]{1,0:T(8,128)(2,1)} %get-tuple-element.369), channel_id=1, source_target_pairs={{0,16},{16,0},{1,17},{17,1},{2,18},{18,2},{3,19},{19,3},{4,20},{20... | collective-permute-start | bytes 3145736 | tf_op jit(solution)/shard_map/ppermute | solution.py:92
  780.0 23.4 %collective-permute-start.53 = (bf16[2048,256]{1,0:T(8,128)(2,1)}, bf16[2048,256]{1,0:T(8,128)(2,1)}, u32[]{:S(2)}, u32[]{:S(2)}) collective-permute-start(bf16[2048,256]{1,0:T(8,128)(2,1)} %get-tuple-element.370), channel_id=1, source_target_pairs={{0,16},{16,0},{1,17},{17,1},{2,18},{18,2},{3,19},{19,3},{4,20},{20... | collective-permute-start | bytes 3145736 | tf_op jit(solution)/shard_map/ppermute | solution.py:92
  781.5 21.9 %collective-permute-start.54 = (bf16[2048,256]{1,0:T(8,128)(2,1)}, bf16[2048,256]{1,0:T(8,128)(2,1)}, u32[]{:S(2)}, u32[]{:S(2)}) collective-permute-start(bf16[2048,256]{1,0:T(8,128)(2,1)} %get-tuple-element.371), channel_id=1, source_target_pairs={{0,16},{16,0},{1,17},{17,1},{2,18},{18,2},{3,19},{19,3},{4,20},{20... | collective-permute-start | bytes 3145736 | tf_op jit(solution)/shard_map/ppermute | solution.py:92
  784.5 18.9 %collective-permute-start.55 = (bf16[2048,256]{1,0:T(8,128)(2,1)}, bf16[2048,256]{1,0:T(8,128)(2,1)}, u32[]{:S(2)}, u32[]{:S(2)}) collective-permute-start(bf16[2048,256]{1,0:T(8,128)(2,1)} %get-tuple-element.372), channel_id=1, source_target_pairs={{0,16},{16,0},{1,17},{17,1},{2,18},{18,2},{3,19},{19,3},{4,20},{20... | collective-permute-start | bytes 3145736 | tf_op jit(solution)/shard_map/ppermute | solution.py:92
  871.6 15.0 %collective-permute-start.56 = (bf16[128,2048]{1,0:T(8,128)(2,1)}, bf16[128,2048]{1,0:T(8,128)(2,1)S(1)}, u32[]{:S(2)}, u32[]{:S(2)}) collective-permute-start(bf16[128,2048]{1,0:T(8,128)(2,1)} %get-tuple-element.387), channel_id=1, source_target_pairs={{0,4},{4,0},{8,12},{12,8},{1,5},{5,1},{9,13},{13,9},{2,6},{6,2},{1... | collective-permute-start | bytes 1572872 | tf_op jit(solution)/shard_map/ppermute | solution.py:112
  872.2 25.6 %collective-permute-start.57 = (bf16[128,2048]{1,0:T(8,128)(2,1)}, bf16[128,2048]{1,0:T(8,128)(2,1)S(1)}, u32[]{:S(2)}, u32[]{:S(2)}) collective-permute-start(bf16[128,2048]{1,0:T(8,128)(2,1)} %get-tuple-element.388), channel_id=1, source_target_pairs={{0,4},{4,0},{8,12},{12,8},{1,5},{5,1},{9,13},{13,9},{2,6},{6,2},{1... | collective-permute-start | bytes 1572872 | tf_op jit(solution)/shard_map/ppermute | solution.py:112
  873.7 24.8 %collective-permute-start.58 = (bf16[128,2048]{1,0:T(8,128)(2,1)}, bf16[128,2048]{1,0:T(8,128)(2,1)S(1)}, u32[]{:S(2)}, u32[]{:S(2)}) collective-permute-start(bf16[128,2048]{1,0:T(8,128)(2,1)} %get-tuple-element.389), channel_id=1, source_target_pairs={{0,8},{4,12},{8,0},{12,4},{1,9},{5,13},{9,1},{13,5},{2,10},{6,14},... | collective-permute-start | bytes 1572872 | tf_op jit(solution)/shard_map/ppermute | solution.py:112
  874.1 25.2 %collective-permute-start.59 = (bf16[128,2048]{1,0:T(8,128)(2,1)}, bf16[128,2048]{1,0:T(8,128)(2,1)S(1)}, u32[]{:S(2)}, u32[]{:S(2)}) collective-permute-start(bf16[128,2048]{1,0:T(8,128)(2,1)} %get-tuple-element.390), channel_id=1, source_target_pairs={{0,8},{4,12},{8,0},{12,4},{1,9},{5,13},{9,1},{13,5},{2,10},{6,14},... | collective-permute-start | bytes 1572872 | tf_op jit(solution)/shard_map/ppermute | solution.py:112
  876.4 62.4 %collective-permute-start.70 = (bf16[512,1024]{1,0:T(8,128)(2,1)}, bf16[512,1024]{1,0:T(8,128)(2,1)}, u32[]{:S(2)}, u32[]{:S(2)}) collective-permute-start(bf16[512,1024]{1,0:T(8,128)(2,1)} %reduce-scatter.6.cloned.1.call-done.refs_3_), channel_id=1, source_target_pairs={{0,16},{16,0},{1,17},{17,1},{2,18},{18,2},{3,19},{19,3},{4,20},{20... | collective-permute-start | bytes 3145736 | tf_op jit(solution)/shard_map/ppermute | solution.py:92
  886.6 22.5 %collective-permute-start.63 = (bf16[128,2048]{1,0:T(8,128)(2,1)S(1)}, bf16[128,2048]{1,0:T(8,128)(2,1)S(1)}, u32[]{:S(2)}, u32[]{:S(2)}) collective-permute-start(bf16[128,2048]{1,0:T(8,128)(2,1)S(1)} %copy-done.82), channel_id=1, source_target_pairs={{0,4},{4,0},{8,12},{12,8},{1,5},{5,1},{9,13},{13,9},{2,6},{6,2},{1... | collective-permute-start | bytes 1572872 | tf_op jit(solution)/shard_map/ppermute | solution.py:112
  897.8 21.9 %collective-permute-start.64 = (bf16[128,2048]{1,0:T(8,128)(2,1)S(1)}, bf16[128,2048]{1,0:T(8,128)(2,1)S(1)}, u32[]{:S(2)}, u32[]{:S(2)}) collective-permute-start(bf16[128,2048]{1,0:T(8,128)(2,1)S(1)} %copy-done.81), channel_id=1, source_target_pairs={{0,4},{4,0},{8,12},{12,8},{1,5},{5,1},{9,13},{13,9},{2,6},{6,2},{1... | collective-permute-start | bytes 1572872 | tf_op jit(solution)/shard_map/ppermute | solution.py:112
  898.5 21.8 %collective-permute-start.65 = (bf16[128,2048]{1,0:T(8,128)(2,1)S(1)}, bf16[128,2048]{1,0:T(8,128)(2,1)S(1)}, u32[]{:S(2)}, u32[]{:S(2)}) collective-permute-start(bf16[128,2048]{1,0:T(8,128)(2,1)S(1)} %copy-done.80), channel_id=1, source_target_pairs={{0,8},{4,12},{8,0},{12,4},{1,9},{5,13},{9,1},{13,5},{2,10},{6,14},... | collective-permute-start | bytes 1572872 | tf_op jit(solution)/shard_map/ppermute | solution.py:112
  899.3 25.3 %collective-permute-start.66 = (bf16[128,2048]{1,0:T(8,128)(2,1)S(1)}, bf16[128,2048]{1,0:T(8,128)(2,1)S(1)}, u32[]{:S(2)}, u32[]{:S(2)}) collective-permute-start(bf16[128,2048]{1,0:T(8,128)(2,1)S(1)} %copy-done.79), channel_id=1, source_target_pairs={{0,8},{4,12},{8,0},{12,4},{1,9},{5,13},{9,1},{13,5},{2,10},{6,14},... | collective-permute-start | bytes 1572872 | tf_op jit(solution)/shard_map/ppermute | solution.py:112
  909.1 26.8 %collective-permute-start.60 = (bf16[128,2048]{1,0:T(8,128)(2,1)}, bf16[128,2048]{1,0:T(8,128)(2,1)}, u32[]{:S(2)}, u32[]{:S(2)}) collective-permute-start(bf16[128,2048]{1,0:T(8,128)(2,1)} %fusion.36), channel_id=1, source_target_pairs={{0,8},{4,12},{8,0},{12,4},{1,9},{5,13},{9,1},{13,5},{2,10},{6,14},... | collective-permute-start | bytes 1572872 | tf_op jit(solution)/shard_map/ppermute | solution.py:112
  919.7 17.6 %collective-permute-start.61 = (bf16[128,2048]{1,0:T(8,128)(2,1)}, bf16[128,2048]{1,0:T(8,128)(2,1)}, u32[]{:S(2)}, u32[]{:S(2)}) collective-permute-start(bf16[128,2048]{1,0:T(8,128)(2,1)} %fusion.34), channel_id=1, source_target_pairs={{0,4},{4,0},{8,12},{12,8},{1,5},{5,1},{9,13},{13,9},{2,6},{6,2},{1... | collective-permute-start | bytes 1572872 | tf_op jit(solution)/shard_map/ppermute | solution.py:112
  926.7 27.4 %collective-permute-start.67 = (bf16[128,2048]{1,0:T(8,128)(2,1)}, bf16[128,2048]{1,0:T(8,128)(2,1)}, u32[]{:S(2)}, u32[]{:S(2)}) collective-permute-start(bf16[128,2048]{1,0:T(8,128)(2,1)} %fusion.28), channel_id=1, source_target_pairs={{0,8},{4,12},{8,0},{12,4},{1,9},{5,13},{9,1},{13,5},{2,10},{6,14},... | collective-permute-start | bytes 1572872 | tf_op jit(solution)/shard_map/ppermute | solution.py:112
  935.9 18.3 %collective-permute-start.68 = (bf16[128,2048]{1,0:T(8,128)(2,1)S(1)}, bf16[128,2048]{1,0:T(8,128)(2,1)}, u32[]{:S(2)}, u32[]{:S(2)}) collective-permute-start(bf16[128,2048]{1,0:T(8,128)(2,1)S(1)} %fusion.26), channel_id=1, source_target_pairs={{0,4},{4,0},{8,12},{12,8},{1,5},{5,1},{9,13},{13,9},{2,6},{6,2},{1... | collective-permute-start | bytes 1572872 | tf_op jit(solution)/shard_map/ppermute | solution.py:112
  937.3 36.7 %collective-permute-start.72 = (bf16[512,1024]{1,0:T(8,128)(2,1)}, bf16[512,1024]{1,0:T(8,128)(2,1)}, u32[]{:S(2)}, u32[]{:S(2)}) collective-permute-start(bf16[512,1024]{1,0:T(8,128)(2,1)} %reduce-scatter.8.cloned.1.call-done.refs_3_), channel_id=1, source_target_pairs={{0,16},{16,0},{1,17},{17,1},{2,18},{18,2},{3,19},{19,3},{4,20},{20... | collective-permute-start | bytes 3145736 | tf_op jit(solution)/shard_map/ppermute | solution.py:92
  938.8 35.2 %collective-permute-start.73 = (bf16[512,1024]{1,0:T(8,128)(2,1)S(1)}, bf16[512,1024]{1,0:T(8,128)(2,1)}, u32[]{:S(2)}, u32[]{:S(2)}) collective-permute-start(bf16[512,1024]{1,0:T(8,128)(2,1)S(1)} %copy-done.13), channel_id=1, source_target_pairs={{0,16},{16,0},{1,17},{17,1},{2,18},{18,2},{3,19},{19,3},{4,20},{20... | collective-permute-start | bytes 3145736 | tf_op jit(solution)/shard_map/ppermute | solution.py:92
  974.0 20.7 %collective-permute-start.74 = (bf16[512,2048]{1,0:T(8,128)(2,1)}, bf16[512,2048]{1,0:T(8,128)(2,1)S(1)}, u32[]{:S(2)}, u32[]{:S(2)}) collective-permute-start(bf16[512,2048]{1,0:T(8,128)(2,1)} %reduce-scatter.14.cloned.1.call-done.refs_0_), channel_id=1, source_target_pairs={{0,16},{16,0},{1,17},{17,1},{2,18},{18,2},{3,19},{19,3},{4,20},{20... | collective-permute-start | bytes 6291464 | tf_op jit(solution)/shard_map/ppermute | solution.py:92
  (127 other events, 1613.3 us)
Sparse Core Ops, SparseCore 0:
  14.7 67.6 all-gather.5
  84.6 165.5 all-gather.7
  252.0 147.9 all-gather.9
  401.9 78.9 all-gather.11
  499.8 75.2 reduce-scatter.5
  577.9 77.2 reduce-scatter.7
  657.5 77.2 reduce-scatter.9
  743.0 74.6 reduce-scatter.11
  823.1 142.6 reduce-scatter.13

commit v4 on v3

--- a/solution.py
+++ b/solution.py
@@ -83,6 +83,9 @@
     bits = peers.bit_length() - 1
     if peers != 1 << bits:
         return lax.psum(array, axis)
+    if peers == 4:
+        got = [lax.ppermute(array, axis, [(i, i ^ by) for i in range(4)]) for by in (1, 2, 3)]
+        return (array + got[0]) + (got[1] + got[2])
     for bit in range(bits):
         array = array + lax.ppermute(array, axis, [(i, i ^ (1 << bit)) for i in range(peers)])
     return array

time: 1040 us -> 1040 us (level)
    ppermute x5 -> x1, waiting for transfers between devices: 13.6 us -> 0.56 us  [added(): lax.ppermute(array, axis, [(i, i ^ 1 << bit) for i in range(peers)])]
  transfers between devices with their start and end apart: 89 -> 91, of which waited for: 50 -> 54; matrix products, arithmetic and copies ran while one was open for 8% -> 8% of each run, Pallas kernels for 43% -> 42%
where the time goes in v4:
time: 1040 us; the launch traced here: 1030 us
  Pallas kernels  459 us (44%)
  waiting for transfers between devices  370 us (36%)
  other arithmetic  67.5 us (6%)
  starting transfers between devices  50.7 us (5%)
  local copies, waits for them, and re-layouts  37.7 us (4%)
  blocking collectives  26.9 us (3%)
  between operations  15.7 us (2%)
    pallas_call x38, Pallas kernels, call(): pl.pallas_call(body, grid_spec=pltpu.PrefetchScalarGridSpec(num_scalar_pr...  459 us
    ppermute x36, waiting for transfers between devices, flipped(): lax.ppermute(array, 'tensor', [(i, i ^ 1 << bit) for i in range(peers)])  169 us
    all_gather x4, waiting for transfers between devices, whole_of(): return lax.all_gather(shard, 'dp', axis=0, tiled=True)  160 us
    ppermute x36, starting transfers between devices, flipped(): lax.ppermute(array, 'tensor', [(i, i ^ 1 << bit) for i in range(peers)])  33.4 us
    ppermute x39, waiting for transfers between devices, swap(): return lax.ppermute(array, 'pipe', [(0, 1), (1, 0)])  32.6 us
    all_gather x1, blocking collectives, local(): lax.all_gather(small, ('pipe', 'dp'), axis=0, tiled=False)  26.9 us
  transfers between devices with their start and end apart: 91, of which 54 were waited for; matrix products, arithmetic and copies ran while one was open for 8% of the time, Pallas kernels for 42%

profile of v4, /device:TPU:0, one launch (start us, length us, event | category | flops | bytes accessed | tf_op | source)
XLA Modules:
  0.0 1028.3 jit_solution(8003554424175679412)
XLA Ops:
  41.4 26.9 %all-gather = bf16[8,1,3072]{2,1,0:T(2,128)(2,1)S(1)} all-gather(bf16[1,1,3072]{2,1,0:T(2,128)(2,1)S(1)} %maximum_bitcast_fusion.2), channel_id=1, replica_groups=mesh['pipe'=2,'tensor'=4,'dp'=4] {'pipe','dp'}, dimensions={0}, use_global_device_ids=true | all-gather | bytes 55296 | tf_op jit(solution)/shard_map/all_gather | solution.py:1021
  74.0 10.4 %shard_map.356 = (bf16[1024,2048]{1,0:T(8,128)(2,1)}, bf16[1024,2048]{1,0:T(8,128)(2,1)}, f32[1024,1]{1,0:T(8,128)}, f32[1024,1]{1,0:T(8,128)}, bf16[2048,1024]{1,0:T(8,128)(2,1)}, /*index=5*/bf16[2048,1024]{1,0:T(8,128)(2,1)}) custom-call(s32[1]{0:T(128)} %dynamic_slice.109.info, bf16[1024,2048]{1,0:T(8,128)(2,1)} %constant_dynamic-slice_fusion.6.z_ref.refs_0_, ...), custom_call_target="tpu_custom_call" | custom-call | flops 1 | bytes 1 | tf_op jit(solution)/shard_map/pallas_call | solution.py:268
  89.4 12.2 %shard_map.358 = (bf16[1024,256]{1,0:T(8,128)(2,1)}, bf16[1024,768]{1,0:T(8,128)(2,1)}, f32[1024,1]{1,0:T(8,128)}) custom-call(s32[1]{0:T(128)} %dynamic_slice.109.info, bf16[1024,2048]{1,0:T(8,128)(2,1)} %get-tuple-element.222.x_ref, bf16[2048,768]{1,0:T(8,128)(2,1)} %all-gather.6.cloned.1.call-done.wq_ref.wk_ref.wv_ref.refs_8_, ...), custom_call_target="tpu_custom_call" | custom-call | flops 1 | bytes 1 | tf_op jit(solution)/shard_map/pallas_call | solution.py:268
  103.3 11.5 %shard_map.359 = (bf16[1024,256]{1,0:T(8,128)(2,1)}, bf16[1024,768]{1,0:T(8,128)(2,1)}, f32[1024,1]{1,0:T(8,128)}) custom-call(s32[1]{0:T(128)} %dynamic_slice.109.info, bf16[1024,2048]{1,0:T(8,128)(2,1)} %get-tuple-element.222.x_ref, bf16[2048,768]{1,0:T(8,128)(2,1)} %copy-done.1, bf16[2048,768]{1,0:T(8,128)(2,1)} %copy-done.1, ...), custom_call_target="tpu_custom_call" | custom-call | flops 1 | bytes 1 | tf_op jit(solution)/shard_map/pallas_call | solution.py:268
  114.8 135.4 %all-gather.8.cloned.1.call-done.refs_0_.refs_1_.refs_2_.refs_3_.refs_16_.refs_18_.outward_ref.refs_10_ = bf16[2048,2304]{1,0:T(8,128)(2,1)} async-done(((bf16[512,2304]{1,0:T(8,128)(2,1)}), bf16[2048,2304]{1,0:T(8,128)(2,1)}) %all-gather.8.cloned.1.call-update) | async-done | bytes 9437200 | tf_op jit(solution)/shard_map/all_gather | solution.py:1038
  253.6 10.8 %shard_map.360 = (bf16[1024,1024]{1,0:T(8,128)(2,1)}, bf16[1024,1024]{1,0:T(8,128)(2,1)}) custom-call(s32[1]{0:T(128)} %dynamic_slice.109.info, bf16[1024,2048]{1,0:T(8,128)(2,1)} %get-tuple-element.223.x_ref, bf16[2048,2304]{1,0:T(8,128)(2,1)} %all-gather.8.cloned.1.call-done.refs_0_.refs_1_.refs_2_.refs_3_.refs_16_.refs_18_.outward_ref.refs_10_, ...), custom_call_target="tpu_custom_call" | custom-call | flops 1 | bytes 1 | tf_op jit(solution)/shard_map/pallas_call | solution.py:268
  265.2 10.6 %shard_map.361 = (bf16[1024,1024]{1,0:T(8,128)(2,1)}, bf16[1024,1024]{1,0:T(8,128)(2,1)}) custom-call(s32[1]{0:T(128)} %dynamic_slice.109.info, bf16[1024,2048]{1,0:T(8,128)(2,1)} %get-tuple-element.223.x_ref, bf16[2048,2304]{1,0:T(8,128)(2,1)} %collective-permute-done.5.refs_0_.refs_1_.refs_2_.refs_3_.refs_17_.refs_19_.outward_ref.refs_11_, ...), custom_call_target="tpu_custom_call" | custom-call | flops 1 | bytes 1 | tf_op jit(solution)/shard_map/pallas_call | solution.py:268
  275.8 17.2 %shard_map.362 = (bf16[128,2048]{1,0:T(8,128)(2,1)}, bf16[128,2048]{1,0:T(8,128)(2,1)}, bf16[256,2048]{1,0:T(8,128)(2,1)}, bf16[128,2048]{1,0:T(8,128)(2,1)}, bf...) custom-call(s32[8]{0:T(128)} %stack.259.info, ...), custom_call_target="tpu_custom_call" | custom-call | flops 1 | bytes 1 | tf_op jit(solution)/shard_map/pallas_call | solution.py:268
  297.1 10.9 %collective-permute-done.6 = bf16[128,2048]{1,0:T(8,128)(2,1)S(1)} collective-permute-done((bf16[128,2048]{1,0:T(8,128)(2,1)}, bf16[128,2048]{1,0:T(8,128)(2,1)S(1)}, u32[]{:S(2)}, u32[]{:S(2)}) %collective-permute-start.6) | collective-permute-done | bytes 524320 | tf_op jit(solution)/shard_map/ppermute | solution.py:115
  308.0 10.4 %collective-permute-done.7 = bf16[128,2048]{1,0:T(8,128)(2,1)S(1)} collective-permute-done((bf16[128,2048]{1,0:T(8,128)(2,1)}, bf16[128,2048]{1,0:T(8,128)(2,1)S(1)}, u32[]{:S(2)}, u32[]{:S(2)}) %collective-permute-start.7) | collective-permute-done | bytes 524320 | tf_op jit(solution)/shard_map/ppermute | solution.py:115
  327.0 9.3 collective-permute-done.10
  346.5 10.8 %collective-permute-done.13.refs_5_ = bf16[128,2048]{1,0:T(8,128)(2,1)S(1)} collective-permute-done((bf16[128,2048]{1,0:T(8,128)(2,1)S(1)}, bf16[128,2048]{1,0:T(8,128)(2,1)S(1)}, u32[]{:S(2)}, u32[]{:S(2)}) %collective-permute-start.13) | collective-permute-done | bytes 524320 | tf_op jit(solution)/shard_map/ppermute | solution.py:115
  361.2 8.8 collective-permute-done.16.refs_6_
  377.7 13.1 %shard_map.363 = (bf16[1024,2048]{1,0:T(8,128)(2,1)}, bf16[1024,2048]{1,0:T(8,128)(2,1)}, bf16[1024,2048]{1,0:T(8,128)(2,1)}, f32[1024,1]{1,0:T(8,128)}, f32[102...) custom-call(s32[8]{0:T(128)} %stack.276.info, bf16[128,2048]{1,0:T(8,128)(2,1)} %copy-done.20, ...), custom_call_target="tpu_custom_call" | custom-call | flops 1 | bytes 1 | tf_op jit(solution)/shard_map/pallas_call | solution.py:268
  390.9 9.0 all-gather.10.cloned.1.call-done.refs_0_.refs_1_.refs_2_.refs_3_.wq_ref.wk_ref.wv_ref.outward_ref.refs_8_.refs_10_.refs_16_
  400.0 10.9 %shard_map.366 = (bf16[1024,1024]{1,0:T(8,128)(2,1)}, bf16[1024,1024]{1,0:T(8,128)(2,1)}) custom-call(s32[1]{0:T(128)} %dynamic_slice.109.info, bf16[1024,2048]{1,0:T(8,128)(2,1)} %get-tuple-element.251.x_ref, bf16[2048,2048]{1,0:T(8,128)(2,1)} %all-gather.10.cloned.1.call-done.refs_0_.refs_1_.refs_2_.refs_3_.wq_ref.wk_ref.wv_ref.outward_ref.refs_8_.refs_10_.refs_16_, ...), custom_call_target="tpu_custom_call" | custom-call | flops 1 | bytes 1 | tf_op jit(solution)/shard_map/pallas_call | solution.py:268
  410.9 10.2 shard_map.367
  421.0 10.7 %shard_map.364 = (bf16[1024,1024]{1,0:T(8,128)(2,1)}, bf16[1024,1024]{1,0:T(8,128)(2,1)}) custom-call(s32[1]{0:T(128)} %dynamic_slice.109.info, bf16[1024,2048]{1,0:T(8,128)(2,1)} %get-tuple-element.251.x_ref, bf16[2048,2048]{1,0:T(8,128)(2,1)} %collective-permute-done.18.refs_0_.refs_1_.refs_2_.refs_3_.wq_ref.wk_ref.wv_ref.outward_ref.refs_9_.refs_11_.refs_17_, ...), custom_call_target="tpu_custom_call" | custom-call | flops 1 | bytes 1 | tf_op jit(solution)/shard_map/pallas_call | solution.py:268
  431.7 10.2 shard_map.365
  441.9 11.5 %shard_map.368 = (bf16[1024,256]{1,0:T(8,128)(2,1)}, bf16[1024,768]{1,0:T(8,128)(2,1)}, f32[1024,1]{1,0:T(8,128)}) custom-call(s32[1]{0:T(128)} %dynamic_slice.109.info, bf16[1024,2048]{1,0:T(8,128)(2,1)} %get-tuple-element.264.x_ref, ...), custom_call_target="tpu_custom_call" | custom-call | flops 1 | bytes 1 | tf_op jit(solution)/shard_map/pallas_call | solution.py:268
  453.4 11.7 %shard_map.369 = (bf16[1024,256]{1,0:T(8,128)(2,1)}, bf16[1024,768]{1,0:T(8,128)(2,1)}, f32[1024,1]{1,0:T(8,128)}) custom-call(s32[1]{0:T(128)} %dynamic_slice.109.info, bf16[1024,2048]{1,0:T(8,128)(2,1)} %get-tuple-element.264.x_ref, ...), custom_call_target="tpu_custom_call" | custom-call | flops 1 | bytes 1 | tf_op jit(solution)/shard_map/pallas_call | solution.py:268
  465.1 15.7 %all-gather.12.cloned.1.call-done.refs_0_.refs_1_.refs_2_.refs_3_.refs_18_ = bf16[2048,1024]{1,0:T(8,128)(2,1)} async-done(((bf16[512,1024]{1,0:T(8,128)(2,1)}), bf16[2048,1024]{1,0:T(8,128)(2,1)}) %all-gather.12.cloned.1.call-update) | async-done | bytes 4194320 | tf_op jit(solution)/shard_map/all_gather | solution.py:1038
  481.4 11.3 %shard_map.370 = (bf16[1024,256]{1,0:T(8,128)(2,1)}, bf16[1024,1024]{1,0:T(8,128)(2,1)}, f32[1,1024]{1,0:T(1,128)}) custom-call(s32[1]{0:T(128)} %dynamic_slice.109.info, bf16[1024,2048]{1,0:T(8,128)(2,1)} %get-tuple-element.293.g_ref, ...), custom_call_target="tpu_custom_call" | custom-call | flops 17179869184 | bytes 16777216 | tf_op jit(solution)/shard_map/pallas_call | solution.py:268
  509.2 10.8 %shard_map.372 = (bf16[1024,256]{1,0:T(8,128)(2,1)}, bf16[1024,1024]{1,0:T(8,128)(2,1)}, f32[1,1024]{1,0:T(1,128)}) custom-call(s32[1]{0:T(128)} %dynamic_slice.109.info, bf16[1024,2048]{1,0:T(8,128)(2,1)} %get-tuple-element.293.g_ref, ...), custom_call_target="tpu_custom_call" | custom-call | flops 1 | bytes 1 | tf_op jit(solution)/shard_map/pallas_call | solution.py:268
  520.1 10.2 shard_map.373
  541.6 11.4 %shard_map.374 = bf16[2048,1024]{1,0:T(8,128)(2,1)} custom-call(s32[1]{0:T(128)} %dynamic_slice.109.info, bf16[2048,1024]{1,0:T(8,128)(2,1)} %get-tuple-element.296.refs_0_, bf16[1024,1024]{1,0:T(8,128)(2,1)} %get-tuple-element.297.refs_1_.refs_2_.refs_3_.refs_4_.refs_6_, bf16[1024,1024]{1,0:T(8,128)(2,1)} %get-tuple-element.297.refs_1_.refs_2_.refs_3_.refs_4_.refs_6_, ...), custom_call_target="tpu_custom_call" | custom-call | flops 1 | bytes 1 | tf_op jit(solution)/shard_map/pallas_call | solution.py:268
  561.6 31.1 %shard_map.376 = (bf16[128,2048]{1,0:T(8,128)(2,1)}, bf16[128,2048]{1,0:T(8,128)(2,1)}, bf16[256,2048]{1,0:T(8,128)(2,1)}, bf16[128,2048]{1,0:T(8,128)(2,1)}, bf...) custom-call(s32[16]{0:T(128)} %stack.282.info, ...), custom_call_target="tpu_custom_call" | custom-call | flops 1 | bytes 1 | tf_op jit(solution)/shard_map/pallas_call | solution.py:268
  592.7 11.0 %shard_map.381 = (bf16[2048,256]{1,0:T(8,128)(2,1)}, bf16[2048,256]{1,0:T(8,128)(2,1)}, bf16[2048,256]{1,0:T(8,128)(2,1)}, bf16[2048,256]{1,0:T(8,128)(2,1)}) custom-call(s32[1]{0:T(128)} %dynamic_slice.109.info, bf16[2048,1024]{1,0:T(8,128)(2,1)} %get-tuple-element.349.refs_0_, bf16[2048,1024]{1,0:T(8,128)(2,1)} %get-tuple-element.224.refs_0_.refs_1_, ...), custom_call_target="tpu_custom_call" | custom-call | flops 17179869184 | bytes 16777216 | tf_op jit(solution)/shard_map/pallas_call | solution.py:268
  612.1 12.3 %shard_map.382 = bf16[2048,1024]{1,0:T(8,128)(2,1)} custom-call(s32[1]{0:T(128)} %dynamic_slice.109.info, bf16[2048,1024]{1,0:T(8,128)(2,1)} %get-tuple-element.349.refs_0_, bf16[2048,1024]{1,0:T(8,128)(2,1)} %get-tuple-element.224.refs_0_.refs_1_, bf16[1024,768]{1,0:T(8,128)(2,1)} %shard_map.371.refs_4_.refs_2_.refs_3_, ...), custom_call_target="tpu_custom_call" | custom-call | flops 17179869184 | bytes 16777216 | tf_op jit(solution)/shard_map/pallas_call | solution.py:268
  629.1 10.9 %collective-permute-done.31 = bf16[128,2048]{1,0:T(8,128)(2,1)S(1)} collective-permute-done((bf16[128,2048]{1,0:T(8,128)(2,1)}, bf16[128,2048]{1,0:T(8,128)(2,1)S(1)}, u32[]{:S(2)}, u32[]{:S(2)}) %collective-permute-start.31) | collective-permute-done | bytes 524320 | tf_op jit(solution)/shard_map/ppermute | solution.py:115
  640.1 10.4 %collective-permute-done.30 = bf16[128,2048]{1,0:T(8,128)(2,1)S(1)} collective-permute-done((bf16[128,2048]{1,0:T(8,128)(2,1)}, bf16[128,2048]{1,0:T(8,128)(2,1)S(1)}, u32[]{:S(2)}, u32[]{:S(2)}) %collective-permute-start.30) | collective-permute-done | bytes 524320 | tf_op jit(solution)/shard_map/ppermute | solution.py:115
  656.1 8.9 collective-permute-done.32
  673.3 10.8 %collective-permute-done.35.refs_5_ = bf16[128,2048]{1,0:T(8,128)(2,1)S(1)} collective-permute-done((bf16[128,2048]{1,0:T(8,128)(2,1)S(1)}, bf16[128,2048]{1,0:T(8,128)(2,1)S(1)}, u32[]{:S(2)}, u32[]{:S(2)}) %collective-permute-start.35) | collective-permute-done | bytes 524320 | tf_op jit(solution)/shard_map/ppermute | solution.py:115
  686.6 10.1 collective-permute-done.38.refs_6_
  712.4 10.1 shard_map.378
  730.9 11.4 %shard_map.379 = bf16[2048,1024]{1,0:T(8,128)(2,1)} custom-call(s32[1]{0:T(128)} %dynamic_slice.109.info, bf16[2048,1024]{1,0:T(8,128)(2,1)} %get-tuple-element.339.refs_0_.refs_2_, bf16[1024,1024]{1,0:T(8,128)(2,1)} %get-tuple-element.230.refs_8_.refs_9_.refs_10_.refs_11_.refs_1_.refs_2_.refs_3_.refs_4_, ...), custom_call_target="tpu_custom_call" | custom-call | flops 1 | bytes 1 | tf_op jit(solution)/shard_map/pallas_call | solution.py:268
  742.6 11.4 %shard_map.384 = (bf16[1024,256]{1,0:T(8,128)(2,1)}, bf16[1024,1024]{1,0:T(8,128)(2,1)}, f32[1,1024]{1,0:T(1,128)}) custom-call(s32[1]{0:T(128)} %dynamic_slice.109.info, bf16[1024,2048]{1,0:T(8,128)(2,1)} %get-tuple-element.345.g_ref, bf16[2048,2304]{1,0:T(8,128)(2,1)} %collective-permute-done.5.refs_0_.refs_1_.refs_2_.refs_3_.refs_17_.refs_19_.outward_ref.refs_11_, ...), custom_call_target="tpu_custom_call" | custom-call | flops 1 | bytes 1 | tf_op jit(solution)/shard_map/pallas_call | solution.py:268
  761.7 15.0 %shard_map.386 = (bf16[2048,256]{1,0:T(8,128)(2,1)}, bf16[2048,256]{1,0:T(8,128)(2,1)}, bf16[2048,256]{1,0:T(8,128)(2,1)}, bf16[2048,256]{1,0:T(8,128)(2,1)}, bf...) custom-call(s32[1]{0:T(128)} %dynamic_slice.109.info, ...), custom_call_target="tpu_custom_call" | custom-call | flops 1 | bytes 1 | tf_op jit(solution)/shard_map/pallas_call | solution.py:268
  784.3 10.9 %shard_map.380 = (bf16[1024,256]{1,0:T(8,128)(2,1)}, bf16[1024,1024]{1,0:T(8,128)(2,1)}, f32[1,1024]{1,0:T(1,128)}) custom-call(s32[1]{0:T(128)} %dynamic_slice.109.info, bf16[1024,2048]{1,0:T(8,128)(2,1)} %get-tuple-element.345.g_ref, bf16[2048,2304]{1,0:T(8,128)(2,1)} %all-gather.8.cloned.1.call-done.refs_0_.refs_1_.refs_2_.refs_3_.refs_16_.refs_18_.outward_ref.refs_10_, ...), custom_call_target="tpu_custom_call" | custom-call | flops 1 | bytes 1 | tf_op jit(solution)/shard_map/pallas_call | solution.py:268
  804.2 18.1 %shard_map.387 = bf16[2048,2048]{1,0:T(8,128)(2,1)} custom-call(s32[1]{0:T(128)} %dynamic_slice.109.info, bf16[2048,1024]{1,0:T(8,128)(2,1)} %get-tuple-element.267.refs_0_, bf16[2048,1024]{1,0:T(8,128)(2,1)} %get-tuple-element.268.refs_1_, bf16[2048,1024]{1,0:T(8,128)(2,1)} %get-tuple-element.339.refs_0_.refs_2_, ...), custom_call_target="tpu_custom_call" | custom-call | flops 1 | bytes 1 | tf_op jit(solution)/shard_map/pallas_call | solution.py:268
  822.4 31.6 %shard_map.388 = (bf16[128,2048]{1,0:T(8,128)(2,1)}, bf16[128,2048]{1,0:T(8,128)(2,1)}, bf16[256,2048]{1,0:T(8,128)(2,1)}, bf16[128,2048]{1,0:T(8,128)(2,1)}, bf...) custom-call(s32[16]{0:T(128)} %stack.282.info, ...), custom_call_target="tpu_custom_call" | custom-call | flops 1 | bytes 1 | tf_op jit(solution)/shard_map/pallas_call | solution.py:268
  854.1 17.3 %shard_map.389 = (bf16[128,2048]{1,0:T(8,128)(2,1)}, bf16[128,2048]{1,0:T(8,128)(2,1)}, bf16[256,2048]{1,0:T(8,128)(2,1)}, bf16[128,2048]{1,0:T(8,128)(2,1)}, bf...) custom-call(s32[8]{0:T(128)} %stack.259.info, ...), custom_call_target="tpu_custom_call" | custom-call | flops 1 | bytes 1 | tf_op jit(solution)/shard_map/pallas_call | solution.py:268
  876.4 10.0 collective-permute-done.56
  886.6 11.2 %collective-permute-done.57 = bf16[128,2048]{1,0:T(8,128)(2,1)} collective-permute-done((bf16[128,2048]{1,0:T(8,128)(2,1)}, bf16[128,2048]{1,0:T(8,128)(2,1)}, u32[]{:S(2)}, u32[]{:S(2)}) %collective-permute-start.57) | collective-permute-done | bytes 524320 | tf_op jit(solution)/shard_map/ppermute | solution.py:115
  908.9 10.7 %collective-permute-done.64 = bf16[128,2048]{1,0:T(8,128)(2,1)S(1)} collective-permute-done((bf16[128,2048]{1,0:T(8,128)(2,1)}, bf16[128,2048]{1,0:T(8,128)(2,1)S(1)}, u32[]{:S(2)}, u32[]{:S(2)}) %collective-permute-start.64) | collective-permute-done | bytes 524320 | tf_op jit(solution)/shard_map/ppermute | solution.py:115
  941.1 13.7 %shard_map.390 = (f32[2048,512]{1,0:T(8,128)}, f32[2048,512]{1,0:T(8,128)}, f32[2048,512]{1,0:T(8,128)}) custom-call(s32[1]{0:T(128)} %bitcast.14.info, bf16[512,1024]{1,0:T(8,128)(2,1)} %reduce-scatter.12.cloned.1.call-done.refs_0_, bf16[512,1024]{1,0:T(8,128)(2,1)} %copy-done.38, bf16[512,1024]{1,0:T(8,128)(2,1)} %collective-permute-done.70.refs_2_, ...), custom_call_target="tpu_custom_call" | custom-call | flops 1 | bytes 1 | tf_op jit(solution)/shard_map/pallas_call | solution.py:268
  996.8 10.4 %shard_map.393 = (f32[1,512,2048]{2,1,0:T(8,128)}, f32[1,512,2048]{2,1,0:T(8,128)}, f32[1,512,2048]{2,1,0:T(8,128)}) custom-call(s32[1]{0:T(128)} %bitcast.14.info, bf16[512,2048]{1,0:T(8,128)(2,1)} %reduce-scatter.14.cloned.1.call-done.refs_0_, bf16[512,2048]{1,0:T(8,128)(2,1)} %copy-done.2, bf16[512,1024]{1,0:T(8,128)(2,1)} %collective-permute-done.72.refs_2_, ...), custom_call_target="tpu_custom_call" | custom-call | flops 1 | bytes 1 | tf_op jit(solution)/shard_map/pallas_call | solution.py:268
  1011.1 10.2 shard_map.391
  (457 shorter events, 282.8 us)
Async XLA Ops:
  7.2 77.2 %all-gather.6.cloned.1.call-start = ((), (), s32[]{:S(2)}) async-start(), calls=%async_computation.5 | async-start | bytes 3932160 | tf_op jit(solution)/shard_map/all_gather | solution.py:1038
  14.6 235.6 %all-gather.8.cloned.1.call-start = ((), (), s32[]{:S(2)}) async-start(), calls=%async_computation.6 | async-start | bytes 11796480 | tf_op jit(solution)/shard_map/all_gather | solution.py:1038
  32.3 367.6 %all-gather.10.cloned.1.call-start = ((), (), s32[]{:S(2)}) async-start(), calls=%async_computation.7 | async-start | bytes 10485760 | tf_op jit(solution)/shard_map/all_gather | solution.py:1038
  84.4 17.2 %collective-permute-start.1 = (bf16[2048,768]{1,0:T(8,128)(2,1)}, bf16[2048,768]{1,0:T(8,128)(2,1)S(1)}, u32[]{:S(2)}, u32[]{:S(2)}) collective-permute-start(bf16[2048,768]{1,0:T(8,128)(2,1)} %all-gather.6.cloned.1.call-done.wq_ref.wk_ref.wv_ref.refs_8_), channel_id=1, source_target_pairs={{0,16},{16,0},{1,17},{17,1},{2,18},{18,2},{3,19},{19,3},{4,20},{20... | collective-permute-start | bytes 9437192 | tf_op jit(solution)/shard_map/ppermute | solution.py:95
  250.2 15.0 %collective-permute-start.5 = (bf16[2048,2304]{1,0:T(8,128)(2,1)}, bf16[2048,2304]{1,0:T(8,128)(2,1)}, u32[]{:S(2)}, u32[]{:S(2)}) collective-permute-start(bf16[2048,2304]{1,0:T(8,128)(2,1)} %all-gather.8.cloned.1.call-done.refs_0_.refs_1_.refs_2_.refs_3_.refs_16_.refs_18_.outward_ref.refs_10_), channel_id=1, source_target_pairs={{0,16},{16,0},{1,17},{17,1},{2,18},{18,2},{3,19},{19,3},{4,20},{20... | collective-permute-start | bytes 28311560 | tf_op jit(solution)/shard_map/ppermute | solution.py:95
  251.8 229.1 %all-gather.12.cloned.1.call-start = ((), (), s32[]{:S(2)}) async-start(), calls=%async_computation.8 | async-start | bytes 5242880 | tf_op jit(solution)/shard_map/all_gather | solution.py:1038
  293.0 15.0 %collective-permute-start.6 = (bf16[128,2048]{1,0:T(8,128)(2,1)}, bf16[128,2048]{1,0:T(8,128)(2,1)S(1)}, u32[]{:S(2)}, u32[]{:S(2)}) collective-permute-start(bf16[128,2048]{1,0:T(8,128)(2,1)} %get-tuple-element.233), channel_id=1, source_target_pairs={{0,4},{4,0},{8,12},{12,8},{1,5},{5,1},{9,13},{13,9},{2,6},{6,2},{1... | collective-permute-start | bytes 1572872 | tf_op jit(solution)/shard_map/ppermute | solution.py:115
  294.5 23.9 %collective-permute-start.7 = (bf16[128,2048]{1,0:T(8,128)(2,1)}, bf16[128,2048]{1,0:T(8,128)(2,1)S(1)}, u32[]{:S(2)}, u32[]{:S(2)}) collective-permute-start(bf16[128,2048]{1,0:T(8,128)(2,1)} %get-tuple-element.234), channel_id=1, source_target_pairs={{0,4},{4,0},{8,12},{12,8},{1,5},{5,1},{9,13},{13,9},{2,6},{6,2},{1... | collective-permute-start | bytes 1572872 | tf_op jit(solution)/shard_map/ppermute | solution.py:115
  295.1 23.4 %collective-permute-start.8 = (bf16[128,2048]{1,0:T(8,128)(2,1)}, bf16[128,2048]{1,0:T(8,128)(2,1)S(1)}, u32[]{:S(2)}, u32[]{:S(2)}) collective-permute-start(bf16[128,2048]{1,0:T(8,128)(2,1)} %get-tuple-element.235), channel_id=1, source_target_pairs={{0,8},{4,12},{8,0},{12,4},{1,9},{5,13},{9,1},{13,5},{2,10},{6,14},... | collective-permute-start | bytes 1572872 | tf_op jit(solution)/shard_map/ppermute | solution.py:115
  296.5 23.4 %collective-permute-start.9 = (bf16[128,2048]{1,0:T(8,128)(2,1)}, bf16[128,2048]{1,0:T(8,128)(2,1)S(1)}, u32[]{:S(2)}, u32[]{:S(2)}) collective-permute-start(bf16[128,2048]{1,0:T(8,128)(2,1)} %get-tuple-element.236), channel_id=1, source_target_pairs={{0,8},{4,12},{8,0},{12,4},{1,9},{5,13},{9,1},{13,5},{2,10},{6,14},... | collective-permute-start | bytes 1572872 | tf_op jit(solution)/shard_map/ppermute | solution.py:115
  344.4 25.6 %collective-permute-start.16 = (bf16[128,2048]{1,0:T(8,128)(2,1)S(1)}, bf16[128,2048]{1,0:T(8,128)(2,1)S(1)}, u32[]{:S(2)}, u32[]{:S(2)}) collective-permute-start(bf16[128,2048]{1,0:T(8,128)(2,1)S(1)} %get-tuple-element.520.refs_4_), channel_id=1, source_target_pairs={{0,8},{4,12},{8,0},{12,4},{1,9},{5,13},{9,1},{13,5},{2,10},{6,14},... | collective-permute-start | bytes 1572872 | tf_op jit(solution)/shard_map/ppermute | solution.py:115
  345.9 24.1 %collective-permute-start.14 = (bf16[128,2048]{1,0:T(8,128)(2,1)S(1)}, bf16[128,2048]{1,0:T(8,128)(2,1)S(1)}, u32[]{:S(2)}, u32[]{:S(2)}) collective-permute-start(bf16[128,2048]{1,0:T(8,128)(2,1)S(1)} %get-tuple-element.521.refs_0_), channel_id=1, source_target_pairs={{0,4},{4,0},{8,12},{12,8},{1,5},{5,1},{9,13},{13,9},{2,6},{6,2},{1... | collective-permute-start | bytes 1572872 | tf_op jit(solution)/shard_map/ppermute | solution.py:115
  358.8 17.8 %collective-permute-start.15 = (bf16[128,2048]{1,0:T(8,128)(2,1)S(1)}, bf16[128,2048]{1,0:T(8,128)(2,1)}, u32[]{:S(2)}, u32[]{:S(2)}) collective-permute-start(bf16[128,2048]{1,0:T(8,128)(2,1)S(1)} %collective-permute-done.12.refs_1_), channel_id=1, source_target_pairs={{0,4},{4,0},{8,12},{12,8},{1,5},{5,1},{9,13},{13,9},{2,6},{6,2},{1... | collective-permute-start | bytes 1572872 | tf_op jit(solution)/shard_map/ppermute | solution.py:115
  359.4 18.3 %collective-permute-start.17 = (bf16[128,2048]{1,0:T(8,128)(2,1)S(1)}, bf16[128,2048]{1,0:T(8,128)(2,1)}, u32[]{:S(2)}, u32[]{:S(2)}) collective-permute-start(bf16[128,2048]{1,0:T(8,128)(2,1)S(1)} %collective-permute-done.13.refs_5_), channel_id=1, source_target_pairs={{0,8},{4,12},{8,0},{12,4},{1,9},{5,13},{9,1},{13,5},{2,10},{6,14},... | collective-permute-start | bytes 1572872 | tf_op jit(solution)/shard_map/ppermute | solution.py:115
  399.9 21.2 %collective-permute-start.18 = (bf16[2048,2048]{1,0:T(8,128)(2,1)}, bf16[2048,2048]{1,0:T(8,128)(2,1)}, u32[]{:S(2)}, u32[]{:S(2)}) collective-permute-start(bf16[2048,2048]{1,0:T(8,128)(2,1)} %all-gather.10.cloned.1.call-done.refs_0_.refs_1_.refs_2_.refs_3_.wq_ref.wk_ref.wv_ref.outward_ref.refs_8_.refs_10_.r, ...), channel_id=1, source_target_pairs={{0,16},{16,0},{1,17},{17,1},{2,18},{18,2},{3,19},{19,3},{4,20},{20... | collective-permute-start | bytes 25165832 | tf_op jit(solution)/shard_map/ppermute | solution.py:95
  399.9 225.1 %reduce-scatter.6.cloned.1.call-start = ((), (), s32[]{:S(2)}) async-start(), calls=%async_computation.9 | async-start | bytes 5242880 | tf_op jit(solution)/shard_map/reduce_scatter | solution.py:895
  499.7 204.7 %reduce-scatter.8.cloned.1.call-start = ((), (), s32[]{:S(2)}) async-start(), calls=%async_computation.10 | async-start | bytes 5242880 | tf_op jit(solution)/shard_map/reduce_scatter | solution.py:895
  553.0 208.7 %reduce-scatter.10.cloned.1.call-start = ((), (), s32[]{:S(2)}) async-start(), calls=%async_computation.11 | async-start | bytes 5242880 | tf_op jit(solution)/shard_map/reduce_scatter | solution.py:895
  624.5 301.6 %reduce-scatter.12.cloned.1.call-start = ((), (), s32[]{:S(2)}) async-start(), calls=%async_computation.12 | async-start | bytes 5242880 | tf_op jit(solution)/shard_map/reduce_scatter | solution.py:895
  625.0 15.0 %collective-permute-start.31 = (bf16[128,2048]{1,0:T(8,128)(2,1)}, bf16[128,2048]{1,0:T(8,128)(2,1)S(1)}, u32[]{:S(2)}, u32[]{:S(2)}) collective-permute-start(bf16[128,2048]{1,0:T(8,128)(2,1)} %get-tuple-element.316), channel_id=1, source_target_pairs={{0,8},{4,12},{8,0},{12,4},{1,9},{5,13},{9,1},{13,5},{2,10},{6,14},... | collective-permute-start | bytes 1572872 | tf_op jit(solution)/shard_map/ppermute | solution.py:115
  626.6 23.8 %collective-permute-start.30 = (bf16[128,2048]{1,0:T(8,128)(2,1)}, bf16[128,2048]{1,0:T(8,128)(2,1)S(1)}, u32[]{:S(2)}, u32[]{:S(2)}) collective-permute-start(bf16[128,2048]{1,0:T(8,128)(2,1)} %get-tuple-element.314), channel_id=1, source_target_pairs={{0,8},{4,12},{8,0},{12,4},{1,9},{5,13},{9,1},{13,5},{2,10},{6,14},... | collective-permute-start | bytes 1572872 | tf_op jit(solution)/shard_map/ppermute | solution.py:115
  627.1 23.4 %collective-permute-start.29 = (bf16[128,2048]{1,0:T(8,128)(2,1)S(1)}, bf16[128,2048]{1,0:T(8,128)(2,1)S(1)}, u32[]{:S(2)}, u32[]{:S(2)}) collective-permute-start(bf16[128,2048]{1,0:T(8,128)(2,1)S(1)} %copy-done.83), channel_id=1, source_target_pairs={{0,4},{4,0},{8,12},{12,8},{1,5},{5,1},{9,13},{13,9},{2,6},{6,2},{1... | collective-permute-start | bytes 1572872 | tf_op jit(solution)/shard_map/ppermute | solution.py:115
  628.7 23.1 %collective-permute-start.28 = (bf16[128,2048]{1,0:T(8,128)(2,1)S(1)}, bf16[128,2048]{1,0:T(8,128)(2,1)S(1)}, u32[]{:S(2)}, u32[]{:S(2)}) collective-permute-start(bf16[128,2048]{1,0:T(8,128)(2,1)S(1)} %copy-done.82), channel_id=1, source_target_pairs={{0,4},{4,0},{8,12},{12,8},{1,5},{5,1},{9,13},{13,9},{2,6},{6,2},{1... | collective-permute-start | bytes 1572872 | tf_op jit(solution)/shard_map/ppermute | solution.py:115
  669.2 14.9 %collective-permute-start.35 = (bf16[128,2048]{1,0:T(8,128)(2,1)S(1)}, bf16[128,2048]{1,0:T(8,128)(2,1)S(1)}, u32[]{:S(2)}, u32[]{:S(2)}) collective-permute-start(bf16[128,2048]{1,0:T(8,128)(2,1)S(1)} %get-tuple-element.333.refs_4_), channel_id=1, source_target_pairs={{0,4},{4,0},{8,12},{12,8},{1,5},{5,1},{9,13},{13,9},{2,6},{6,2},{1... | collective-permute-start | bytes 1572872 | tf_op jit(solution)/shard_map/ppermute | solution.py:115
  671.2 25.5 %collective-permute-start.38 = (bf16[128,2048]{1,0:T(8,128)(2,1)S(1)}, bf16[128,2048]{1,0:T(8,128)(2,1)S(1)}, u32[]{:S(2)}, u32[]{:S(2)}) collective-permute-start(bf16[128,2048]{1,0:T(8,128)(2,1)S(1)} %get-tuple-element.333.refs_4_), channel_id=1, source_target_pairs={{0,8},{4,12},{8,0},{12,4},{1,9},{5,13},{9,1},{13,5},{2,10},{6,14},... | collective-permute-start | bytes 1572872 | tf_op jit(solution)/shard_map/ppermute | solution.py:115
  672.7 24.1 %collective-permute-start.36 = (bf16[128,2048]{1,0:T(8,128)(2,1)S(1)}, bf16[128,2048]{1,0:T(8,128)(2,1)S(1)}, u32[]{:S(2)}, u32[]{:S(2)}) collective-permute-start(bf16[128,2048]{1,0:T(8,128)(2,1)S(1)} %get-tuple-element.325.refs_0_), channel_id=1, source_target_pairs={{0,4},{4,0},{8,12},{12,8},{1,5},{5,1},{9,13},{13,9},{2,6},{6,2},{1... | collective-permute-start | bytes 1572872 | tf_op jit(solution)/shard_map/ppermute | solution.py:115
  685.5 17.5 %collective-permute-start.37 = (bf16[128,2048]{1,0:T(8,128)(2,1)S(1)}, bf16[128,2048]{1,0:T(8,128)(2,1)S(1)}, u32[]{:S(2)}, u32[]{:S(2)}) collective-permute-start(bf16[128,2048]{1,0:T(8,128)(2,1)S(1)} %collective-permute-done.34.refs_1_), channel_id=1, source_target_pairs={{0,4},{4,0},{8,12},{12,8},{1,5},{5,1},{9,13},{13,9},{2,6},{6,2},{1... | collective-permute-start | bytes 1572872 | tf_op jit(solution)/shard_map/ppermute | solution.py:115
  686.1 18.3 %collective-permute-start.39 = (bf16[128,2048]{1,0:T(8,128)(2,1)S(1)}, bf16[128,2048]{1,0:T(8,128)(2,1)}, u32[]{:S(2)}, u32[]{:S(2)}) collective-permute-start(bf16[128,2048]{1,0:T(8,128)(2,1)S(1)} %collective-permute-done.35.refs_5_), channel_id=1, source_target_pairs={{0,8},{4,12},{8,0},{12,4},{1,9},{5,13},{9,1},{13,5},{2,10},{6,14},... | collective-permute-start | bytes 1572872 | tf_op jit(solution)/shard_map/ppermute | solution.py:115
  742.4 237.8 %reduce-scatter.14.cloned.1.call-start = ((), (), s32[]{:S(2)}) async-start(), calls=%async_computation.13 | async-start | bytes 10485760 | tf_op jit(solution)/shard_map/reduce_scatter | solution.py:895
  777.4 25.4 %collective-permute-start.51 = (bf16[2048,256]{1,0:T(8,128)(2,1)}, bf16[2048,256]{1,0:T(8,128)(2,1)S(1)}, u32[]{:S(2)}, u32[]{:S(2)}) collective-permute-start(bf16[2048,256]{1,0:T(8,128)(2,1)} %get-tuple-element.368), channel_id=1, source_target_pairs={{0,16},{16,0},{1,17},{17,1},{2,18},{18,2},{3,19},{19,3},{4,20},{20... | collective-permute-start | bytes 3145736 | tf_op jit(solution)/shard_map/ppermute | solution.py:95
  777.8 25.0 %collective-permute-start.52 = (bf16[2048,256]{1,0:T(8,128)(2,1)}, bf16[2048,256]{1,0:T(8,128)(2,1)S(1)}, u32[]{:S(2)}, u32[]{:S(2)}) collective-permute-start(bf16[2048,256]{1,0:T(8,128)(2,1)} %get-tuple-element.369), channel_id=1, source_target_pairs={{0,16},{16,0},{1,17},{17,1},{2,18},{18,2},{3,19},{19,3},{4,20},{20... | collective-permute-start | bytes 3145736 | tf_op jit(solution)/shard_map/ppermute | solution.py:95
  779.7 23.2 %collective-permute-start.53 = (bf16[2048,256]{1,0:T(8,128)(2,1)}, bf16[2048,256]{1,0:T(8,128)(2,1)}, u32[]{:S(2)}, u32[]{:S(2)}) collective-permute-start(bf16[2048,256]{1,0:T(8,128)(2,1)} %get-tuple-element.370), channel_id=1, source_target_pairs={{0,16},{16,0},{1,17},{17,1},{2,18},{18,2},{3,19},{19,3},{4,20},{20... | collective-permute-start | bytes 3145736 | tf_op jit(solution)/shard_map/ppermute | solution.py:95
  781.2 21.7 %collective-permute-start.54 = (bf16[2048,256]{1,0:T(8,128)(2,1)}, bf16[2048,256]{1,0:T(8,128)(2,1)}, u32[]{:S(2)}, u32[]{:S(2)}) collective-permute-start(bf16[2048,256]{1,0:T(8,128)(2,1)} %get-tuple-element.371), channel_id=1, source_target_pairs={{0,16},{16,0},{1,17},{17,1},{2,18},{18,2},{3,19},{19,3},{4,20},{20... | collective-permute-start | bytes 3145736 | tf_op jit(solution)/shard_map/ppermute | solution.py:95
  784.2 18.7 %collective-permute-start.55 = (bf16[2048,256]{1,0:T(8,128)(2,1)}, bf16[2048,256]{1,0:T(8,128)(2,1)}, u32[]{:S(2)}, u32[]{:S(2)}) collective-permute-start(bf16[2048,256]{1,0:T(8,128)(2,1)} %get-tuple-element.372), channel_id=1, source_target_pairs={{0,16},{16,0},{1,17},{17,1},{2,18},{18,2},{3,19},{19,3},{4,20},{20... | collective-permute-start | bytes 3145736 | tf_op jit(solution)/shard_map/ppermute | solution.py:95
  871.4 15.0 %collective-permute-start.56 = (bf16[128,2048]{1,0:T(8,128)(2,1)}, bf16[128,2048]{1,0:T(8,128)(2,1)S(1)}, u32[]{:S(2)}, u32[]{:S(2)}) collective-permute-start(bf16[128,2048]{1,0:T(8,128)(2,1)} %get-tuple-element.387), channel_id=1, source_target_pairs={{0,4},{4,0},{8,12},{12,8},{1,5},{5,1},{9,13},{13,9},{2,6},{6,2},{1... | collective-permute-start | bytes 1572872 | tf_op jit(solution)/shard_map/ppermute | solution.py:115
  871.6 26.1 %collective-permute-start.57 = (bf16[128,2048]{1,0:T(8,128)(2,1)}, bf16[128,2048]{1,0:T(8,128)(2,1)}, u32[]{:S(2)}, u32[]{:S(2)}) collective-permute-start(bf16[128,2048]{1,0:T(8,128)(2,1)} %get-tuple-element.388), channel_id=1, source_target_pairs={{0,4},{4,0},{8,12},{12,8},{1,5},{5,1},{9,13},{13,9},{2,6},{6,2},{1... | collective-permute-start | bytes 1572872 | tf_op jit(solution)/shard_map/ppermute | solution.py:115
  873.5 24.4 %collective-permute-start.58 = (bf16[128,2048]{1,0:T(8,128)(2,1)}, bf16[128,2048]{1,0:T(8,128)(2,1)S(1)}, u32[]{:S(2)}, u32[]{:S(2)}) collective-permute-start(bf16[128,2048]{1,0:T(8,128)(2,1)} %get-tuple-element.389), channel_id=1, source_target_pairs={{0,8},{4,12},{8,0},{12,4},{1,9},{5,13},{9,1},{13,5},{2,10},{6,14},... | collective-permute-start | bytes 1572872 | tf_op jit(solution)/shard_map/ppermute | solution.py:115
  873.5 25.2 %collective-permute-start.59 = (bf16[128,2048]{1,0:T(8,128)(2,1)}, bf16[128,2048]{1,0:T(8,128)(2,1)}, u32[]{:S(2)}, u32[]{:S(2)}) collective-permute-start(bf16[128,2048]{1,0:T(8,128)(2,1)} %get-tuple-element.390), channel_id=1, source_target_pairs={{0,8},{4,12},{8,0},{12,4},{1,9},{5,13},{9,1},{13,5},{2,10},{6,14},... | collective-permute-start | bytes 1572872 | tf_op jit(solution)/shard_map/ppermute | solution.py:115
  876.2 63.9 %collective-permute-start.70 = (bf16[512,1024]{1,0:T(8,128)(2,1)}, bf16[512,1024]{1,0:T(8,128)(2,1)}, u32[]{:S(2)}, u32[]{:S(2)}) collective-permute-start(bf16[512,1024]{1,0:T(8,128)(2,1)} %reduce-scatter.6.cloned.1.call-done.refs_3_), channel_id=1, source_target_pairs={{0,16},{16,0},{1,17},{17,1},{2,18},{18,2},{3,19},{19,3},{4,20},{20... | collective-permute-start | bytes 3145736 | tf_op jit(solution)/shard_map/ppermute | solution.py:95
  886.4 22.5 %collective-permute-start.63 = (bf16[128,2048]{1,0:T(8,128)(2,1)}, bf16[128,2048]{1,0:T(8,128)(2,1)S(1)}, u32[]{:S(2)}, u32[]{:S(2)}) collective-permute-start(bf16[128,2048]{1,0:T(8,128)(2,1)} %get-tuple-element.376), channel_id=1, source_target_pairs={{0,4},{4,0},{8,12},{12,8},{1,5},{5,1},{9,13},{13,9},{2,6},{6,2},{1... | collective-permute-start | bytes 1572872 | tf_op jit(solution)/shard_map/ppermute | solution.py:115
  897.7 21.8 %collective-permute-start.64 = (bf16[128,2048]{1,0:T(8,128)(2,1)}, bf16[128,2048]{1,0:T(8,128)(2,1)S(1)}, u32[]{:S(2)}, u32[]{:S(2)}) collective-permute-start(bf16[128,2048]{1,0:T(8,128)(2,1)} %get-tuple-element.377), channel_id=1, source_target_pairs={{0,4},{4,0},{8,12},{12,8},{1,5},{5,1},{9,13},{13,9},{2,6},{6,2},{1... | collective-permute-start | bytes 1572872 | tf_op jit(solution)/shard_map/ppermute | solution.py:115
  897.9 21.7 %collective-permute-start.65 = (bf16[128,2048]{1,0:T(8,128)(2,1)}, bf16[128,2048]{1,0:T(8,128)(2,1)S(1)}, u32[]{:S(2)}, u32[]{:S(2)}) collective-permute-start(bf16[128,2048]{1,0:T(8,128)(2,1)} %get-tuple-element.379), channel_id=1, source_target_pairs={{0,8},{4,12},{8,0},{12,4},{1,9},{5,13},{9,1},{13,5},{2,10},{6,14},... | collective-permute-start | bytes 1572872 | tf_op jit(solution)/shard_map/ppermute | solution.py:115
  898.7 23.6 %collective-permute-start.66 = (bf16[128,2048]{1,0:T(8,128)(2,1)}, bf16[128,2048]{1,0:T(8,128)(2,1)S(1)}, u32[]{:S(2)}, u32[]{:S(2)}) collective-permute-start(bf16[128,2048]{1,0:T(8,128)(2,1)} %get-tuple-element.380), channel_id=1, source_target_pairs={{0,8},{4,12},{8,0},{12,4},{1,9},{5,13},{9,1},{13,5},{2,10},{6,14},... | collective-permute-start | bytes 1572872 | tf_op jit(solution)/shard_map/ppermute | solution.py:115
  908.9 71.2 %collective-permute-start.72 = (bf16[512,1024]{1,0:T(8,128)(2,1)}, bf16[512,1024]{1,0:T(8,128)(2,1)}, u32[]{:S(2)}, u32[]{:S(2)}) collective-permute-start(bf16[512,1024]{1,0:T(8,128)(2,1)} %reduce-scatter.8.cloned.1.call-done.refs_3_), channel_id=1, source_target_pairs={{0,16},{16,0},{1,17},{17,1},{2,18},{18,2},{3,19},{19,3},{4,20},{20... | collective-permute-start | bytes 3145736 | tf_op jit(solution)/shard_map/ppermute | solution.py:95
  933.5 21.3 %collective-permute-start.67 = (bf16[128,2048]{1,0:T(8,128)(2,1)S(1)}, bf16[128,2048]{1,0:T(8,128)(2,1)}, u32[]{:S(2)}, u32[]{:S(2)}) collective-permute-start(bf16[128,2048]{1,0:T(8,128)(2,1)S(1)} %fusion.28), channel_id=1, source_target_pairs={{0,8},{4,12},{8,0},{12,4},{1,9},{5,13},{9,1},{13,5},{2,10},{6,14},... | collective-permute-start | bytes 1572872 | tf_op jit(solution)/shard_map/ppermute | solution.py:115
  933.8 21.0 %collective-permute-start.68 = (bf16[128,2048]{1,0:T(8,128)(2,1)}, bf16[128,2048]{1,0:T(8,128)(2,1)}, u32[]{:S(2)}, u32[]{:S(2)}) collective-permute-start(bf16[128,2048]{1,0:T(8,128)(2,1)} %fusion.26), channel_id=1, source_target_pairs={{0,4},{4,0},{8,12},{12,8},{1,5},{5,1},{9,13},{13,9},{2,6},{6,2},{1... | collective-permute-start | bytes 1572872 | tf_op jit(solution)/shard_map/ppermute | solution.py:115
  940.1 40.0 %collective-permute-start.73 = (bf16[512,1024]{1,0:T(8,128)(2,1)S(1)}, bf16[512,1024]{1,0:T(8,128)(2,1)S(1)}, u32[]{:S(2)}, u32[]{:S(2)}) collective-permute-start(bf16[512,1024]{1,0:T(8,128)(2,1)S(1)} %copy-done.15), channel_id=1, source_target_pairs={{0,16},{16,0},{1,17},{17,1},{2,18},{18,2},{3,19},{19,3},{4,20},{20... | collective-permute-start | bytes 3145736 | tf_op jit(solution)/shard_map/ppermute | solution.py:95
  980.1 15.3 %collective-permute-start.74 = (bf16[512,2048]{1,0:T(8,128)(2,1)}, bf16[512,2048]{1,0:T(8,128)(2,1)S(1)}, u32[]{:S(2)}, u32[]{:S(2)}) collective-permute-start(bf16[512,2048]{1,0:T(8,128)(2,1)} %reduce-scatter.14.cloned.1.call-done.refs_0_), channel_id=1, source_target_pairs={{0,16},{16,0},{1,17},{17,1},{2,18},{18,2},{3,19},{19,3},{4,20},{20... | collective-permute-start | bytes 6291464 | tf_op jit(solution)/shard_map/ppermute | solution.py:95
  (128 other events, 1556.7 us)
Sparse Core Ops, SparseCore 0:
  14.7 67.7 all-gather.5
  84.6 165.5 all-gather.7
  251.9 147.9 all-gather.9
  401.9 78.9 all-gather.11
  499.9 75.2 reduce-scatter.5
  578.0 77.2 reduce-scatter.7
  657.6 77.2 reduce-scatter.9
  742.5 73.8 reduce-scatter.11
  822.5 141.2 reduce-scatter.13
